TPU v7x, 32 devices: a whole 2x2x4 slice. The times are simulated.
32 devices in a mesh: fsdp: 2 (over x), ctx: 4 (over y, core), tp: 4 (over z).
Axes of the slice: x: 2, y: 2, z: 4, core: 2. Of those that a mesh axis runs over, the one named last changes fastest.
Arguments:
- stream_in: bfloat16 [8192, 2048], P(('fsdp', 'ctx', 'tp')), may hold values from -6 to 6
- stream_grad: bfloat16 [8192, 2048], P(('fsdp', 'ctx', 'tp')), may hold values from -6 to 6
- segments: int32 [8192], P('fsdp'), may hold values from 0 to 8, as said below
- positions: int32 [8192], P('fsdp'), may hold values from 0 to 2431, as said below
- first_gain: float32 [2048], replicated, may hold values from 0.5 to 1.5
- first_shift: float32 [2048], replicated, may hold values from -3 to 3
- second_gain: float32 [2048], replicated, may hold values from 0.5 to 1.5
- second_shift: float32 [2048], replicated, may hold values from -3 to 3
- attend_weight: bfloat16 [2048, 8, 768], P(('fsdp', 'ctx'), 'tp'), may hold values from -0.125 to 0.125
- attend_bias: float32 [8, 768], P('tp'), may hold values from -3 to 3
- output_weight: bfloat16 [2048, 2048], P(('fsdp', 'ctx'), 'tp'), may hold values from -1 to 1
- expand_weight: bfloat16 [2048, 8192], P(('fsdp', 'ctx'), 'tp'), may hold values from -0.125 to 0.125
- expand_bias: float32 [8192], P('tp'), may hold values from -3 to 3
- contract_weight: bfloat16 [2048, 8192], P(('fsdp', 'ctx'), 'tp'), may hold values from -0.0625 to 0.0625
- output_bias: float32 [2048], replicated, may hold values from -3 to 3
Outputs:
- stream_out: bfloat16 [8192, 2048], P(('fsdp', 'ctx', 'tp'))
- input_grad: float32 [8192, 2048], P(('fsdp', 'ctx', 'tp'))
- first_gain_grad: float32 [2048], replicated
- first_shift_grad: float32 [2048], replicated
- second_gain_grad: float32 [2048], replicated
- second_shift_grad: float32 [2048], replicated
- attend_weight_grad: float32 [2048, 8, 768], P(('fsdp', 'ctx'), 'tp')
- attend_bias_grad: float32 [8, 768], P('tp')
- output_weight_grad: float32 [2048, 2048], P(('fsdp', 'ctx'), 'tp')
- expand_weight_grad: float32 [2048, 8192], P(('fsdp', 'ctx'), 'tp')
- expand_bias_grad: float32 [8192], P('tp')
- contract_weight_grad: float32 [2048, 8192], P(('fsdp', 'ctx'), 'tp')
- output_bias_grad: float32 [2048], replicated
Inputs may be any that keep to these rules, and one draw needn't show every extreme that they name: `segments`: each group's 4096 tokens form 4 runs of 1024; a run begins with 512 prompt tokens (id 0) and then holds 2 continuations, consecutive pairs of them 256 + o and 256 - o tokens long with 1 <= o <= 128; the first pair of each group's first run has o = 128; ids 1 to 8 each name one continuation of a group. The prompt tokens of a run hold positions k * 512 to k * 512 + 511 in order, each k once in a group; a continuation's tokens hold 2048, 2049 and so on in order.
All inputs are finite; a program needn't handle non-finite values.
Results may differ from a plain program's by a relative error of at most 0.012.
Values may be sent and summed in bfloat16 or wider, within the bound.
A program may use at most 256 MiB of HBM per device.

v0:
```python
from functools import partial
import math

import jax
import jax.numpy as jnp
from jax import lax
from jax.sharding import PartitionSpec as P

ROT = 64
PROMPT = 2048


EPS = 1e-05


def layer_norm(values, gain_row, shift_row):
    center = values - jnp.mean(values, -1, keepdims=True)
    spread = jnp.mean(center * center, -1, keepdims=True)
    return center * lax.rsqrt(spread + EPS) * gain_row + shift_row


def rotate(values, where_at):
    half_rot = ROT // 2
    frequency = jnp.exp(jnp.arange(half_rot, dtype=jnp.float32) * (-2.0 * math.log(10000.0) / ROT))
    angles = where_at.astype(jnp.float32)[:, None] * frequency[None, :]
    cosine = jnp.concatenate([jnp.cos(angles), jnp.cos(angles)], -1)[:, None, :]
    sine_rows = jnp.concatenate([jnp.sin(angles), jnp.sin(angles)], -1)[:, None, :]
    rotated_part = values[..., :ROT]
    turned = jnp.concatenate([-rotated_part[..., half_rot:], rotated_part[..., :half_rot]], -1)
    return jnp.concatenate([rotated_part * cosine + turned * sine_rows, values[..., ROT:]], -1)


def attention_probs(query_heads, key_heads, allowed):
    score_scale = 1.0 / math.sqrt(query_heads.shape[-1])
    scores = (
        jnp.einsum("qhd,khd->hqk", query_heads, key_heads, preferred_element_type=jnp.float32)
        * score_scale
    )
    scores = jnp.where(allowed[None], scores, -1e30)
    row_top = jnp.max(scores, -1, keepdims=True)
    exponent = jnp.exp(scores - row_top)
    return exponent / jnp.sum(exponent, -1, keepdims=True)


def row_product(left, right):
    return jnp.einsum("tf,df->td", left, right, preferred_element_type=jnp.float32)


def column_product(left, right):
    return jnp.einsum("tc,tk->ck", left, right, preferred_element_type=jnp.float32)


def shards(
    stream_in,
    stream_grad,
    segments,
    positions,
    first_gain,
    first_shift,
    second_gain,
    second_shift,
    attend_weight,
    attend_bias,
    output_weight,
    expand_weight,
    expand_bias,
    contract_weight,
    output_bias,
):
    full_rows, grad_rows = (
        lax.all_gather(stream_in, "tp", axis=0, tiled=True),
        lax.all_gather(stream_grad, "tp", axis=0, tiled=True),
    )
    row_count = full_rows.shape[0]
    holders = lax.axis_size("ctx")
    holder = lax.axis_index("ctx")
    prompt_here = PROMPT // holders
    heads_here = attend_bias.shape[0]
    head_size = attend_bias.shape[1] // 3
    hidden_here = expand_bias.shape[0]
    score_scale = 1.0 / math.sqrt(head_size)
    row_pos = lax.dynamic_slice_in_dim(positions, holder * row_count, row_count)
    row_seg = lax.dynamic_slice_in_dim(segments, holder * row_count, row_count)
    prompt_pos = positions.reshape(holders, row_count)[:, :prompt_here].reshape(-1)
    key_pos = jnp.concatenate([prompt_pos, row_pos[prompt_here:]])
    key_seg = jnp.concatenate([jnp.zeros_like(prompt_pos), row_seg[prompt_here:]])
    allowed = ((key_seg[None, :] == 0) | (key_seg[None, :] == row_seg[:, None])) & (
        key_pos[None, :] <= row_pos[:, None]
    )
    inputs = full_rows.astype(jnp.float32)
    first_norm = layer_norm(inputs, first_gain, first_shift).astype(jnp.bfloat16)
    second_norm = layer_norm(inputs, second_gain, second_shift).astype(jnp.bfloat16)
    pieces = (
        lax.all_gather(attend_weight, ("fsdp", "ctx"), axis=0, tiled=True),
        lax.all_gather(expand_weight, ("fsdp", "ctx"), axis=0, tiled=True),
    )
    span = pieces[0].shape[0]
    first_cols = first_norm
    second_cols = second_norm
    projected = jnp.dot(first_cols, pieces[0].reshape(span, -1), preferred_element_type=jnp.float32)
    pre_gelu = jnp.dot(second_cols, pieces[1], preferred_element_type=jnp.float32)
    projected = projected.reshape(row_count, heads_here, 3 * head_size) + attend_bias
    pre_gelu = pre_gelu + expand_bias
    query_heads = rotate(projected[..., :head_size], row_pos).astype(jnp.bfloat16)
    key_heads = rotate(projected[..., head_size : 2 * head_size], row_pos).astype(jnp.bfloat16)
    value_heads = projected[..., 2 * head_size :].astype(jnp.bfloat16)
    prompt_pairs = jnp.concatenate([key_heads[:prompt_here], value_heads[:prompt_here]], -1)
    gathered = lax.all_gather(prompt_pairs, "ctx", axis=0, tiled=True)
    all_keys = jnp.concatenate([gathered[..., :head_size], key_heads[prompt_here:]], 0)
    all_values = jnp.concatenate([gathered[..., head_size:], value_heads[prompt_here:]], 0)
    probability = attention_probs(query_heads, all_keys, allowed)
    attended = jnp.einsum(
        "hqk,khd->qhd",
        probability.astype(jnp.bfloat16),
        all_values,
        preferred_element_type=jnp.float32,
    )
    attended = attended.astype(jnp.bfloat16).reshape(row_count, heads_here * head_size)
    activated = jax.nn.gelu(pre_gelu, approximate=False).astype(jnp.bfloat16)
    pieces = lax.all_gather((output_weight, contract_weight), ("fsdp", "ctx"), axis=0, tiled=True)
    mixed = row_product(attended, pieces[0]) + row_product(activated, pieces[1])
    branch_total = lax.psum_scatter(mixed, "tp", scatter_dimension=0, tiled=True)
    local_inputs = stream_in.astype(jnp.float32)
    stream_out = (local_inputs + branch_total + output_bias).astype(jnp.bfloat16)
    grad_local = stream_grad.astype(jnp.float32)
    pieces = (
        lax.all_gather(output_weight, ("fsdp", "ctx"), axis=0, tiled=True),
        lax.all_gather(contract_weight, ("fsdp", "ctx"), axis=0, tiled=True),
    )
    grad_cols = grad_rows
    grad_attended = jnp.dot(grad_cols, pieces[0], preferred_element_type=jnp.float32)
    grad_activated = jnp.dot(grad_cols, pieces[1], preferred_element_type=jnp.float32)
    regathered = lax.all_gather(prompt_pairs, "ctx", axis=0, tiled=True)
    back_keys = jnp.concatenate([regathered[..., :head_size], key_heads[prompt_here:]], 0)
    back_values = jnp.concatenate([regathered[..., head_size:], value_heads[prompt_here:]], 0)
    back_prob = attention_probs(query_heads, back_keys, allowed)
    grad_att_low = grad_attended.astype(jnp.bfloat16).reshape(row_count, heads_here, head_size)
    gelu_back = jax.vjp(partial(jax.nn.gelu, approximate=False), pre_gelu)[1]
    grad_pre = gelu_back(grad_activated)[0].astype(jnp.bfloat16)
    grad_prob = jnp.einsum(
        "qhd,khd->hqk", grad_att_low, back_values, preferred_element_type=jnp.float32
    )
    inner = jnp.sum(back_prob * grad_prob, -1, keepdims=True)
    grad_scores = (back_prob * (grad_prob - inner)).astype(jnp.bfloat16)
    grad_queries = (
        jnp.einsum("hqk,khd->qhd", grad_scores, back_keys, preferred_element_type=jnp.float32)
        * score_scale
    )
    grad_keys = (
        jnp.einsum("hqk,qhd->khd", grad_scores, query_heads, preferred_element_type=jnp.float32)
        * score_scale
    )
    grad_values = jnp.einsum(
        "hqk,qhd->khd",
        back_prob.astype(jnp.bfloat16),
        grad_att_low,
        preferred_element_type=jnp.float32,
    )
    prompt_grad = lax.psum_scatter(
        jnp.concatenate([grad_keys[:PROMPT], grad_values[:PROMPT]], -1),
        "ctx",
        scatter_dimension=0,
        tiled=True,
    )
    grad_key_rows = jnp.concatenate([prompt_grad[..., :head_size], grad_keys[PROMPT:]], 0)
    grad_value_rows = jnp.concatenate([prompt_grad[..., head_size:], grad_values[PROMPT:]], 0)

    def rotate_rows(values):
        return rotate(values, row_pos)

    rotate_back = jax.vjp(rotate_rows, projected[..., :head_size])[1]
    grad_query_pre = rotate_back(grad_queries)[0]
    grad_key_pre = rotate_back(grad_key_rows)[0]
    grad_projected = jnp.concatenate([grad_query_pre, grad_key_pre, grad_value_rows], -1).astype(
        jnp.bfloat16
    )
    grad_flat = grad_projected.reshape(row_count, heads_here * 3 * head_size)
    attend_bias_part = jnp.sum(grad_projected, 0, dtype=jnp.float32)
    expand_bias_part = jnp.sum(grad_pre, 0, dtype=jnp.float32)
    attend_bias_grad, expand_bias_grad = lax.psum(
        (attend_bias_part, expand_bias_part), ("fsdp", "ctx")
    )
    pieces = lax.all_gather((attend_weight, expand_weight), ("fsdp", "ctx"), axis=0, tiled=True)
    span = pieces[0].shape[0]
    grad_norms = jnp.stack(
        [row_product(grad_flat, pieces[0].reshape(span, -1)), row_product(grad_pre, pieces[1])]
    )
    local_norms = lax.psum_scatter(
        grad_norms.astype(jnp.bfloat16), "tp", scatter_dimension=1, tiled=True
    ).astype(jnp.float32)

    def both_norms(values, gains):
        return (layer_norm(values, gains[0], gains[1]), layer_norm(values, gains[2], gains[3]))

    norm_back = jax.vjp(
        both_norms, local_inputs, (first_gain, first_shift, second_gain, second_shift)
    )[1]
    grad_inputs, gain_parts = norm_back((local_norms[0], local_norms[1]))
    input_grad = grad_local + grad_inputs
    out_bias_part = jnp.sum(grad_local, 0)
    norm_sums = lax.psum(
        (gain_parts[0], gain_parts[1], gain_parts[2], gain_parts[3], out_bias_part),
        ("fsdp", "ctx", "tp"),
    )
    local_rows = attend_weight.shape[0]
    first_cols = first_norm
    second_cols = second_norm
    grad_cols = grad_rows
    weight_grads = lax.psum_scatter(
        jnp.concatenate(
            [
                column_product(first_cols, grad_flat),
                column_product(grad_cols, attended),
                column_product(second_cols, grad_pre),
                column_product(grad_cols, activated),
            ],
            1,
        ).astype(jnp.bfloat16),
        ("fsdp", "ctx"),
        scatter_dimension=0,
        tiled=True,
    ).astype(jnp.float32)
    attend_cols = heads_here * 3 * head_size
    output_cols = heads_here * head_size
    attend_weight_grad = weight_grads[:, :attend_cols].reshape(
        local_rows, heads_here, 3 * head_size
    )
    output_weight_grad = weight_grads[:, attend_cols : attend_cols + output_cols]
    expand_weight_grad = weight_grads[
        :, attend_cols + output_cols : attend_cols + output_cols + hidden_here
    ]
    contract_weight_grad = weight_grads[:, attend_cols + output_cols + hidden_here :]
    return (
        stream_out,
        input_grad,
        norm_sums[0],
        norm_sums[1],
        norm_sums[2],
        norm_sums[3],
        attend_weight_grad,
        attend_bias_grad,
        output_weight_grad,
        expand_weight_grad,
        expand_bias_grad,
        contract_weight_grad,
        norm_sums[4],
    )


def solution(mesh):
    placed = (
        P(("fsdp", "ctx", "tp"), None),
        P(("fsdp", "ctx", "tp"), None),
        P("fsdp"),
        P("fsdp"),
        P(),
        P(),
        P(),
        P(),
        P(("fsdp", "ctx"), "tp", None),
        P("tp", None),
        P(("fsdp", "ctx"), "tp"),
        P(("fsdp", "ctx"), "tp"),
        P("tp"),
        P(("fsdp", "ctx"), "tp"),
        P(),
    )
    return jax.shard_map(
        shards,
        mesh=mesh,
        in_specs=placed,
        out_specs=(
            P(("fsdp", "ctx", "tp"), None),
            P(("fsdp", "ctx", "tp"), None),
            P(),
            P(),
            P(),
            P(),
            P(("fsdp", "ctx"), "tp", None),
            P("tp", None),
            P(("fsdp", "ctx"), "tp"),
            P(("fsdp", "ctx"), "tp"),
            P("tp"),
            P(("fsdp", "ctx"), "tp"),
            P(),
        ),
        check_vma=False,
    )
```

profile of v0, /device:TPU:0, one launch (start us, length us, event | category | flops | bytes accessed | tf_op | source)
XLA Modules:
  0.0 975.3 jit_solution(1142379070800161493)
XLA Ops:
  8.0 2.1 copy.38
  12.8 80.3 %all-gather.8.cloned.1.call-done = bf16[1024,2048]{1,0:T(8,128)(2,1)} async-done(((bf16[256,2048]{1,0:T(8,128)(2,1)}), bf16[1024,2048]{1,0:T(8,128)(2,1)}) %all-gather.8.cloned.1.call-update) | async-done | bytes 4194320 | tf_op jit(solution)/shard_map/all_gather | solution.py:71
  93.1 3.0 convert_reduce_fusion
  97.8 41.8 %all-gather.10.cloned.1.call-done = bf16[2048,2,768]{2,0,1:T(8,128)(2,1)} async-done(((bf16[256,2,768]{2,0,1:T(8,128)(2,1)}), bf16[2048,2,768]{2,0,1:T(8,128)(2,1)}) %all-gather.10.cloned.1.call-update) | async-done | bytes 6291472 | tf_op jit(solution)/shard_map/all_gather | solution.py:94
  139.6 8.7 copy.39
  148.3 10.6 %fusion.98 = (bf16[1024,2,768]{0,2,1:T(8,128)(2,1)S(1)}, f32[1024,2,768]{0,2,1:T(8,128)S(1)}) fusion(f32[2,768]{1,0:T(2,128)S(1)} %copy-done.46, bf16[2048,2,768]{0,2,1:T(8,128)(2,1)} %copy.39, f32[2048]{0:T(1024)S(1)} %copy-done.44, f32[2048]{0:T(1024)S(1)} %copy-done.25, f32[1024]{0:T(1024)S(1)} %add_rsqrt_fusion, ...), kind=kOutput, calls=%fused_computation.164 | convolution fusion | flops 6458179584 | bytes 19953664 | tf_op jit(solution)/shard_map/dot_general | solution.py:100
  163.3 4.5 compare_and_fusion
  169.5 82.2 %all-gather.20.cloned.1.call-done = bf16[1024,2048]{1,0:T(8,128)(2,1)} async-done(((bf16[256,2048]{1,0:T(8,128)(2,1)}), bf16[1024,2048]{1,0:T(8,128)(2,1)}) %all-gather.20.cloned.1.call-update) | async-done | bytes 4194320 | tf_op jit(solution)/shard_map/all_gather | solution.py:72
  251.7 6.2 convolution_convert_fusion.3
  257.9 28.8 %all-gather.12.cloned.1.call-done = bf16[2048,2,512]{0,2,1:T(8,128)(2,1)} async-done(((bf16[512,2,512]{0,2,1:T(8,128)(2,1)}), bf16[2048,2,512]{0,2,1:T(8,128)(2,1)}) %all-gather.12.cloned.1.call-update) | async-done | bytes 4194320 | tf_op jit(solution)/shard_map/all_gather | solution.py:108
  286.7 4.8 fusion.92
  291.5 13.3 %fusion.99 = (f32[2,1024]{1,0:T(2,128)S(1)}, f32[2,1024,2560]{2,1,0:T(8,128)}) fusion(pred[1024,2560]{1,0:T(8,128)(4,1)} %compare_and_fusion, bf16[1024,2,192]{0,2,1:T(8,128)(2,1)S(1)} %get-tuple-element.76, bf16[1024,2,64]{0,2,1:T(8,128)(2,1)S(1)} %get-tuple-element.66, bf16[1024,2,192]{0,2,1:T(8,128)(2,1)S(1)} %get-tuple-element.77, ...), kind=kOutput, calls=%fused_computation.165 | convolution fusion | flops 2719222272 | bytes 27795456 | tf_op jit(solution)/shard_map/sub | solution.py:41
  304.8 15.1 %multiply_reduce_fusion = (f32[2,1024]{1,0:T(2,128)S(1)}, f32[2,1024,2560]{2,1,0:T(8,128)}) fusion(f32[2,1024,2560]{2,1,0:T(8,128)} %get-tuple-element.96, f32[2,1024]{1,0:T(2,128)S(1)} %get-tuple-element.95, bf16[1024,2,256]{0,2,1:T(8,128)(2,1)} %bitcast.97, bf16[512,2,256]{0,2,1:T(8,128)(2,1)S(1)} %get-tuple-element.79, ...), kind=kOutput, calls=%fused_computation.3 | convolution fusion | flops 2705324032 | bytes 45629440 | tf_op jit(solution)/shard_map/qhd,khd->hqk/dot_general | solution.py:140
  319.9 14.7 %multiply_convert_fusion = bf16[2,1024,2560]{2,1,0:T(8,128)(2,1)S(1)} fusion(f32[2,1024,2560]{2,1,0:T(8,128)} %get-tuple-element.98, f32[2,1024]{1,0:T(2,128)S(1)} %get-tuple-element.97, f32[2,1024,2560]{2,1,0:T(8,128)} %get-tuple-element.96, f32[2,1024]{1,0:T(2,128)S(1)} %get-tuple-element.95), kind=kLoop, calls=%fused_computation.2 | loop fusion | flops 20971520 | bytes 52445184 | tf_op jit(solution)/shard_map/convert_element_type | solution.py:144
  334.6 2.9 multiply_bitcast_fusion
  338.6 2.3 copy-done.1
  342.1 8.6 fusion.28
  350.7 2.4 copy-done.7
  353.5 3.9 pad_maximum_fusion.1
  358.0 14.7 %fusion.81 = f32[1024,2048]{1,0:T(8,128)} fusion(bf16[2048,2048]{1,0:T(8,128)(2,1)} %all-gather.16.cloned.1.call-done, bf16[1024,2048]{1,0:T(8,128)(2,1)} %all-gather.8.cloned.1.call-done, f32[2048]{0:T(1024)S(1)} %copy-done.42, f32[2048]{0:T(1024)S(1)} %copy-done.27, f32[1024]{0:T(1024)S(1)} %add_rsqrt_fusion, f32[1024]{0:T(1024)S(1)} %broadcast_multiply_fusion.1), kind=kOutput, calls=%fused_computation.156 | convolution fusion | flops 8602517504 | bytes 20996096 | tf_op jit(solution)/shard_map/dot_general | solution.py:101
  372.7 26.5 %all-gather.18.cloned.1.call-done = bf16[2048,2048]{1,0:T(8,128)(2,1)} async-done(((bf16[256,2048]{1,0:T(8,128)(2,1)}), bf16[2048,2048]{1,0:T(8,128)(2,1)}) %all-gather.18.cloned.1.call-update) | async-done | bytes 8388624 | tf_op jit(solution)/shard_map/all_gather | solution.py:120
  399.2 33.6 %convert_reduce_fusion.1 = (f32[2048]{0:T(1024)}, bf16[1024,2048]{1,0:T(8,128)(2,1)S(1)}, f32[1024,2048]{1,0:T(8,128)}) fusion(f32[1024,2048]{1,0:T(8,128)} %fusion.81, f32[2048]{0:T(1024)S(1)} %copy-done.33, bf16[1024,2048]{1,0:T(8,128)(2,1)} %all-gather.20.cloned.1.call-done, bf16[2048,2048]{1,0:T(8,128)(2,1)} %all-gather.18.cloned.1.call-done), kind=kOutput, calls=%fused_computation.28 | convolution fusion | flops 8747218944 | bytes 33570816 | tf_op jit(solution)/shard_map/dot_general | solution.py:132
  434.8 10.7 %convert_bitcast_fusion.1 = bf16[1,1024,2048]{2,1,0:T(8,128)(2,1)} fusion(bf16[1024,2048]{1,0:T(8,128)(2,1)S(1)} %get-tuple-element.56, bf16[2048,2048]{1,0:T(8,128)(2,1)S(1)} %copy-done.40), kind=kOutput, calls=%fused_computation.61 | convolution fusion | flops 8592031744 | bytes 16777216 | tf_op jit(solution)/shard_map/tf,df->td/dot_general | solution.py:46
  448.1 5.9 multiply_bitcast_fusion.1
  455.5 18.1 %reduce-scatter.7.cloned.1.call-done = f32[512,2,512]{0,2,1:T(8,128)} async-done(((f32[2048,2,512]{0,2,1:T(8,128)}), f32[512,2,512]{0,2,1:T(8,128)}) %reduce-scatter.7.cloned.1.call-update) | async-done | bytes 2097168 | tf_op jit(solution)/shard_map/reduce_scatter | solution.py:159
  482.4 8.4 fusion.32
  490.8 6.2 pad_maximum_fusion.2
  497.3 8.0 multiply_convert_fusion.1
  507.3 13.4 %fusion.104 = f32[1024,2048]{1,0:T(8,128)} fusion(bf16[1024,2048]{1,0:T(8,128)(2,1)S(1)} %multiply_convert_fusion.1, bf16[2048,2048]{1,0:T(8,128)(2,1)} %all-gather.18.cloned.1.call-done), kind=kOutput, calls=%fused_computation.166 | convolution fusion | flops 8589934592 | bytes 20971520 | tf_op jit(solution)/shard_map/tf,df->td/dot_general | solution.py:46
  520.7 11.0 %fusion.59 = bf16[2,256,1024]{2,1,0:T(8,128)(2,1)S(1)} fusion(bf16[512,2,256]{0,2,1:T(8,128)(2,1)} %copy-done.24, bf16[2048,2,256]{0,2,1:T(8,128)(2,1)} %get-tuple-element.73, f32[2,1024,2560]{2,1,0:T(8,128)} %get-tuple-element.96, f32[2,1024]{1,0:T(2,128)S(1)} %copy-done.35), kind=kOutput, calls=%fused_computation.104 | convolution fusion | flops 2700607488 | bytes 24649728 | tf_op jit(solution)/shard_map/hqk,khd->qhd/dot_general | solution.py:112
  531.7 9.1 convolution_add_fusion
  541.4 14.3 %convert_bitcast_fusion = bf16[2048,2048]{0,1:T(8,128)(2,1)} fusion(bf16[1024,2048]{1,0:T(8,128)(2,1)} %copy-done.8, bf16[1024,2048]{1,0:T(8,128)(2,1)} %all-gather.20.cloned.1.call-done), kind=kOutput, calls=%fused_computation.29 | convolution fusion | flops 8594128896 | bytes 16777216 | tf_op jit(solution)/shard_map/tc,tk->ck/dot_general | solution.py:50
  555.7 12.5 %convolution_convert_fusion.1 = bf16[2048,2048]{0,1:T(8,128)(2,1)} fusion(bf16[1024,2048]{1,0:T(8,128)(2,1)S(1)} %copy-done.49, bf16[1024,2048]{1,0:T(8,128)(2,1)S(1)} %copy-done.5, f32[2048]{0:T(1024)S(1)} %copy-done.43, f32[2048]{0:T(1024)S(1)} %copy-done.28, f32[1024]{0:T(1024)S(1)} %copy-done.39, f32[1024]{0:T(1024)S(1)} %copy-done.32), kind=kOutput, calls=%fused_computation.46 | convolution fusion | flops 8606711808 | bytes 16801792 | tf_op jit(solution)/shard_map/tc,tk->ck/dot_general | solution.py:50
  568.3 2.4 fusion.39
  570.7 9.3 convolution_convert_fusion
  580.0 17.4 %pad_maximum_fusion = bf16[2048,6144]{0,1:T(8,128)(2,1)} fusion(bf16[2048,2048]{0,1:T(8,128)(2,1)} %convert_bitcast_fusion, bf16[2048,2048]{0,1:T(8,128)(2,1)} %convolution_convert_fusion.1, bf16[2048,512]{0,1:T(8,128)(2,1)S(1)} %fusion.39, bf16[2048,1536]{0,1:T(8,128)(2,1)} %convolution_convert_fusion), kind=kLoop, calls=%fused_computation.1 | loop fusion | flops 100663296 | bytes 50331648 | tf_op jit(solution)/shard_map/concatenate | solution.py:210
  598.9 23.6 %all-reduce.10 = (f32[2,768]{1,0:T(2,128)}, f32[2048]{0:T(1024)}) all-reduce(f32[2,768]{1,0:T(2,128)S(1)} %copy-done.30, f32[2048]{0:T(1024)S(1)} %copy-done.36), channel_id=1, replica_groups=mesh['fsdp'=2,'ctx'=4,'tp'=4] {'fsdp','ctx'}, use_global_device_ids=true, to_apply=%region_24.25 | all-reduce | flops 3584 | bytes 28672 | tf_op jit(solution)/shard_map/psum | solution.py:180
  622.5 19.2 %reduce-scatter.9.cloned.1.call-done = bf16[2,256,2048]{2,1,0:T(8,128)(2,1)} async-done(((bf16[2,1024,2048]{2,1,0:T(8,128)(2,1)}), bf16[2,256,2048]{2,1,0:T(8,128)(2,1)}) %reduce-scatter.9.cloned.1.call-update) | async-done | bytes 2097168 | tf_op jit(solution)/shard_map/reduce_scatter | solution.py:188
  641.7 2.1 convert_element_type.84
  646.9 142.3 %reduce-scatter.5.cloned.1.call-done = f32[256,2048]{1,0:T(8,128)} async-done(((f32[1024,2048]{1,0:T(8,128)}), f32[256,2048]{1,0:T(8,128)}) %reduce-scatter.5.cloned.1.call-update) | async-done | bytes 2097168 | tf_op jit(solution)/shard_map/reduce_scatter | solution.py:122
  789.3 5.1 convert_reduce_fusion.4
  794.3 42.1 %all-reduce.9 = (f32[2048]{0:T(1024)}, f32[2048]{0:T(1024)}, f32[2048]{0:T(1024)}, f32[2048]{0:T(1024)}, f32[2048]{0:T(1024)}) all-reduce(f32[2048]{0:T(1024)S(1)} %get-tuple-element.42, f32[2048]{0:T(1024)S(1)} %get-tuple-element.46, f32[2048]{0:T(1024)S(1)} %get-tuple-element.39, ...), channel_id=1, replica_groups=mesh['fsdp'=2,'ctx'=4,'tp'=4] {'fsdp','ctx','tp'}, use_global_device_ids=true, to_apply=%region_15.16 | all-reduce | flops 10240 | bytes 81920 | tf_op jit(solution)/shard_map/psum | solution.py:201
  836.4 114.6 %reduce-scatter.11.cloned.1.call-done = bf16[256,6144]{0,1:T(8,128)(2,1)} async-done(((bf16[2048,6144]{0,1:T(8,128)(2,1)}), bf16[256,6144]{0,1:T(8,128)(2,1)}) %reduce-scatter.11.cloned.1.call-update) | async-done | bytes 3145744 | tf_op jit(solution)/shard_map/reduce_scatter | solution.py:209
  951.0 3.9 fusion.93
  954.8 3.0 copy.47
  957.9 2.9 copy.48
  962.1 3.7 copy.45
  966.6 2.0 copy.46
  (175 shorter events, 38.5 us)
Async XLA Ops:
  7.2 85.9 %all-gather.8.cloned.1.call-start = ((), (), s32[]{:S(2)}) async-start(), calls=%async_computation.4 | async-start | bytes 5242880 | tf_op jit(solution)/shard_map/all_gather | solution.py:71
  7.9 131.7 %all-gather.10.cloned.1.call-start = ((), (), s32[]{:S(2)}) async-start(), calls=%async_computation.5 | async-start | bytes 7077888 | tf_op jit(solution)/shard_map/all_gather | solution.py:94
  10.1 159.4 %all-gather.14.cloned.1.call-start = ((), (), s32[]{:S(2)}) async-start(), calls=%async_computation.7 | async-start | bytes 2359296 | tf_op jit(solution)/shard_map/all_gather | solution.py:120
  10.8 240.9 %all-gather.20.cloned.1.call-start = ((), (), s32[]{:S(2)}) async-start(), calls=%async_computation.11 | async-start | bytes 5242880 | tf_op jit(solution)/shard_map/all_gather | solution.py:72
  11.4 275.3 %all-gather.12.cloned.1.call-start = ((), (), s32[]{:S(2)}) async-start(), calls=%async_computation.6 | async-start | bytes 5242880 | tf_op jit(solution)/shard_map/all_gather | solution.py:108
  12.7 146.3 %copy-start.16 = (f32[1024,64]{0,1:T(8,128)}, f32[1024,64]{0,1:T(8,128)S(1)}, u32[]{:S(2)}) copy-start(f32[1024,64]{0,1:T(8,128)S(1)} %get-tuple-element.100) | copy-start | bytes 786436
  12.8 146.3 %copy-start.18 = (f32[1024,64]{0,1:T(8,128)}, f32[1024,64]{0,1:T(8,128)S(1)}, u32[]{:S(2)}) copy-start(f32[1024,64]{0,1:T(8,128)S(1)} %get-tuple-element.99) | copy-start | bytes 786436
  93.1 3.4 copy-start.4
  96.5 260.9 %copy-start.31 = (f32[1024]{0:T(1024)}, f32[1024]{0:T(1024)S(1)}, u32[]{:S(2)}) copy-start(f32[1024]{0:T(1024)S(1)} %broadcast_multiply_fusion.1) | copy-start | bytes 12292
  97.8 259.7 %copy-start.38 = (f32[1024]{0:T(1024)}, f32[1024]{0:T(1024)S(1)}, u32[]{:S(2)}) copy-start(f32[1024]{0:T(1024)S(1)} %add_rsqrt_fusion) | copy-start | bytes 12292
  97.8 50.6 %copy-start.25 = (f32[2048]{0:T(1024)S(1)}, f32[2048]{0:T(1024)}, u32[]{:S(2)}) copy-start(f32[2048]{0:T(1024)} %param.19) | copy-start | bytes 24580
  97.8 50.5 %copy-start.44 = (f32[2048]{0:T(1024)S(1)}, f32[2048]{0:T(1024)}, u32[]{:S(2)}) copy-start(f32[2048]{0:T(1024)} %param.20) | copy-start | bytes 24580
  97.8 50.5 %copy-start.46 = (f32[2,768]{1,0:T(2,128)S(1)}, f32[2,768]{1,0:T(2,128)}, u32[]{:S(2)}) copy-start(f32[2,768]{1,0:T(2,128)} %param.24) | copy-start | bytes 18436
  159.4 132.2 %copy-start.22 = (bf16[1024,2,64]{0,2,1:T(8,128)(2,1)}, bf16[1024,2,64]{0,2,1:T(8,128)(2,1)S(1)}, u32[]{:S(2)}) copy-start(bf16[1024,2,64]{0,2,1:T(8,128)(2,1)S(1)} %get-tuple-element.67) | copy-start | bytes 786436
  159.5 132.0 %copy-start.14 = (bf16[1024,2,192]{0,2,1:T(8,128)(2,1)}, bf16[1024,2,192]{0,2,1:T(8,128)(2,1)S(1)}, u32[]{:S(2)}) copy-start(bf16[1024,2,192]{0,2,1:T(8,128)(2,1)S(1)} %get-tuple-element.77) | copy-start | bytes 2359300
  159.6 3.0 copy-start.29
  159.7 145.1 %copy-start.24 = (bf16[512,2,256]{0,2,1:T(8,128)(2,1)}, bf16[512,2,256]{0,2,1:T(8,128)(2,1)S(1)}, u32[]{:S(2)}) copy-start(bf16[512,2,256]{0,2,1:T(8,128)(2,1)S(1)} %get-tuple-element.79) | copy-start | bytes 1572868
  160.9 196.5 %all-gather.16.cloned.1.call-start = ((), (), s32[]{:S(2)}) async-start(), calls=%async_computation.8 | async-start | bytes 9437184 | tf_op jit(solution)/shard_map/all_gather | solution.py:95
  161.5 237.7 %all-gather.18.cloned.1.call-start = ((), (), s32[]{:S(2)}) async-start(), calls=%async_computation.9 | async-start | bytes 9437184 | tf_op jit(solution)/shard_map/all_gather | solution.py:120
  162.3 311.3 %reduce-scatter.7.cloned.1.call-start = ((), (), s32[]{:S(2)}) async-start(), calls=%async_computation.12 | async-start | bytes 10485760 | tf_op jit(solution)/shard_map/reduce_scatter | solution.py:159
  304.8 36.5 %copy-start.34 = (f32[2,1024]{1,0:T(2,128)}, f32[2,1024]{1,0:T(2,128)S(1)}, u32[]{:S(2)}) copy-start(f32[2,1024]{1,0:T(2,128)S(1)} %get-tuple-element.95) | copy-start | bytes 24580
  334.6 4.0 copy-start.2
  357.3 41.9 %copy-start.33 = (f32[2048]{0:T(1024)S(1)}, f32[2048]{0:T(1024)}, u32[]{:S(2)}) copy-start(f32[2048]{0:T(1024)} %param.27) | copy-start | bytes 24580
  357.4 284.3 %reduce-scatter.9.cloned.1.call-start = ((), (), s32[]{:S(2)}) async-start(), calls=%async_computation.13 | async-start | bytes 10485760 | tf_op jit(solution)/shard_map/reduce_scatter | solution.py:188
  399.2 35.6 %copy-start.40 = (bf16[2048,2048]{1,0:T(8,128)(2,1)S(1)}, bf16[2048,2048]{1,0:T(8,128)(2,1)}, u32[]{:S(2)}) copy-start(bf16[2048,2048]{1,0:T(8,128)(2,1)} %all-gather.16.cloned.1.call-done) | copy-start | bytes 25165828
  434.8 13.3 %copy-start.15 = (bf16[1024,2,192]{0,2,1:T(8,128)(2,1)S(1)}, bf16[1024,2,192]{0,2,1:T(8,128)(2,1)}, u32[]{:S(2)}) copy-start(bf16[1024,2,192]{0,2,1:T(8,128)(2,1)} %copy-done.14) | copy-start | bytes 2359300
  434.8 13.3 %copy-start.21 = (bf16[2048,2,256]{0,2,1:T(8,128)(2,1)S(1)}, bf16[2048,2,256]{0,2,1:T(8,128)(2,1)}, u32[]{:S(2)}) copy-start(bf16[2048,2,256]{0,2,1:T(8,128)(2,1)} %get-tuple-element.72) | copy-start | bytes 6291460
  434.8 13.3 %copy-start.23 = (bf16[1024,2,64]{0,2,1:T(8,128)(2,1)S(1)}, bf16[1024,2,64]{0,2,1:T(8,128)(2,1)}, u32[]{:S(2)}) copy-start(bf16[1024,2,64]{0,2,1:T(8,128)(2,1)} %copy-done.22) | copy-start | bytes 786436
  455.4 19.5 %copy-start.17 = (f32[1024,64]{0,1:T(8,128)S(1)}, f32[1024,64]{0,1:T(8,128)}, u32[]{:S(2)}) copy-start(f32[1024,64]{0,1:T(8,128)} %copy-done.16) | copy-start | bytes 786436
  476.3 6.2 slice-start
  478.0 4.5 slice-start.1
  482.4 8.4 copy-start.10
  497.0 292.2 %reduce-scatter.5.cloned.1.call-start = ((), (), s32[]{:S(2)}) async-start(), calls=%async_computation.10 | async-start | bytes 10485760 | tf_op jit(solution)/shard_map/reduce_scatter | solution.py:122
  507.3 13.4 %copy-start.35 = (f32[2,1024]{1,0:T(2,128)S(1)}, f32[2,1024]{1,0:T(2,128)}, u32[]{:S(2)}) copy-start(f32[2,1024]{1,0:T(2,128)} %copy-done.34) | copy-start | bytes 24580
  520.7 11.0 %copy-start.20 = (bf16[2048,512]{1,0:T(8,128)(2,1)S(1)}, bf16[2048,512]{1,0:T(8,128)(2,1)}, u32[]{:S(2)}) copy-start(bf16[2048,512]{1,0:T(8,128)(2,1)} %all-gather.14.cloned.1.call-done) | copy-start | bytes 6291460
  540.8 14.8 %copy-start.28 = (f32[2048]{0:T(1024)S(1)}, f32[2048]{0:T(1024)}, u32[]{:S(2)}) copy-start(f32[2048]{0:T(1024)} %param.21) | copy-start | bytes 24580
  540.9 14.8 %copy-start.32 = (f32[1024]{0:T(1024)S(1)}, f32[1024]{0:T(1024)}, u32[]{:S(2)}) copy-start(f32[1024]{0:T(1024)} %copy-done.31) | copy-start | bytes 12292
  540.9 14.8 %copy-start.39 = (f32[1024]{0:T(1024)S(1)}, f32[1024]{0:T(1024)}, u32[]{:S(2)}) copy-start(f32[1024]{0:T(1024)} %copy-done.38) | copy-start | bytes 12292
  540.9 14.8 %copy-start.43 = (f32[2048]{0:T(1024)S(1)}, f32[2048]{0:T(1024)}, u32[]{:S(2)}) copy-start(f32[2048]{0:T(1024)} %param.22) | copy-start | bytes 24580
  540.9 410.1 %reduce-scatter.11.cloned.1.call-start = ((), (), s32[]{:S(2)}) async-start(), calls=%async_computation.14 | async-start | bytes 28311552 | tf_op jit(solution)/shard_map/reduce_scatter | solution.py:209
  541.4 14.3 %copy-start.5 = (bf16[1024,2048]{1,0:T(8,128)(2,1)S(1)}, bf16[1024,2048]{1,0:T(8,128)(2,1)}, u32[]{:S(2)}) copy-start(bf16[1024,2048]{1,0:T(8,128)(2,1)} %all-gather.8.cloned.1.call-done) | copy-start | bytes 12582916
  541.4 14.3 %copy-start.49 = (bf16[1024,2048]{1,0:T(8,128)(2,1)S(1)}, bf16[1024,2048]{1,0:T(8,128)(2,1)}, u32[]{:S(2)}) copy-start(bf16[1024,2048]{1,0:T(8,128)(2,1)} %copy-done.48) | copy-start | bytes 12582916
  555.7 12.6 %copy-start.41 = (bf16[1024,2048]{1,0:T(8,128)(2,1)S(1)}, bf16[1024,2048]{1,0:T(8,128)(2,1)}, u32[]{:S(2)}) copy-start(bf16[1024,2048]{1,0:T(8,128)(2,1)} %all-gather.20.cloned.1.call-done) | copy-start | bytes 12582916
  568.3 2.4 copy-start.45
  643.8 3.1 copy-start
  644.0 145.2 %copy-start.9 = (bf16[256,2048]{1,0:T(8,128)(2,1)S(1)}, bf16[256,2048]{1,0:T(8,128)(2,1)}, u32[]{:S(2)}) copy-start(bf16[256,2048]{1,0:T(8,128)(2,1)} %param.16) | copy-start | bytes 3145732
  644.0 145.2 %copy-start.37 = (f32[2048]{0:T(1024)S(1)}, f32[2048]{0:T(1024)}, u32[]{:S(2)}) copy-start(f32[2048]{0:T(1024)} %param.29) | copy-start | bytes 24580
  954.8 5.9 copy-start.6
  (15 other events, 24.7 us)
Sparse Core Ops, SparseCore 0:
  9.6 83.4 all-gather.7
  95.6 44.0 all-gather.9
  141.5 27.8 all-gather.13
  170.9 80.7 all-gather.19
  253.7 33.0 all-gather.11
  288.5 54.3 all-gather.15
  344.8 54.3 all-gather.17
  401.8 71.7 reduce-scatter.6
  497.2 144.4 reduce-scatter.8
  644.0 145.2 reduce-scatter.4
  793.3 157.6 reduce-scatter.10
where the time goes:
time: 982 us; the launch traced here: 975 us
  waiting for transfers between devices  559 us (57%)
  matrix products  202 us (21%)
  other arithmetic  76.6 us (8%)
  blocking collectives  65.7 us (7%)
  local copies, waits for them, and re-layouts  56.3 us (6%)
  between operations  14.8 us (2%)
    reduce_scatter x1, waiting for transfers between devices, shards(): lax.psum_scatter(mixed, 'tp', scatter_dimension=0, tiled=True)  142 us
    reduce_scatter x1, waiting for transfers between devices, shards(): lax.psum_scatter(jnp.concatenate([column_product(first_cols, grad_flat),...  115 us
    all_gather x1, waiting for transfers between devices, shards(): lax.all_gather(stream_grad, 'tp', axis=0, tiled=True)  82.2 us
    all_gather x1, waiting for transfers between devices, shards(): lax.all_gather(stream_in, 'tp', axis=0, tiled=True)  80.3 us
    psum x1, blocking collectives, shards(): lax.psum((gain_parts[0], gain_parts[1], gain_parts[2], gain_parts[3], out...  42.1 us
    all_gather x1, waiting for transfers between devices, shards(): lax.all_gather(attend_weight, ('fsdp', 'ctx'), axis=0, tiled=True)  41.8 us
    dot_general x4, matrix products, row_product(): jnp.einsum('tf,df->td', left, right, preferred_element_type=jnp.float32)  41.5 us
    dot_general x4, matrix products, column_product(): jnp.einsum('tc,tk->ck', left, right, preferred_element_type=jnp.float32)  38.5 us
  transfers between devices with their start and end apart: 11, of which 10 were waited for; matrix products, arithmetic and copies ran while one was open for 29% of the time, Pallas kernels for 0%

commit v1 on v0

v1 whole, which is shorter than its diff:
```python
from functools import partial
import math

import jax
import jax.numpy as jnp
from jax import lax
from jax.sharding import PartitionSpec as P

ROT = 64
PROMPT = 2048
EPS = 1e-05
F32 = jnp.float32
BF16 = jnp.bfloat16


def dot(left, right):
    return jnp.dot(left, right, preferred_element_type=F32)


def row_product(left, right):
    return jnp.einsum("tf,df->td", left, right, preferred_element_type=F32)


def column_product(left, right):
    return jnp.einsum("tc,tk->ck", left, right, preferred_element_type=F32)


def rotate(values, where_at):
    half_rot = ROT // 2
    frequency = jnp.exp(jnp.arange(half_rot, dtype=F32) * (-2.0 * math.log(10000.0) / ROT))
    angles = where_at.astype(F32)[:, None] * frequency[None, :]
    cosine = jnp.concatenate([jnp.cos(angles), jnp.cos(angles)], -1)[:, None, :]
    sine_rows = jnp.concatenate([jnp.sin(angles), jnp.sin(angles)], -1)[:, None, :]
    rotated_part = values[..., :ROT]
    turned = jnp.concatenate([-rotated_part[..., half_rot:], rotated_part[..., :half_rot]], -1)
    return jnp.concatenate([rotated_part * cosine + turned * sine_rows, values[..., ROT:]], -1)


class SquareLinks:
    blocks = 8
    order = ((0, 0, 0), (1, 0, 0), (0, 1, 0), (1, 1, 0), (0, 0, 1), (1, 0, 1), (0, 1, 1), (1, 1, 1))

    def __init__(self):
        self.f = lax.axis_index("fsdp")
        c = lax.axis_index("ctx")
        self.y, self.c = c // 2, c % 2

    def x_hop(self, v):
        return lax.ppermute(v, "fsdp", [(0, 1), (1, 0)])

    def y_hop(self, v):
        return lax.ppermute(v, "ctx", [(0, 2), (2, 0), (1, 3), (3, 1)])

    def core_hop(self, v):
        return lax.ppermute(v, "ctx", [(0, 1), (1, 0), (2, 3), (3, 2)])

    def place(self, bits):
        a, b, d = bits
        return ((self.f ^ a) * 2 + (self.y ^ b)) * 2 + (self.c ^ d)

    def to_relative(self, v, axis):
        size = v.shape[axis] // self.blocks
        return jnp.concatenate(
            [lax.dynamic_slice_in_dim(v, self.place(bits) * size, size, axis) for bits in self.order], axis
        )

    def to_whole(self, v, axis):
        size = v.shape[axis] // self.blocks
        where = {bits: i for i, bits in enumerate(self.order)}
        table = jnp.array([where[(p // 4, p // 2 % 2, p % 2)] for p in range(8)], jnp.int32)
        return jnp.concatenate(
            [
                lax.dynamic_slice_in_dim(v, table[self.place((p // 4, p // 2 % 2, p % 2))] * size, size, axis)
                for p in range(8)
            ],
            axis,
        )

    def gather(self, block):
        rows = block.shape[0]
        half = rows // 2
        from_x, from_y = self.x_hop(block), self.y_hop(block)
        corner = (self.x_hop(from_y[:half]), self.y_hop(from_x[half:]))
        near = jnp.concatenate([block, from_x, from_y, *corner], 0)
        return jnp.concatenate([near, self.core_hop(near)], 0)

    def scatter(self, near, far):
        near = near.astype(F32) + self.core_hop(far.astype(BF16)).astype(F32)
        rows = near.shape[0] // 4
        half = rows // 2
        own, to_x, to_y, corner = (near[i * rows : (i + 1) * rows] for i in range(4))
        corner = corner.astype(BF16)
        via_x, via_y = self.x_hop(corner[:half]), self.y_hop(corner[half:])
        to_y = jnp.concatenate([to_y[:half] + via_x.astype(F32), to_y[half:]], 0).astype(BF16)
        to_x = jnp.concatenate([to_x[:half], to_x[half:] + via_y.astype(F32)], 0).astype(BF16)
        return own + self.x_hop(to_x).astype(F32) + self.y_hop(to_y).astype(F32)

    def ctx_order(self, v):
        size = v.shape[0] // 4
        return jnp.concatenate(
            [
                lax.dynamic_slice_in_dim(v, ((self.y ^ b) * 2 + (self.c ^ d)) * size, size, 0)
                for b, d in ((0, 0), (1, 0), (0, 1), (1, 1))
            ],
            0,
        )

    def gather_ctx(self, block):
        near = jnp.concatenate([block, self.y_hop(block)], 0)
        return jnp.concatenate([near, self.core_hop(near)], 0)

    def scatter_ctx(self, parts):
        half = parts.shape[0] // 2
        near = parts[:half] + self.core_hop(parts[half:].astype(BF16)).astype(F32)
        rows = half // 2
        return near[:rows] + self.y_hop(near[rows:].astype(BF16)).astype(F32)

    def sum_rows(self, v):
        v = v + self.core_hop(v)
        v = v + self.x_hop(v)
        return v + self.y_hop(v)


class AnyLinks:
    def to_relative(self, v, axis):
        return v

    def to_whole(self, v, axis):
        return v

    def gather(self, block):
        return lax.all_gather(block, ("fsdp", "ctx"), axis=0, tiled=True)

    def scatter(self, near, far):
        whole = jnp.concatenate([near, far], 0).astype(BF16)
        return lax.psum_scatter(whole, ("fsdp", "ctx"), scatter_dimension=0, tiled=True).astype(F32)

    def ctx_order(self, v):
        return v

    def gather_ctx(self, block):
        return lax.all_gather(block, "ctx", axis=0, tiled=True)

    def scatter_ctx(self, parts):
        return lax.psum_scatter(parts, "ctx", scatter_dimension=0, tiled=True)

    def sum_rows(self, v):
        return lax.psum(v, ("fsdp", "ctx"))


def sum_tp(v):
    size = lax.axis_size("tp")
    if size & (size - 1):
        return lax.psum(v, "tp")
    step = 1
    while step < size:
        v = v + lax.ppermute(v, "tp", [(i, i ^ step) for i in range(size)])
        step *= 2
    return v


def attention_probs(query_heads, key_heads, allowed):
    score_scale = 1.0 / math.sqrt(query_heads.shape[-1])
    scores = jnp.einsum("qhd,khd->hqk", query_heads, key_heads, preferred_element_type=F32) * score_scale
    scores = jnp.where(allowed[None], scores, -1e30)
    row_top = jnp.max(scores, -1, keepdims=True)
    exponent = jnp.exp(scores - row_top)
    return exponent / jnp.sum(exponent, -1, keepdims=True)


def shards(
    stream_in,
    stream_grad,
    segments,
    positions,
    first_gain,
    first_shift,
    second_gain,
    second_shift,
    attend_weight,
    attend_bias,
    output_weight,
    expand_weight,
    expand_bias,
    contract_weight,
    output_bias,
):
    square = lax.axis_size("fsdp") == 2 and lax.axis_size("ctx") == 4
    links = SquareLinks() if square else AnyLinks()
    local_rows = attend_weight.shape[0]
    heads_here = attend_bias.shape[0]
    head_size = attend_bias.shape[1] // 3
    hidden_here = expand_bias.shape[0]
    score_scale = 1.0 / math.sqrt(head_size)
    holders = lax.axis_size("ctx")
    holder = lax.axis_index("ctx")
    prompt_here = PROMPT // holders

    in_part = links.to_relative(stream_in, 1)
    grad_part = links.to_relative(stream_grad, 1)
    gains = links.to_relative(jnp.stack([first_gain, first_shift, second_gain, second_shift]), 1)
    full_rows = lax.all_gather(in_part, "tp", axis=0, tiled=True)
    grad_part_late, full_rows = lax.optimization_barrier((grad_part, full_rows))
    grad_rows = lax.all_gather(grad_part_late, "tp", axis=0, tiled=True)
    row_count = full_rows.shape[0]

    attend_all = links.gather(attend_weight.reshape(local_rows, -1))
    expand_all = links.gather(expand_weight)
    contract_all = links.gather(contract_weight)
    output_all = links.gather(output_weight)
    width = attend_all.shape[0]

    row_pos = lax.dynamic_slice_in_dim(positions, holder * row_count, row_count)
    row_seg = lax.dynamic_slice_in_dim(segments, holder * row_count, row_count)
    prompt_pos = links.ctx_order(positions.reshape(holders, row_count)[:, :prompt_here].reshape(-1))
    key_pos = jnp.concatenate([prompt_pos, row_pos[prompt_here:]])
    key_seg = jnp.concatenate([jnp.zeros_like(prompt_pos), row_seg[prompt_here:]])
    allowed = ((key_seg[None, :] == 0) | (key_seg[None, :] == row_seg[:, None])) & (
        key_pos[None, :] <= row_pos[:, None]
    )

    inputs = full_rows.astype(F32)
    center = inputs - jnp.mean(inputs, -1, keepdims=True)
    scale = lax.rsqrt(jnp.mean(center * center, -1, keepdims=True) + EPS)
    unit = center * scale
    first_norm = (unit * gains[0] + gains[1]).astype(BF16)
    second_norm = (unit * gains[2] + gains[3]).astype(BF16)

    projected = dot(first_norm, attend_all).reshape(row_count, heads_here, 3 * head_size) + attend_bias
    query_heads = rotate(projected[..., :head_size], row_pos).astype(BF16)
    key_heads = rotate(projected[..., head_size : 2 * head_size], row_pos).astype(BF16)
    value_heads = projected[..., 2 * head_size :].astype(BF16)
    prompt_pairs = jnp.concatenate([key_heads[:prompt_here], value_heads[:prompt_here]], -1)
    gathered = links.gather_ctx(prompt_pairs)
    all_keys = jnp.concatenate([gathered[..., :head_size], key_heads[prompt_here:]], 0)
    all_values = jnp.concatenate([gathered[..., head_size:], value_heads[prompt_here:]], 0)

    pre_gelu = dot(second_norm, expand_all) + expand_bias
    activated = jax.nn.gelu(pre_gelu, approximate=False).astype(BF16)

    probability = attention_probs(query_heads, all_keys, allowed)
    prob_low = probability.astype(BF16)
    attended = jnp.einsum("hqk,khd->qhd", prob_low, all_values, preferred_element_type=F32)
    attended = attended.astype(BF16).reshape(row_count, heads_here * head_size)
    mixed = (row_product(attended, output_all) + row_product(activated, contract_all)).astype(BF16)
    branch_total = lax.psum_scatter(mixed, "tp", scatter_dimension=0, tiled=True)
    local_inputs = in_part.astype(F32)
    stream_out = links.to_whole(branch_total.astype(F32) + local_inputs, 1) + output_bias
    stream_out = stream_out.astype(BF16)

    grad_attended = dot(grad_rows, output_all).astype(BF16).reshape(row_count, heads_here, head_size)
    grad_activated = dot(grad_rows, contract_all)
    gelu_back = jax.vjp(partial(jax.nn.gelu, approximate=False), pre_gelu)[1]
    grad_pre = gelu_back(grad_activated)[0].astype(BF16)

    grad_prob = jnp.einsum("qhd,khd->hqk", grad_attended, all_values, preferred_element_type=F32)
    inner = jnp.sum(probability * grad_prob, -1, keepdims=True)
    grad_scores = (probability * (grad_prob - inner)).astype(BF16)
    grad_queries = (
        jnp.einsum("hqk,khd->qhd", grad_scores, all_keys, preferred_element_type=F32) * score_scale
    )
    grad_keys = (
        jnp.einsum("hqk,qhd->khd", grad_scores, query_heads, preferred_element_type=F32) * score_scale
    )
    grad_values = jnp.einsum("hqk,qhd->khd", prob_low, grad_attended, preferred_element_type=F32)
    pair_grads = jnp.concatenate([grad_keys, grad_values], -1)
    prompt_grad = links.scatter_ctx(pair_grads[:PROMPT])
    pair_rows = jnp.concatenate([prompt_grad, pair_grads[PROMPT:]], 0)

    def rotate_rows(values):
        return rotate(values, row_pos)

    rotate_back = jax.vjp(rotate_rows, jnp.zeros((row_count, heads_here, head_size), F32))[1]
    grad_projected = jnp.concatenate(
        [rotate_back(grad_queries)[0], rotate_back(pair_rows[..., :head_size])[0], pair_rows[..., head_size:]],
        -1,
    ).astype(BF16)
    grad_flat = grad_projected.reshape(row_count, heads_here * 3 * head_size)

    bias_parts = jnp.concatenate([jnp.sum(grad_flat, 0, dtype=F32), jnp.sum(grad_pre, 0, dtype=F32)])
    bias_sums = links.sum_rows(bias_parts)
    attend_bias_grad = bias_sums[: grad_flat.shape[1]].reshape(attend_bias.shape)
    expand_bias_grad = bias_sums[grad_flat.shape[1] :]

    grad_first = row_product(grad_flat, attend_all)
    grad_second = row_product(grad_pre, expand_all)
    grad_unit = (grad_first * gains[0] + grad_second * gains[2]).astype(BF16)
    local_unit_grad = lax.psum_scatter(grad_unit, "tp", scatter_dimension=0, tiled=True).astype(F32)
    vector_parts = jnp.stack(
        [
            jnp.sum(grad_first * unit, 0),
            jnp.sum(grad_first, 0),
            jnp.sum(grad_second * unit, 0),
            jnp.sum(grad_second, 0),
            jnp.sum(grad_part.astype(F32), 0),
        ]
    )
    norm_sums = sum_tp(links.sum_rows(links.to_whole(vector_parts, 1)))

    local_center = local_inputs - jnp.mean(local_inputs, -1, keepdims=True)
    local_scale = lax.rsqrt(jnp.mean(local_center * local_center, -1, keepdims=True) + EPS)
    local_unit = local_center * local_scale
    input_grad = links.to_whole(
        grad_part.astype(F32)
        + local_scale
        * (
            local_unit_grad
            - jnp.mean(local_unit_grad, -1, keepdims=True)
            - local_unit * jnp.mean(local_unit_grad * local_unit, -1, keepdims=True)
        ),
        1,
    )

    half = width // 2

    def weight_grad(left, right):
        far = column_product(left[:, half:], right).astype(BF16)
        near = column_product(left[:, :half], right)
        return links.scatter(near, far)

    contract_weight_grad = weight_grad(grad_rows, activated)
    expand_weight_grad = weight_grad(second_norm, grad_pre)
    output_weight_grad = weight_grad(grad_rows, attended)
    attend_weight_grad = weight_grad(first_norm, grad_flat).reshape(attend_weight.shape)
    return (
        stream_out,
        input_grad,
        norm_sums[0],
        norm_sums[1],
        norm_sums[2],
        norm_sums[3],
        attend_weight_grad,
        attend_bias_grad,
        output_weight_grad,
        expand_weight_grad,
        expand_bias_grad,
        contract_weight_grad,
        norm_sums[4],
    )


def solution(mesh):
    tokens = P(("fsdp", "ctx", "tp"), None)
    weight = P(("fsdp", "ctx"), "tp")
    heads = P(("fsdp", "ctx"), "tp", None)
    return jax.shard_map(
        shards,
        mesh=mesh,
        in_specs=(
            tokens,
            tokens,
            P("fsdp"),
            P("fsdp"),
            P(),
            P(),
            P(),
            P(),
            heads,
            P("tp", None),
            weight,
            weight,
            P("tp"),
            weight,
            P(),
        ),
        out_specs=(
            tokens,
            tokens,
            P(),
            P(),
            P(),
            P(),
            heads,
            P("tp", None),
            weight,
            weight,
            P("tp"),
            weight,
            P(),
        ),
        check_vma=False,
    )
```

time: 982 us -> 636 us (0.65)
  waiting for transfers between devices: 559 us -> 158 us
  blocking collectives: 65.7 us -> 0 us
  starting transfers between devices: 1.27 us -> 50.1 us
  local copies, waits for them, and re-layouts: 56.3 us -> 99.9 us
  matrix products: 202 us -> 230 us
    all_gather x7 -> x2, waiting for transfers between devices: 261 us -> 0.02 us  [the longest x1 0.02 us: shards(): grad_rows = lax.all_gather(grad_part_late, 'tp', axis=0, tiled=True)]
    ppermute x0 -> x52, waiting for transfers between devices: none -> 158 us  [the longest x20 81.5 us: y_hop(): return lax.ppermute(v, 'ctx', [(0, 2), (2, 0), (1, 3), (3, 1)])]
    reduce_scatter x3 -> x1, waiting for transfers between devices: 152 us -> 0.01 us  [shards(): lax.psum_scatter(grad_unit, 'tp', scatter_dimension=0, tiled=True)]
    reduce_scatter x1, waiting for transfers between devices: 142 us -> 0.02 us  [shards(): lax.psum_scatter(mixed, 'tp', scatter_dimension=0, tiled=True)]
    psum x2 -> x0, blocking collectives: 65.7 us -> none  [the longest x1 42.1 us: shards(): lax.psum((gain_parts[0], gain_parts[1], gain_parts[2], gain_parts[3], out...]
    ppermute x0 -> x52, starting transfers between devices: none -> 49.9 us  [the longest x20 23.6 us: y_hop(): return lax.ppermute(v, 'ctx', [(0, 2), (2, 0), (1, 3), (3, 1)])]
    unnamed x111 -> x206, local copies, waits for them, and re-layouts: 29.6 us -> 58.1 us
    dot_general x16 -> x20, matrix products: 186 us -> 209 us  [the longest x4 61.2 us: dot(): return jnp.dot(left, right, preferred_element_type=F32)]
  transfers between devices with their start and end apart: 11 -> 56, of which waited for: 10 -> 21; matrix products, arithmetic and copies ran while one was open for 29% -> 54% of each run, Pallas kernels for 0% -> 0%
where the time goes in v1:
time: 636 us; the launch traced here: 627 us
  matrix products  230 us (36%)
  waiting for transfers between devices  158 us (25%)
  local copies, waits for them, and re-layouts  99.9 us (16%)
  other arithmetic  68.8 us (11%)
  starting transfers between devices  50.1 us (8%)
  between operations  21 us (3%)
    ppermute x20, waiting for transfers between devices, y_hop(): return lax.ppermute(v, 'ctx', [(0, 2), (2, 0), (1, 3), (3, 1)])  81.5 us
    ppermute x18, waiting for transfers between devices, x_hop(): return lax.ppermute(v, 'fsdp', [(0, 1), (1, 0)])  71.4 us
    dot_general x4, matrix products, dot(): return jnp.dot(left, right, preferred_element_type=F32)  61.2 us
    unnamed x206, local copies, waits for them, and re-layouts  58.1 us
    dot_general x4, matrix products, row_product(): return jnp.einsum('tf,df->td', left, right, preferred_element_type=F32)  53.3 us
    dot_general x8, matrix products, column_product(): return jnp.einsum('tc,tk->ck', left, right, preferred_element_type=F32)  49.5 us
    ppermute x20, starting transfers between devices, y_hop(): return lax.ppermute(v, 'ctx', [(0, 2), (2, 0), (1, 3), (3, 1)])  23.6 us
    ppermute x18, starting transfers between devices, x_hop(): return lax.ppermute(v, 'fsdp', [(0, 1), (1, 0)])  20.8 us
  transfers between devices with their start and end apart: 56, of which 21 were waited for; matrix products, arithmetic and copies ran while one was open for 54% of the time, Pallas kernels for 0%

profile of v1, /device:TPU:0, one launch (start us, length us, event | category | flops | bytes accessed | tf_op | source)
XLA Modules:
  0.0 627.5 jit_solution(16884468335201667676)
XLA Ops:
  7.3 3.0 collective-permute-start.7
  44.3 20.2 %collective-permute-done.2 = bf16[128,1536]{1,0:T(8,128)(2,1)S(1)} collective-permute-done((bf16[128,1536]{1,0:T(8,128)(2,1)S(1)}, bf16[128,1536]{1,0:T(8,128)(2,1)S(1)}, u32[]{:S(2)}, u32[]{:S(2)}) %collective-permute-start.2) | collective-permute-done | bytes 393248 | tf_op jit(solution)/shard_map/ppermute | solution.py:49
  70.1 2.8 constant_dynamic-update-slice_fusion.51
  79.3 4.5 compare_and_fusion
  85.2 5.1 collective-permute-done.13
  91.9 2.8 constant_dynamic-update-slice_fusion.50
  96.2 5.9 collective-permute-done.14
  105.9 3.7 constant_dynamic-update-slice_fusion.29
  109.7 3.0 convert_reduce_fusion
  114.4 4.6 fusion.12
  119.1 10.3 %fusion.130 = f32[1024,1536]{1,0:T(8,128)S(1)} fusion(bf16[1024,2048]{1,0:T(8,128)(2,1)S(1)} %get-tuple-element.47, bf16[2048,1536]{1,0:T(8,128)(2,1)} %constant_dynamic-update-slice_fusion.29), kind=kOutput, calls=%fused_computation.327 | convolution fusion | flops 6442450944 | bytes 16777216 | tf_op jit(solution)/shard_map/dot_general | solution.py:17
  142.5 3.0 collective-permute-done.9
  146.4 15.7 %collective-permute-done.5 = bf16[512,2,512]{2,0,1:T(8,128)(2,1)S(1)} collective-permute-done((bf16[512,2,512]{2,0,1:T(8,128)(2,1)S(1)}, bf16[512,2,512]{2,0,1:T(8,128)(2,1)S(1)}, u32[]{:S(2)}, u32[]{:S(2)}) %collective-permute-start.5) | collective-permute-done | bytes 1048608 | tf_op jit(solution)/shard_map/ppermute | solution.py:52
  162.4 24.9 %collective-permute-done.10 = bf16[128,512]{1,0:T(8,128)(2,1)S(1)} collective-permute-done((bf16[128,512]{1,0:T(8,128)(2,1)S(1)}, bf16[128,512]{1,0:T(8,128)(2,1)S(1)}, u32[]{:S(2)}, u32[]{:S(2)}) %collective-permute-start.10) | collective-permute-done | bytes 131104 | tf_op jit(solution)/shard_map/ppermute | solution.py:52
  195.4 11.0 %collective-permute-done.19 = bf16[128,2048]{1,0:T(8,128)(2,1)S(1)} collective-permute-done((bf16[128,2048]{1,0:T(8,128)(2,1)S(1)}, bf16[128,2048]{1,0:T(8,128)(2,1)S(1)}, u32[]{:S(2)}, u32[]{:S(2)}) %collective-permute-start.19) | collective-permute-done | bytes 524320 | tf_op jit(solution)/shard_map/ppermute | solution.py:49
  208.2 3.2 copy-done.35
  214.5 3.0 copy-done.34
  219.8 13.6 %fusion.121 = (f32[2,1024]{1,0:T(2,128)S(1)}, f32[2,1024,2560]{2,1,0:T(8,128)}) fusion(pred[1024,2560]{1,0:T(8,128)(4,1)} %compare_and_fusion, bf16[1024,2,192]{2,0,1:T(8,128)(2,1)S(1)} %copy-done.28, bf16[1024,2,64]{2,0,1:T(8,128)(2,1)S(1)} %copy-done.29, bf16[1024,2,192]{2,0,1:T(8,128)(2,1)S(1)} %get-tuple-element.64, ...), kind=kOutput, calls=%fused_computation.322 | convolution fusion | flops 2719222272 | bytes 27795456 | tf_op jit(solution)/shard_map/sub | solution.py:167
  233.5 6.3 %convolution_convert_fusion.3 = bf16[1024,512]{0,1:T(8,128)(2,1)} fusion(bf16[1024,2048]{1,0:T(8,128)(2,1)} %all-gather.5.cloned.1.call-done, bf16[2048,512]{1,0:T(8,128)(2,1)} %copy-done.38), kind=kOutput, calls=%fused_computation.125 | convolution fusion | flops 2148007936 | bytes 7340032 | tf_op jit(solution)/shard_map/dot_general | solution.py:17
  239.8 13.9 %multiply_reduce_fusion = (f32[2,1024]{1,0:T(2,128)S(1)}, f32[2,1024,2560]{2,1,0:T(8,128)}) fusion(f32[2,1024,2560]{2,1,0:T(8,128)} %get-tuple-element.144, f32[2,1024]{1,0:T(2,128)S(1)} %get-tuple-element.143, bf16[1024,2,256]{0,2,1:T(8,128)(2,1)} %bitcast.115, bf16[512,2,256]{2,0,1:T(8,128)(2,1)} %get-tuple-element.66, bf16[2048,2,256]{2,0,1:T(8,128)(2,1)S(1)} %copy-done.24), kind=kOutput, calls=%fused_computation.2 | convolution fusion | flops 2705324032 | bytes 45629440 | tf_op jit(solution)/shard_map/qhd,khd->hqk/dot_general | solution.py:256
  253.7 14.0 %multiply_convert_fusion = bf16[2,1024,2560]{2,1,0:T(8,128)(2,1)S(1)} fusion(f32[2,1024,2560]{2,1,0:T(8,128)} %get-tuple-element.146, f32[2,1024]{1,0:T(2,128)S(1)} %get-tuple-element.145, f32[2,1024,2560]{2,1,0:T(8,128)} %get-tuple-element.144, f32[2,1024]{1,0:T(2,128)S(1)} %get-tuple-element.143), kind=kLoop, calls=%fused_computation.1 | loop fusion | flops 20971520 | bytes 52445184 | tf_op jit(solution)/shard_map/convert_element_type | solution.py:258
  267.8 3.9 copy-done.5
  271.7 6.8 %multiply_bitcast_fusion = f32[2560,2,256]{2,0,1:T(8,128)} fusion(bf16[2,1024,2560]{2,1,0:T(8,128)(2,1)S(1)} %multiply_convert_fusion, bf16[1024,2,192]{2,0,1:T(8,128)(2,1)S(1)} %copy-done.28, bf16[1024,2,64]{2,0,1:T(8,128)(2,1)S(1)} %copy-done.30), kind=kOutput, calls=%fused_computation.59 | convolution fusion | flops 2687762432 | bytes 16777216 | tf_op jit(solution)/shard_map/hqk,qhd->khd/dot_general | solution.py:263
  278.5 14.2 %fusion.30 = f32[2560,2,256]{2,0,1:T(8,128)} fusion(bf16[1024,2,256]{0,2,1:T(8,128)(2,1)} %bitcast.116, f32[2,1024,2560]{2,1,0:T(8,128)} %get-tuple-element.144, f32[2,1024]{1,0:T(2,128)S(1)} %get-tuple-element.143), kind=kOutput, calls=%fused_computation.64 | convolution fusion | flops 2694840320 | bytes 27271168 | tf_op jit(solution)/shard_map/hqk,qhd->khd/dot_general | solution.py:265
  295.3 5.1 constant_dynamic-update-slice_fusion.63
  300.4 11.4 %fusion.131 = f32[1024,2048]{1,0:T(8,128)S(1)} fusion(bf16[1024,2048]{1,0:T(8,128)(2,1)S(1)} %copy-done.18, bf16[2048,2048]{1,0:T(8,128)(2,1)} %copy-done.34), kind=kOutput, calls=%fused_computation.328 | convolution fusion | flops 8589934592 | bytes 20971520 | tf_op jit(solution)/shard_map/dot_general | solution.py:17
  315.5 33.1 %convert_reduce_fusion.1 = (f32[2048]{0:T(1024)S(1)}, bf16[1024,2048]{1,0:T(8,128)(2,1)}, f32[1024,2048]{1,0:T(8,128)}) fusion(f32[1024,2048]{1,0:T(8,128)S(1)} %fusion.131, f32[2048]{0:T(1024)S(1)} %copy-done.52, bf16[1024,2048]{1,0:T(8,128)(2,1)} %all-gather.5.cloned.1.call-done, bf16[2048,2048]{1,0:T(8,128)(2,1)} %constant_dynamic-update-slice_fusion.63), kind=kOutput, calls=%fused_computation.34 | convolution fusion | flops 8747218944 | bytes 33570816 | tf_op jit(solution)/shard_map/dot_general | solution.py:17
  348.6 5.8 multiply_bitcast_fusion.1
  362.2 2.9 copy.47
  365.2 12.0 %fusion.133 = f32[1024,2048]{1,0:T(8,128)} fusion(bf16[1024,1536]{0,1:T(8,128)(2,1)} %bitcast.79, bf16[2048,1536]{1,0:T(8,128)(2,1)} %constant_dynamic-update-slice_fusion.29), kind=kOutput, calls=%fused_computation.330 | convolution fusion | flops 6442450944 | bytes 17825792 | tf_op jit(solution)/shard_map/tf,df->td/dot_general | solution.py:21
  377.2 18.0 %fusion.104 = (f32[2048]{0:T(1024)S(1)}, f32[2048]{0:T(1024)S(1)}, bf16[1024,2048]{1,0:T(8,128)(2,1)}, f32[2048]{0:T(1024)S(1)}, f32[2048]{0:T(1024)S(1)}) fusion(f32[1024]{0:T(1024)S(1)} %copy-done.48, f32[1024]{0:T(1024)S(1)} %copy-done.37, bf16[1024,2048]{1,0:T(8,128)(2,1)S(1)} %copy-done.1, f32[2048]{0:T(1024)S(1)} %bitcast.96, ...), kind=kOutput, calls=%fused_computation.306 | convolution fusion | flops 8617189376 | bytes 29417472 | tf_op jit(solution)/shard_map/tf,df->td/dot_general | solution.py:21
  396.9 11.4 %fusion.77 = bf16[2,256,1024]{2,1,0:T(8,128)(2,1)} fusion(bf16[512,2,256]{2,0,1:T(8,128)(2,1)S(1)} %copy-done.32, bf16[2048,2,256]{2,0,1:T(8,128)(2,1)S(1)} %copy-done.25, f32[2,1024,2560]{2,1,0:T(8,128)} %get-tuple-element.144, f32[2,1024]{1,0:T(2,128)S(1)} %copy-done.55), kind=kOutput, calls=%fused_computation.124 | convolution fusion | flops 2700607488 | bytes 24649728 | tf_op jit(solution)/shard_map/hqk,khd->qhd/dot_general | solution.py:243
  408.3 8.6 %convolution_convert_fusion.2 = bf16[1024,2048]{1,0:T(8,128)(2,1)} fusion(bf16[1024,2048]{1,0:T(8,128)(2,1)} %get-tuple-element.26, bf16[1024,2048]{1,0:T(8,128)(2,1)S(1)} %copy-done.19), kind=kOutput, calls=%fused_computation.75 | convolution fusion | flops 4297064448 | bytes 10485760 | tf_op jit(solution)/shard_map/tc,tk->ck/dot_general | solution.py:25
  418.7 8.1 %multiply_convert_fusion.1 = bf16[1024,2048]{1,0:T(8,128)(2,1)S(1)} fusion(f32[1024,2048]{1,0:T(8,128)} %get-tuple-element.27, f32[1024,2048]{1,0:T(8,128)} %copy-done.6, f32[2048]{0:T(1024)S(1)} %copy-done.52), kind=kLoop, calls=%fused_computation.38 | loop fusion | flops 8388608 | bytes 20979712 | tf_op jit(solution)/shard_map/convert_element_type | solution.py:239
  426.8 15.1 %fusion.132 = f32[1024,2048]{1,0:T(8,128)} fusion(bf16[1024,2048]{1,0:T(8,128)(2,1)S(1)} %multiply_convert_fusion.1, bf16[2048,2048]{1,0:T(8,128)(2,1)} %constant_dynamic-update-slice_fusion.63), kind=kOutput, calls=%fused_computation.329 | convolution fusion | flops 8589934592 | bytes 20971520 | tf_op jit(solution)/shard_map/tf,df->td/dot_general | solution.py:21
  444.3 6.3 %convolution_convert_fusion.1 = bf16[1024,2048]{1,0:T(8,128)(2,1)} fusion(bf16[1024,2048]{1,0:T(8,128)(2,1)S(1)} %multiply_convert_fusion.1, bf16[1024,2048]{1,0:T(8,128)(2,1)S(1)} %copy-done.62), kind=kOutput, calls=%fused_computation.74 | convolution fusion | flops 4297064448 | bytes 10485760 | tf_op jit(solution)/shard_map/tc,tk->ck/dot_general | solution.py:25
  454.8 8.1 %add_convert_fusion.2 = bf16[1024,2048]{1,0:T(8,128)(2,1)} fusion(f32[1024,2048]{1,0:T(8,128)} %fusion.132, bf16[1024,512]{0,1:T(8,128)(2,1)} %bitcast.112, bf16[2048,512]{1,0:T(8,128)(2,1)S(1)} %copy-done.39), kind=kOutput, calls=%fused_computation.37 | convolution fusion | flops 2151677952 | bytes 15728640 | tf_op jit(solution)/shard_map/tf,df->td/dot_general | solution.py:21
  467.1 6.8 %convolution_convert_fusion = bf16[1024,1536]{1,0:T(8,128)(2,1)} fusion(bf16[1024,1536]{0,1:T(8,128)(2,1)S(1)} %bitcast.80, bf16[1024,2048]{1,0:T(8,128)(2,1)} %copy-done.16), kind=kOutput, calls=%fused_computation.73 | convolution fusion | flops 3222798336 | bytes 8388608 | tf_op jit(solution)/shard_map/tc,tk->ck/dot_general | solution.py:25
  475.3 8.9 %fusion.128 = (bf16[1024,2048]{1,0:T(8,128)(2,1)S(1)}, f32[1024,2048]{1,0:T(8,128)S(1)}) fusion(bf16[1024,2048]{1,0:T(8,128)(2,1)} %collective-permute-done.42, bf16[1024,2048]{1,0:T(8,128)(2,1)} %get-tuple-element.26, bf16[1024,2048]{1,0:T(8,128)(2,1)} %get-tuple-element.48), kind=kOutput, calls=%fused_computation.325 | convolution fusion | flops 4301258752 | bytes 23068672 | tf_op jit(solution)/shard_map/tc,tk->ck/dot_general | solution.py:25
  486.8 8.6 %fusion.129 = (bf16[1024,2048]{1,0:T(8,128)(2,1)}, f32[1024,2048]{1,0:T(8,128)S(1)}) fusion(bf16[1024,2048]{1,0:T(8,128)(2,1)} %collective-permute-done.47, bf16[1024,2048]{1,0:T(8,128)(2,1)S(1)} %copy-done.13, bf16[1024,2048]{1,0:T(8,128)(2,1)} %all-gather.5.cloned.1.call-done), kind=kOutput, calls=%fused_computation.326 | convolution fusion | flops 4301258752 | bytes 23068672 | tf_op jit(solution)/shard_map/tc,tk->ck/dot_general | solution.py:25
  502.8 9.2 %collective-permute-done.50 = bf16[128,2048]{1,0:T(8,128)(2,1)S(1)} collective-permute-done((bf16[128,2048]{1,0:T(8,128)(2,1)S(1)}, bf16[128,2048]{1,0:T(8,128)(2,1)S(1)}, u32[]{:S(2)}, u32[]{:S(2)}) %collective-permute-start.50) | collective-permute-done | bytes 524320 | tf_op jit(solution)/shard_map/ppermute | solution.py:49
  513.8 7.7 %fusion.126 = (bf16[1024,1536]{1,0:T(8,128)(2,1)}, f32[1024,1536]{1,0:T(8,128)}) fusion(bf16[1024,1536]{1,0:T(8,128)(2,1)} %collective-permute-done.29, bf16[1024,1536]{0,1:T(8,128)(2,1)S(1)} %bitcast.81, bf16[1024,2048]{1,0:T(8,128)(2,1)S(1)} %copy-done.17), kind=kOutput, calls=%fused_computation.323 | convolution fusion | flops 3225944064 | bytes 17825792 | tf_op jit(solution)/shard_map/tc,tk->ck/dot_general | solution.py:25
  526.2 15.7 %collective-permute-done.32 = bf16[128,1536]{1,0:T(8,128)(2,1)S(1)} collective-permute-done((bf16[128,1536]{1,0:T(8,128)(2,1)S(1)}, bf16[128,1536]{1,0:T(8,128)(2,1)S(1)}, u32[]{:S(2)}, u32[]{:S(2)}) %collective-permute-start.32) | collective-permute-done | bytes 393248 | tf_op jit(solution)/shard_map/ppermute | solution.py:49
  546.6 3.3 fusion.48
  549.9 16.9 %collective-permute-done.51 = bf16[256,2048]{1,0:T(8,128)(2,1)S(1)} collective-permute-done((bf16[256,2048]{1,0:T(8,128)(2,1)S(1)}, bf16[256,2048]{1,0:T(8,128)(2,1)S(1)}, u32[]{:S(2)}, u32[]{:S(2)}) %collective-permute-start.51) | collective-permute-done | bytes 1048608 | tf_op jit(solution)/shard_map/ppermute | solution.py:52
  569.8 12.4 %collective-permute-done.33 = bf16[256,1536]{1,0:T(8,128)(2,1)S(1)} collective-permute-done((bf16[256,1536]{1,0:T(8,128)(2,1)S(1)}, bf16[256,1536]{1,0:T(8,128)(2,1)S(1)}, u32[]{:S(2)}, u32[]{:S(2)}) %collective-permute-start.33) | collective-permute-done | bytes 786464 | tf_op jit(solution)/shard_map/ppermute | solution.py:52
  587.6 4.3 convert_reduce_fusion.5
  602.6 3.3 collective-permute-done.25
  (414 shorter events, 163.9 us)
Async XLA Ops:
  7.2 102.4 %all-gather.3.cloned.1.call-start = ((), (), s32[]{:S(2)}) async-start(), calls=%async_computation.2 | async-start | bytes 5242880 | tf_op jit(solution)/shard_map/all_gather | solution.py:202
  7.3 132.6 %collective-permute-start.7 = (bf16[256,512]{1,0:T(8,128)(2,1)}, bf16[256,512]{1,0:T(8,128)(2,1)}, u32[]{:S(2)}, u32[]{:S(2)}) collective-permute-start(bf16[256,512]{1,0:T(8,128)(2,1)} %param.28), channel_id=1, source_target_pairs={{0,16},{16,0},{1,17},{17,1},{2,18},{18,2},{3,19},{19,3},{4,20},{20... | collective-permute-start | bytes 786440 | tf_op jit(solution)/shard_map/ppermute | solution.py:49
  10.3 128.5 %collective-permute-start.8 = (bf16[256,512]{1,0:T(8,128)(2,1)}, bf16[256,512]{1,0:T(8,128)(2,1)S(1)}, u32[]{:S(2)}, u32[]{:S(2)}) collective-permute-start(bf16[256,512]{1,0:T(8,128)(2,1)} %param.28), channel_id=1, source_target_pairs={{0,8},{8,0},{4,12},{12,4},{1,9},{9,1},{5,13},{13,5},{2,10},{10,2},... | collective-permute-start | bytes 786440 | tf_op jit(solution)/shard_map/ppermute | solution.py:52
  13.0 22.2 %collective-permute-start.1 = (bf16[256,1536]{1,0:T(8,128)(2,1)S(1)}, bf16[256,1536]{1,0:T(8,128)(2,1)}, u32[]{:S(2)}, u32[]{:S(2)}) collective-permute-start(bf16[256,1536]{1,0:T(8,128)(2,1)S(1)} %bitcast.82), channel_id=1, source_target_pairs={{0,8},{8,0},{4,12},{12,4},{1,9},{9,1},{5,13},{13,5},{2,10},{10,2},... | collective-permute-start | bytes 2359304 | tf_op jit(solution)/shard_map/ppermute | solution.py:52
  13.6 23.1 %collective-permute-start = (bf16[256,1536]{1,0:T(8,128)(2,1)S(1)}, bf16[256,1536]{1,0:T(8,128)(2,1)}, u32[]{:S(2)}, u32[]{:S(2)}) collective-permute-start(bf16[256,1536]{1,0:T(8,128)(2,1)S(1)} %bitcast.83), channel_id=1, source_target_pairs={{0,16},{16,0},{1,17},{17,1},{2,18},{18,2},{3,19},{19,3},{4,20},{20... | collective-permute-start | bytes 2359304 | tf_op jit(solution)/shard_map/ppermute | solution.py:49
  13.7 70.1 %collective-permute-start.12 = (bf16[256,2048]{1,0:T(8,128)(2,1)}, bf16[256,2048]{1,0:T(8,128)(2,1)}, u32[]{:S(2)}, u32[]{:S(2)}) collective-permute-start(bf16[256,2048]{1,0:T(8,128)(2,1)} %param.29), channel_id=1, source_target_pairs={{0,16},{16,0},{1,17},{17,1},{2,18},{18,2},{3,19},{19,3},{4,20},{20... | collective-permute-start | bytes 3145736 | tf_op jit(solution)/shard_map/ppermute | solution.py:49
  24.1 209.3 %all-gather.5.cloned.1.call-start = ((), (), s32[]{:S(2)}) async-start(), calls=%async_computation.4 | async-start | bytes 5242880 | tf_op jit(solution)/shard_map/all_gather | solution.py:204
  36.2 28.3 %collective-permute-start.2 = (bf16[128,1536]{1,0:T(8,128)(2,1)S(1)}, bf16[128,1536]{1,0:T(8,128)(2,1)S(1)}, u32[]{:S(2)}, u32[]{:S(2)}) collective-permute-start(bf16[128,1536]{1,0:T(8,128)(2,1)S(1)} %slice.382), channel_id=1, source_target_pairs={{0,16},{16,0},{1,17},{17,1},{2,18},{18,2},{3,19},{19,3},{4,20},{20... | collective-permute-start | bytes 1179656 | tf_op jit(solution)/shard_map/ppermute | solution.py:49
  37.8 29.5 %collective-permute-start.3 = (bf16[128,1536]{1,0:T(8,128)(2,1)S(1)}, bf16[128,1536]{1,0:T(8,128)(2,1)S(1)}, u32[]{:S(2)}, u32[]{:S(2)}) collective-permute-start(bf16[128,1536]{1,0:T(8,128)(2,1)S(1)} %slice.383), channel_id=1, source_target_pairs={{0,8},{8,0},{4,12},{12,4},{1,9},{9,1},{5,13},{13,5},{2,10},{10,2},... | collective-permute-start | bytes 1179656 | tf_op jit(solution)/shard_map/ppermute | solution.py:52
  64.5 25.7 %collective-permute-start.13 = (bf16[256,2048]{1,0:T(8,128)(2,1)}, bf16[256,2048]{1,0:T(8,128)(2,1)S(1)}, u32[]{:S(2)}, u32[]{:S(2)}) collective-permute-start(bf16[256,2048]{1,0:T(8,128)(2,1)} %param.29), channel_id=1, source_target_pairs={{0,8},{8,0},{4,12},{12,4},{1,9},{9,1},{5,13},{13,5},{2,10},{10,2},... | collective-permute-start | bytes 3145736 | tf_op jit(solution)/shard_map/ppermute | solution.py:52
  68.2 37.7 %collective-permute-start.4 = (bf16[1024,1536]{1,0:T(8,128)(2,1)}, bf16[1024,1536]{1,0:T(8,128)(2,1)}, u32[]{:S(2)}, u32[]{:S(2)}) collective-permute-start(bf16[1024,1536]{1,0:T(8,128)(2,1)} %get-tuple-element.110), channel_id=1, source_target_pairs={{0,4},{4,0},{8,12},{12,8},{1,5},{5,1},{9,13},{13,9},{2,6},{6,2},{1... | collective-permute-start | bytes 9437192 | tf_op jit(solution)/shard_map/ppermute | solution.py:55
  84.9 19.8 %collective-permute-start.15 = (bf16[128,2048]{1,0:T(8,128)(2,1)S(1)}, bf16[128,2048]{1,0:T(8,128)(2,1)S(1)}, u32[]{:S(2)}, u32[]{:S(2)}) collective-permute-start(bf16[128,2048]{1,0:T(8,128)(2,1)S(1)} %slice.404), channel_id=1, source_target_pairs={{0,8},{8,0},{4,12},{12,4},{1,9},{9,1},{5,13},{13,5},{2,10},{10,2},... | collective-permute-start | bytes 1572872 | tf_op jit(solution)/shard_map/ppermute | solution.py:52
  90.3 11.8 %collective-permute-start.14 = (bf16[128,2048]{1,0:T(8,128)(2,1)S(1)}, bf16[128,2048]{1,0:T(8,128)(2,1)S(1)}, u32[]{:S(2)}, u32[]{:S(2)}) collective-permute-start(bf16[128,2048]{1,0:T(8,128)(2,1)S(1)} %slice.403), channel_id=1, source_target_pairs={{0,16},{16,0},{1,17},{17,1},{2,18},{18,2},{3,19},{19,3},{4,20},{20... | collective-permute-start | bytes 1572872 | tf_op jit(solution)/shard_map/ppermute | solution.py:49
  102.2 88.2 %collective-permute-start.17 = (bf16[256,2048]{1,0:T(8,128)(2,1)}, bf16[256,2048]{1,0:T(8,128)(2,1)S(1)}, u32[]{:S(2)}, u32[]{:S(2)}) collective-permute-start(bf16[256,2048]{1,0:T(8,128)(2,1)} %param.31), channel_id=1, source_target_pairs={{0,16},{16,0},{1,17},{17,1},{2,18},{18,2},{3,19},{19,3},{4,20},{20... | collective-permute-start | bytes 3145736 | tf_op jit(solution)/shard_map/ppermute | solution.py:49
  105.9 102.3 %collective-permute-start.16 = (bf16[1024,2048]{1,0:T(8,128)(2,1)}, bf16[1024,2048]{1,0:T(8,128)(2,1)}, u32[]{:S(2)}, u32[]{:S(2)}) collective-permute-start(bf16[1024,2048]{1,0:T(8,128)(2,1)} %get-tuple-element.102), channel_id=1, source_target_pairs={{0,4},{4,0},{8,12},{12,8},{1,5},{5,1},{9,13},{13,9},{2,6},{6,2},{1... | collective-permute-start | bytes 12582920 | tf_op jit(solution)/shard_map/ppermute | solution.py:55
  109.6 476.0 %reduce-scatter.5.cloned.1.call-start = ((), (), s32[]{:S(2)}) async-start(), calls=%async_computation.5 | async-start | bytes 5242880 | tf_op jit(solution)/shard_map/reduce_scatter | solution.py:288
  135.7 26.4 %collective-permute-start.5 = (bf16[512,2,512]{2,0,1:T(8,128)(2,1)S(1)}, bf16[512,2,512]{2,0,1:T(8,128)(2,1)S(1)}, u32[]{:S(2)}, u32[]{:S(2)}) collective-permute-start(bf16[512,2,512]{2,0,1:T(8,128)(2,1)S(1)} %pad_maximum_fusion.7), channel_id=1, source_target_pairs={{0,8},{8,0},{4,12},{12,4},{1,9},{9,1},{5,13},{13,5},{2,10},{10,2},... | collective-permute-start | bytes 3145736 | tf_op jit(solution)/shard_map/ppermute | solution.py:52
  138.8 53.4 %collective-permute-start.18 = (bf16[256,2048]{1,0:T(8,128)(2,1)}, bf16[256,2048]{1,0:T(8,128)(2,1)S(1)}, u32[]{:S(2)}, u32[]{:S(2)}) collective-permute-start(bf16[256,2048]{1,0:T(8,128)(2,1)} %param.31), channel_id=1, source_target_pairs={{0,8},{8,0},{4,12},{12,4},{1,9},{9,1},{5,13},{13,5},{2,10},{10,2},... | collective-permute-start | bytes 3145736 | tf_op jit(solution)/shard_map/ppermute | solution.py:52
  145.6 41.7 %collective-permute-start.10 = (bf16[128,512]{1,0:T(8,128)(2,1)S(1)}, bf16[128,512]{1,0:T(8,128)(2,1)S(1)}, u32[]{:S(2)}, u32[]{:S(2)}) collective-permute-start(bf16[128,512]{1,0:T(8,128)(2,1)S(1)} %slice.400), channel_id=1, source_target_pairs={{0,8},{8,0},{4,12},{12,4},{1,9},{9,1},{5,13},{13,5},{2,10},{10,2},... | collective-permute-start | bytes 393224 | tf_op jit(solution)/shard_map/ppermute | solution.py:52
  162.3 51.8 %collective-permute-start.6 = (bf16[1024,2,512]{2,0,1:T(8,128)(2,1)S(1)}, bf16[1024,2,512]{2,0,1:T(8,128)(2,1)S(1)}, u32[]{:S(2)}, u32[]{:S(2)}) collective-permute-start(bf16[1024,2,512]{2,0,1:T(8,128)(2,1)S(1)} %pad_maximum_fusion.2), channel_id=1, source_target_pairs={{0,4},{4,0},{8,12},{12,8},{1,5},{5,1},{9,13},{13,9},{2,6},{6,2},{1... | collective-permute-start | bytes 6291464 | tf_op jit(solution)/shard_map/ppermute | solution.py:55
  187.2 8.0 %collective-permute-start.11 = (bf16[1024,512]{1,0:T(8,128)(2,1)S(1)}, bf16[1024,512]{1,0:T(8,128)(2,1)S(1)}, u32[]{:S(2)}, u32[]{:S(2)}) collective-permute-start(bf16[1024,512]{1,0:T(8,128)(2,1)S(1)} %get-tuple-element.120), channel_id=1, source_target_pairs={{0,4},{4,0},{8,12},{12,8},{1,5},{5,1},{9,13},{13,9},{2,6},{6,2},{1... | collective-permute-start | bytes 3145736 | tf_op jit(solution)/shard_map/ppermute | solution.py:55
  190.4 16.8 %collective-permute-start.20 = (bf16[128,2048]{1,0:T(8,128)(2,1)S(1)}, bf16[128,2048]{1,0:T(8,128)(2,1)S(1)}, u32[]{:S(2)}, u32[]{:S(2)}) collective-permute-start(bf16[128,2048]{1,0:T(8,128)(2,1)S(1)} %slice.406), channel_id=1, source_target_pairs={{0,8},{8,0},{4,12},{12,4},{1,9},{9,1},{5,13},{13,5},{2,10},{10,2},... | collective-permute-start | bytes 1572872 | tf_op jit(solution)/shard_map/ppermute | solution.py:52
  192.3 14.1 %collective-permute-start.19 = (bf16[128,2048]{1,0:T(8,128)(2,1)S(1)}, bf16[128,2048]{1,0:T(8,128)(2,1)S(1)}, u32[]{:S(2)}, u32[]{:S(2)}) collective-permute-start(bf16[128,2048]{1,0:T(8,128)(2,1)S(1)} %slice.405), channel_id=1, source_target_pairs={{0,16},{16,0},{1,17},{17,1},{2,18},{18,2},{3,19},{19,3},{4,20},{20... | collective-permute-start | bytes 1572872 | tf_op jit(solution)/shard_map/ppermute | solution.py:49
  208.2 87.1 %collective-permute-start.21 = (bf16[1024,2048]{1,0:T(8,128)(2,1)}, bf16[1024,2048]{1,0:T(8,128)(2,1)}, u32[]{:S(2)}, u32[]{:S(2)}) collective-permute-start(bf16[1024,2048]{1,0:T(8,128)(2,1)} %get-tuple-element.106), channel_id=1, source_target_pairs={{0,4},{4,0},{8,12},{12,8},{1,5},{5,1},{9,13},{13,9},{2,6},{6,2},{1... | collective-permute-start | bytes 12582920 | tf_op jit(solution)/shard_map/ppermute | solution.py:55
  295.2 16.6 %collective-permute-start.22 = (bf16[1024,2,512]{2,0,1:T(8,128)(2,1)S(1)}, bf16[1024,2,512]{2,0,1:T(8,128)(2,1)S(1)}, u32[]{:S(2)}, u32[]{:S(2)}) collective-permute-start(bf16[1024,2,512]{2,0,1:T(8,128)(2,1)S(1)} %fusion.34), channel_id=1, source_target_pairs={{0,4},{4,0},{8,12},{12,8},{1,5},{5,1},{9,13},{13,9},{2,6},{6,2},{1... | collective-permute-start | bytes 6291464 | tf_op jit(solution)/shard_map/ppermute | solution.py:55
  314.2 40.9 %collective-permute-start.23 = (bf16[512,2,512]{2,0,1:T(8,128)(2,1)}, bf16[512,2,512]{2,0,1:T(8,128)(2,1)}, u32[]{:S(2)}, u32[]{:S(2)}) collective-permute-start(bf16[512,2,512]{2,0,1:T(8,128)(2,1)} %slice.555), channel_id=1, source_target_pairs={{0,8},{8,0},{4,12},{12,4},{1,9},{9,1},{5,13},{13,5},{2,10},{10,2},... | collective-permute-start | bytes 3145736 | tf_op jit(solution)/shard_map/ppermute | solution.py:52
  395.3 192.3 %reduce-scatter.3.cloned.1.call-start = ((), (), s32[]{:S(2)}) async-start(), calls=%async_computation.3 | async-start | bytes 5242880 | tf_op jit(solution)/shard_map/reduce_scatter | solution.py:246
  416.8 58.4 %collective-permute-start.42 = (bf16[1024,2048]{1,0:T(8,128)(2,1)}, bf16[1024,2048]{1,0:T(8,128)(2,1)}, u32[]{:S(2)}, u32[]{:S(2)}) collective-permute-start(bf16[1024,2048]{1,0:T(8,128)(2,1)} %convolution_convert_fusion.2), channel_id=1, source_target_pairs={{0,4},{4,0},{8,12},{12,8},{1,5},{5,1},{9,13},{13,9},{2,6},{6,2},{1... | collective-permute-start | bytes 12582920 | tf_op jit(solution)/shard_map/ppermute | solution.py:55
  418.6 23.4 %collective-permute-start.37 = (bf16[1024,512]{1,0:T(8,128)(2,1)S(1)}, bf16[1024,512]{1,0:T(8,128)(2,1)S(1)}, u32[]{:S(2)}, u32[]{:S(2)}) collective-permute-start(bf16[1024,512]{1,0:T(8,128)(2,1)S(1)} %fusion.74), channel_id=1, source_target_pairs={{0,4},{4,0},{8,12},{12,8},{1,5},{5,1},{9,13},{13,9},{2,6},{6,2},{1... | collective-permute-start | bytes 3145736 | tf_op jit(solution)/shard_map/ppermute | solution.py:55
  450.5 36.3 %collective-permute-start.47 = (bf16[1024,2048]{1,0:T(8,128)(2,1)}, bf16[1024,2048]{1,0:T(8,128)(2,1)}, u32[]{:S(2)}, u32[]{:S(2)}) collective-permute-start(bf16[1024,2048]{1,0:T(8,128)(2,1)} %convolution_convert_fusion.1), channel_id=1, source_target_pairs={{0,4},{4,0},{8,12},{12,8},{1,5},{5,1},{9,13},{13,9},{2,6},{6,2},{1... | collective-permute-start | bytes 12582920 | tf_op jit(solution)/shard_map/ppermute | solution.py:55
  450.7 13.0 %collective-permute-start.41 = (bf16[256,512]{1,0:T(8,128)(2,1)S(1)}, bf16[256,512]{1,0:T(8,128)(2,1)}, u32[]{:S(2)}, u32[]{:S(2)}) collective-permute-start(bf16[256,512]{1,0:T(8,128)(2,1)S(1)} %pad_maximum_fusion.18), channel_id=1, source_target_pairs={{0,8},{8,0},{4,12},{12,4},{1,9},{9,1},{5,13},{13,5},{2,10},{10,2},... | collective-permute-start | bytes 786440 | tf_op jit(solution)/shard_map/ppermute | solution.py:52
  453.3 10.5 %collective-permute-start.39 = (bf16[256,512]{1,0:T(8,128)(2,1)}, bf16[256,512]{1,0:T(8,128)(2,1)}, u32[]{:S(2)}, u32[]{:S(2)}) collective-permute-start(bf16[256,512]{1,0:T(8,128)(2,1)} %pad_maximum_fusion.17), channel_id=1, source_target_pairs={{0,16},{16,0},{1,17},{17,1},{2,18},{18,2},{3,19},{19,3},{4,20},{20... | collective-permute-start | bytes 786440 | tf_op jit(solution)/shard_map/ppermute | solution.py:49
  454.7 8.2 %collective-permute-start.34 = (f32[3584]{0:T(1024)S(1)}, f32[3584]{0:T(1024)S(1)}, u32[]{:S(2)}, u32[]{:S(2)}) collective-permute-start(f32[3584]{0:T(1024)S(1)} %pad_maximum_fusion.20), channel_id=1, source_target_pairs={{0,4},{4,0},{8,12},{12,8},{1,5},{5,1},{9,13},{13,9},{2,6},{6,2},{1... | collective-permute-start | bytes 43016 | tf_op jit(solution)/shard_map/ppermute | solution.py:55
  466.8 7.2 %collective-permute-start.36 = (f32[3584]{0:T(1024)S(1)}, f32[3584]{0:T(1024)S(1)}, u32[]{:S(2)}, u32[]{:S(2)}) collective-permute-start(f32[3584]{0:T(1024)S(1)} %add.598), channel_id=1, source_target_pairs={{0,8},{8,0},{4,12},{12,4},{1,9},{9,1},{5,13},{13,5},{2,10},{10,2},... | collective-permute-start | bytes 43016 | tf_op jit(solution)/shard_map/ppermute | solution.py:52
  473.9 39.8 %collective-permute-start.29 = (bf16[1024,1536]{1,0:T(8,128)(2,1)}, bf16[1024,1536]{1,0:T(8,128)(2,1)}, u32[]{:S(2)}, u32[]{:S(2)}) collective-permute-start(bf16[1024,1536]{1,0:T(8,128)(2,1)} %convolution_convert_fusion), channel_id=1, source_target_pairs={{0,4},{4,0},{8,12},{12,8},{1,5},{5,1},{9,13},{13,9},{2,6},{6,2},{1... | collective-permute-start | bytes 9437192 | tf_op jit(solution)/shard_map/ppermute | solution.py:55
  484.4 14.7 %collective-permute-start.45 = (bf16[128,2048]{1,0:T(8,128)(2,1)S(1)}, bf16[128,2048]{1,0:T(8,128)(2,1)S(1)}, u32[]{:S(2)}, u32[]{:S(2)}) collective-permute-start(bf16[128,2048]{1,0:T(8,128)(2,1)S(1)} %get-tuple-element.55), channel_id=1, source_target_pairs={{0,16},{16,0},{1,17},{17,1},{2,18},{18,2},{3,19},{19,3},{4,20},{20... | collective-permute-start | bytes 1572872 | tf_op jit(solution)/shard_map/ppermute | solution.py:49
  485.0 14.1 %collective-permute-start.43 = (bf16[128,2048]{1,0:T(8,128)(2,1)S(1)}, bf16[128,2048]{1,0:T(8,128)(2,1)S(1)}, u32[]{:S(2)}, u32[]{:S(2)}) collective-permute-start(bf16[128,2048]{1,0:T(8,128)(2,1)S(1)} %get-tuple-element.56), channel_id=1, source_target_pairs={{0,8},{8,0},{4,12},{12,4},{1,9},{9,1},{5,13},{13,5},{2,10},{10,2},... | collective-permute-start | bytes 1572872 | tf_op jit(solution)/shard_map/ppermute | solution.py:52
  497.2 14.9 %collective-permute-start.50 = (bf16[128,2048]{1,0:T(8,128)(2,1)S(1)}, bf16[128,2048]{1,0:T(8,128)(2,1)S(1)}, u32[]{:S(2)}, u32[]{:S(2)}) collective-permute-start(bf16[128,2048]{1,0:T(8,128)(2,1)S(1)} %get-tuple-element.51), channel_id=1, source_target_pairs={{0,16},{16,0},{1,17},{17,1},{2,18},{18,2},{3,19},{19,3},{4,20},{20... | collective-permute-start | bytes 1572872 | tf_op jit(solution)/shard_map/ppermute | solution.py:49
  498.6 14.8 %collective-permute-start.48 = (bf16[128,2048]{1,0:T(8,128)(2,1)S(1)}, bf16[128,2048]{1,0:T(8,128)(2,1)S(1)}, u32[]{:S(2)}, u32[]{:S(2)}) collective-permute-start(bf16[128,2048]{1,0:T(8,128)(2,1)S(1)} %get-tuple-element.52), channel_id=1, source_target_pairs={{0,8},{8,0},{4,12},{12,4},{1,9},{9,1},{5,13},{13,5},{2,10},{10,2},... | collective-permute-start | bytes 1572872 | tf_op jit(solution)/shard_map/ppermute | solution.py:52
  499.6 45.7 %collective-permute-start.46 = (bf16[256,2048]{1,0:T(8,128)(2,1)S(1)}, bf16[256,2048]{1,0:T(8,128)(2,1)}, u32[]{:S(2)}, u32[]{:S(2)}) collective-permute-start(bf16[256,2048]{1,0:T(8,128)(2,1)S(1)} %pad_maximum_fusion.10), channel_id=1, source_target_pairs={{0,8},{8,0},{4,12},{12,4},{1,9},{9,1},{5,13},{13,5},{2,10},{10,2},... | collective-permute-start | bytes 3145736 | tf_op jit(solution)/shard_map/ppermute | solution.py:52
  501.4 45.2 %collective-permute-start.44 = (bf16[256,2048]{1,0:T(8,128)(2,1)S(1)}, bf16[256,2048]{1,0:T(8,128)(2,1)}, u32[]{:S(2)}, u32[]{:S(2)}) collective-permute-start(bf16[256,2048]{1,0:T(8,128)(2,1)S(1)} %pad_maximum_fusion.9), channel_id=1, source_target_pairs={{0,16},{16,0},{1,17},{17,1},{2,18},{18,2},{3,19},{19,3},{4,20},{20... | collective-permute-start | bytes 3145736 | tf_op jit(solution)/shard_map/ppermute | solution.py:49
  523.1 18.8 %collective-permute-start.32 = (bf16[128,1536]{1,0:T(8,128)(2,1)S(1)}, bf16[128,1536]{1,0:T(8,128)(2,1)S(1)}, u32[]{:S(2)}, u32[]{:S(2)}) collective-permute-start(bf16[128,1536]{1,0:T(8,128)(2,1)S(1)} %get-tuple-element.61), channel_id=1, source_target_pairs={{0,16},{16,0},{1,17},{17,1},{2,18},{18,2},{3,19},{19,3},{4,20},{20... | collective-permute-start | bytes 1179656 | tf_op jit(solution)/shard_map/ppermute | solution.py:49
  523.9 20.4 %collective-permute-start.30 = (bf16[128,1536]{1,0:T(8,128)(2,1)S(1)}, bf16[128,1536]{1,0:T(8,128)(2,1)S(1)}, u32[]{:S(2)}, u32[]{:S(2)}) collective-permute-start(bf16[128,1536]{1,0:T(8,128)(2,1)S(1)} %get-tuple-element.62), channel_id=1, source_target_pairs={{0,8},{8,0},{4,12},{12,4},{1,9},{9,1},{5,13},{13,5},{2,10},{10,2},... | collective-permute-start | bytes 1179656 | tf_op jit(solution)/shard_map/ppermute | solution.py:52
  525.2 41.6 %collective-permute-start.51 = (bf16[256,2048]{1,0:T(8,128)(2,1)S(1)}, bf16[256,2048]{1,0:T(8,128)(2,1)S(1)}, u32[]{:S(2)}, u32[]{:S(2)}) collective-permute-start(bf16[256,2048]{1,0:T(8,128)(2,1)S(1)} %pad_maximum_fusion.12), channel_id=1, source_target_pairs={{0,8},{8,0},{4,12},{12,4},{1,9},{9,1},{5,13},{13,5},{2,10},{10,2},... | collective-permute-start | bytes 3145736 | tf_op jit(solution)/shard_map/ppermute | solution.py:52
  542.0 26.1 %collective-permute-start.49 = (bf16[256,2048]{1,0:T(8,128)(2,1)S(1)}, bf16[256,2048]{1,0:T(8,128)(2,1)S(1)}, u32[]{:S(2)}, u32[]{:S(2)}) collective-permute-start(bf16[256,2048]{1,0:T(8,128)(2,1)S(1)} %pad_maximum_fusion.11), channel_id=1, source_target_pairs={{0,16},{16,0},{1,17},{17,1},{2,18},{18,2},{3,19},{19,3},{4,20},{20... | collective-permute-start | bytes 3145736 | tf_op jit(solution)/shard_map/ppermute | solution.py:49
  544.6 37.7 %collective-permute-start.33 = (bf16[256,1536]{1,0:T(8,128)(2,1)S(1)}, bf16[256,1536]{1,0:T(8,128)(2,1)S(1)}, u32[]{:S(2)}, u32[]{:S(2)}) collective-permute-start(bf16[256,1536]{1,0:T(8,128)(2,1)S(1)} %pad_maximum_fusion.14), channel_id=1, source_target_pairs={{0,8},{8,0},{4,12},{12,4},{1,9},{9,1},{5,13},{13,5},{2,10},{10,2},... | collective-permute-start | bytes 2359304 | tf_op jit(solution)/shard_map/ppermute | solution.py:52
  545.2 37.9 %collective-permute-start.31 = (bf16[256,1536]{1,0:T(8,128)(2,1)S(1)}, bf16[256,1536]{1,0:T(8,128)(2,1)S(1)}, u32[]{:S(2)}, u32[]{:S(2)}) collective-permute-start(bf16[256,1536]{1,0:T(8,128)(2,1)S(1)} %pad_maximum_fusion.13), channel_id=1, source_target_pairs={{0,16},{16,0},{1,17},{17,1},{2,18},{18,2},{3,19},{19,3},{4,20},{20... | collective-permute-start | bytes 2359304 | tf_op jit(solution)/shard_map/ppermute | solution.py:49
  592.1 9.3 %collective-permute-start.24 = (f32[5,2048]{1,0:T(8,128)S(1)}, f32[5,2048]{1,0:T(8,128)S(1)}, u32[]{:S(2)}, u32[]{:S(2)}) collective-permute-start(f32[5,2048]{1,0:T(8,128)S(1)} %constant_dynamic-update-slice_fusion.69), channel_id=1, source_target_pairs={{0,4},{4,0},{8,12},{12,8},{1,5},{5,1},{9,13},{13,9},{2,6},{6,2},{1... | collective-permute-start | bytes 122888 | tf_op jit(solution)/shard_map/ppermute | solution.py:55
  (79 other events, 1108.7 us)
Sparse Core Ops, SparseCore 0:
  24.2 81.0 all-gather.2
  109.8 82.0 all-gather.4
  395.4 76.2 reduce-scatter.4
  473.9 77.2 reduce-scatter.2

commit v2 on v1

v2 whole, which is shorter than its diff:
```python
from functools import partial, reduce
import math

import jax
import jax.numpy as jnp
from jax import lax
from jax.experimental import pallas as pl
from jax.experimental.pallas import tpu as pltpu
from jax.sharding import PartitionSpec as P

ROT = 64
PROMPT = 2048
EPS = 1e-05
F32 = jnp.float32
BF16 = jnp.bfloat16
ROWS = 256
HEAD = 256
NN = (((1,), (0,)), ((), ()))
NT = (((1,), (1,)), ((), ()))
TN = (((0,), (0,)), ((), ()))


def mul(a, b, dims):
    return lax.dot_general(a, b, dims, preferred_element_type=F32)


def call(kernel, grid, in_specs, out_specs, out_shape, flops, moved, exps=0, scratch=(), mib=48, name=None):
    return pl.pallas_call(
        kernel,
        grid=grid,
        in_specs=in_specs,
        out_specs=out_specs,
        out_shape=out_shape,
        scratch_shapes=scratch,
        compiler_params=pltpu.CompilerParams(vmem_limit_bytes=mib * 2**20),
        cost_estimate=pl.CostEstimate(flops=flops, bytes_accessed=moved, transcendentals=exps),
        name=name,
    )


def shape(*dims, kind=BF16):
    return jax.ShapeDtypeStruct(dims, kind)


def wide(row):
    return jnp.broadcast_to(row[None], (8, row.shape[0]))


def after(value, *others):
    return lax.optimization_barrier((value, *others))[0]


def turn(v, table, sign):
    head = v[:, :128]
    other = pltpu.roll(head, 96, 1) * table[:, 128:256] + pltpu.roll(head, 32, 1) * table[:, 256:]
    return jnp.concatenate([head * table[:, :128] + sign * other, v[:, 128:]], 1)


def turn_table(where_at):
    half = ROT // 2
    frequency = jnp.exp(jnp.arange(half, dtype=F32) * (-2.0 * math.log(10000.0) / ROT))
    angles = where_at.astype(F32)[:, None] * frequency[None, :]
    c, s = jnp.cos(angles), jnp.sin(angles)
    rows = where_at.shape[0]
    one, none = jnp.ones((rows, 128 - ROT), F32), jnp.zeros((rows, 128 - half), F32)
    return jnp.concatenate([c, c, one, -s, none, none[:, :half], s, none[:, : 128 - ROT]], 1)


def reorder_kernel(places, x_ref, o_ref):
    size = x_ref.shape[1] // len(places)
    for i, place in enumerate(places):
        o_ref[:, i * size : (i + 1) * size] = x_ref[:, pl.ds(pl.multiple_of(place() * size, size), size)]


def reorder(x, places):
    rows, cols = x.shape
    block = pl.BlockSpec((rows, cols), lambda: (0, 0))
    return call(partial(reorder_kernel, places), (), [block], block, shape(rows, cols, kind=x.dtype), 0, 4 * rows * cols, name="reorder")(x)


def norm_kernel(x_ref, gain_ref, first_ref, second_ref, stat_ref):
    x = x_ref[...].astype(F32)
    mean = jnp.mean(x, -1, keepdims=True)
    center = x - mean
    scale = lax.rsqrt(jnp.mean(center * center, -1, keepdims=True) + EPS)
    unit = center * scale
    first_ref[...] = (unit * gain_ref[0:1] + gain_ref[1:2]).astype(BF16)
    second_ref[...] = (unit * gain_ref[2:3] + gain_ref[3:4]).astype(BF16)
    lane = lax.broadcasted_iota(jnp.int32, stat_ref.shape, 1)
    stat_ref[...] = jnp.where(lane == 0, mean, scale)


def norms(x, gains):
    rows, width = x.shape
    block = pl.BlockSpec((128, width), lambda i: (i, 0))
    return call(
        norm_kernel,
        (rows // 128,),
        [block, pl.BlockSpec((8, width), lambda i: (0, 0))],
        [block, block, pl.BlockSpec((128, 128), lambda i: (i, 0))],
        [shape(rows, width), shape(rows, width), shape(rows, 128, kind=F32)],
        10 * rows * width,
        6 * rows * width,
        name="norms",
    )(x, gains)


def project_kernel(n_ref, w_ref, b_ref, table_ref, q_ref, kv_ref):
    head = q_ref.shape[1]
    for i in range(n_ref.shape[0] // ROWS):
        at = pl.ds(i * ROWS, ROWS)
        out = mul(n_ref[at, :], w_ref[...], NN) + b_ref[:1]
        q_ref[at, :] = turn(out[:, :head], table_ref[at, :], 1.0).astype(BF16)
        kv_ref[at, :head] = turn(out[:, head : 2 * head], table_ref[at, :], 1.0).astype(BF16)
        kv_ref[at, head:] = out[:, 2 * head :].astype(BF16)


def project(n, w, bias, table, heads):
    rows, depth = n.shape
    width = w.shape[1] // heads
    head = width // 3
    return call(
        project_kernel,
        (heads,),
        [
            pl.BlockSpec((rows, depth), lambda h: (0, 0)),
            pl.BlockSpec((depth, width), lambda h: (0, h)),
            pl.BlockSpec((8, width), lambda h: (0, h)),
            pl.BlockSpec((rows, 384), lambda h: (0, 0)),
        ],
        [pl.BlockSpec((rows, head), lambda h: (0, h)), pl.BlockSpec((rows, 2 * head), lambda h: (0, h))],
        [shape(rows, heads * head), shape(rows, heads * 2 * head)],
        2 * rows * depth * w.shape[1],
        2 * (rows * depth + w.size + rows * w.shape[1]),
        name="project",
    )(n, w, wide(bias), table)


def expand_kernel(n_ref, w_ref, b_ref, h_ref, d_ref):
    for i in range(n_ref.shape[0] // ROWS):
        at = pl.ds(i * ROWS, ROWS)
        pre = mul(n_ref[at, :], w_ref[...], NN) + b_ref[:1]
        below = 0.5 + 0.5 * lax.erf(pre * math.sqrt(0.5))
        h_ref[at, :] = (pre * below).astype(BF16)
        d_ref[at, :] = (below + pre * jnp.exp(-0.5 * pre * pre) * (1.0 / math.sqrt(2 * math.pi))).astype(BF16)


def expand(n, w, bias, tile=512):
    rows, depth = n.shape
    cols = w.shape[1]
    out = pl.BlockSpec((rows, tile), lambda j: (0, j))
    return call(
        expand_kernel,
        (cols // tile,),
        [
            pl.BlockSpec((rows, depth), lambda j: (0, 0)),
            pl.BlockSpec((depth, tile), lambda j: (0, j)),
            pl.BlockSpec((8, tile), lambda j: (0, j)),
        ],
        [out, out],
        [shape(rows, cols), shape(rows, cols)],
        2 * rows * depth * cols,
        2 * (rows * depth + w.size + 2 * rows * cols),
        2 * rows * cols,
        name="expand",
    )(n, w, wide(bias))


def attend_kernel(prompt, q_ref, ko, vo, kt, vt, bias_ref, segc_ref, segr_ref, o_ref, stat_ref):
    block = pl.program_id(1)
    tq = q_ref.shape[0]
    first_cont = prompt // tq
    cont = ko.shape[0] - prompt
    q = q_ref[...] * BF16(1.0 / math.sqrt(q_ref.shape[1]))
    rows = lax.broadcasted_iota(jnp.int32, (tq, 1), 0)

    def finish(scores, values):
        top = reduce(jnp.maximum, [jnp.max(s, -1, keepdims=True) for s in scores])
        exps = [jnp.exp(s - top) for s in scores]
        total = sum(jnp.sum(e, -1, keepdims=True) for e in exps)
        out = sum(mul(e.astype(BF16), v, NN) for e, v in zip(exps, values))
        o_ref[...] = (out / total).astype(BF16)
        stat_ref[0] = jnp.transpose(jnp.broadcast_to(top + jnp.log(total), (tq, 128)))[:8]

    @pl.when(block < first_cont)
    def _():
        cols = lax.broadcasted_iota(jnp.int32, (1, prompt), 1)
        own = jnp.where(cols <= rows + block * tq, mul(q, ko[:prompt], NT), -1e30)
        far = mul(q, kt[...], NT) + bias_ref[:1]
        finish([own, far], [vo[:prompt], vt[...]])

    @pl.when(block >= first_cont)
    def _():
        cols = lax.broadcasted_iota(jnp.int32, (1, cont), 1)
        own = mul(q, ko[:prompt], NT)
        read = (cols <= rows + (block - first_cont) * tq) & (segc_ref[:, :1] == segr_ref[:1])
        follow = jnp.where(read, mul(q, ko[prompt:], NT), -1e30)
        far = mul(q, kt[...], NT)
        finish([own, follow, far], [vo[:prompt], vo[prompt:], vt[...]])


def attend(q, kv, kv_far, bias, seg, prompt):
    rows, width = q.shape
    head = HEAD
    heads = width // head
    far = kv_far.shape[0]
    cont = rows - prompt
    tq = ROWS
    first = prompt // tq
    return call(
        partial(attend_kernel, prompt),
        (heads, rows // tq),
        [
            pl.BlockSpec((tq, head), lambda h, b: (b, h)),
            pl.BlockSpec((rows, head), lambda h, b: (0, 2 * h)),
            pl.BlockSpec((rows, head), lambda h, b: (0, 2 * h + 1)),
            pl.BlockSpec((far, head), lambda h, b: (0, 2 * h)),
            pl.BlockSpec((far, head), lambda h, b: (0, 2 * h + 1)),
            pl.BlockSpec((8, far), lambda h, b: (0, 0)),
            pl.BlockSpec((tq, 128), lambda h, b: (jnp.maximum(b - first, 0), 0)),
            pl.BlockSpec((8, cont), lambda h, b: (0, 0)),
        ],
        [pl.BlockSpec((tq, head), lambda h, b: (b, h)), pl.BlockSpec((1, 8, tq), lambda h, b: (h, 0, b))],
        [shape(rows, width), shape(heads, 8, rows, kind=F32)],
        4 * rows * (rows + far) * width,
        2 * (2 * q.size + kv.size + kv_far.size),
        rows * (rows + far) * heads,
        name="attend",
    )(q, kv, kv, kv_far, kv_far, wide(bias), jnp.broadcast_to(seg[prompt:, None], (cont, 128)), wide(seg[prompt:]))


def attend_back_kernel(
    prompt, q_ref, do_ref, o_ref, stat_ref, ko, vo, kt, vt, bias_ref, segc_ref, segr_ref, table_ref,
    dq_ref, own_ref, near_ref, far_ref, acc_k, acc_v,
):
    block = pl.program_id(1)
    tq, head = q_ref.shape
    first_cont = prompt // tq
    scale = 1.0 / math.sqrt(head)
    q = q_ref[...] * BF16(scale)
    do = do_ref[...]
    inner = jnp.sum(do.astype(F32) * o_ref[...].astype(F32), -1, keepdims=True)
    inner = jnp.transpose(jnp.broadcast_to(inner, (tq, 128)))[:1]
    stat = stat_ref[0, :1]
    cols = lax.broadcasted_iota(jnp.int32, (1, tq), 1)

    @pl.when(block == 0)
    def _():
        acc_k[...] = jnp.zeros_like(acc_k)
        acc_v[...] = jnp.zeros_like(acc_v)

    def part(keys, values, at, seen):
        probs = jnp.exp(seen(mul(keys, q, NT)) - stat)
        grads = (probs * (mul(values, do, NT) - inner)).astype(BF16)
        acc_v[at, :] += mul(probs.astype(BF16), do, NN)
        acc_k[at, :] += mul(grads, q, NN)
        return mul(grads, keys, TN)

    def far_parts(total, seen):
        for i in range(kt.shape[0] // prompt):
            at = pl.ds(i * prompt, prompt)
            total += part(kt[at, :], vt[at, :], pl.ds(ko.shape[0] + i * prompt, prompt), partial(seen, at))
        dq_ref[...] = turn(total * scale, table_ref[...], -1.0).astype(BF16)

    @pl.when(block < first_cont)
    def _():
        rows = lax.broadcasted_iota(jnp.int32, (prompt, 1), 0)
        total = part(
            ko[:prompt], vo[:prompt], pl.ds(0, prompt), lambda s: jnp.where(rows <= cols + block * tq, s, -1e30)
        )
        far_parts(total, lambda at, s: s + bias_ref[at, :1])

    @pl.when(block >= first_cont)
    def _():
        cont = ko.shape[0] - prompt
        rows = lax.broadcasted_iota(jnp.int32, (cont, 1), 0)
        total = part(ko[:prompt], vo[:prompt], pl.ds(0, prompt), lambda s: s)
        read = (rows <= cols + (block - first_cont) * tq) & (segc_ref[:, :1] == segr_ref[:1])
        total += part(ko[prompt:], vo[prompt:], pl.ds(prompt, cont), lambda s: jnp.where(read, s, -1e30))
        far_parts(total, lambda at, s: s)

    @pl.when(block == pl.num_programs(1) - 1)
    def _():
        start = 0
        for ref in (own_ref, near_ref, far_ref):
            at = pl.ds(start, ref.shape[0])
            ref[:, :head] = acc_k[at, :].astype(ref.dtype)
            ref[:, head:] = acc_v[at, :].astype(ref.dtype)
            start += ref.shape[0]


def attend_back(q, do, o, stat, kv, kv_far, bias, seg, prompt, table):
    rows, width = q.shape
    head = HEAD
    heads = width // head
    far = kv_far.shape[0]
    cont = rows - prompt
    tq = ROWS
    first = prompt // tq
    row = pl.BlockSpec((tq, head), lambda h, b: (b, h))

    def column(n, odd):
        return pl.BlockSpec((n, head), lambda h, b: (0, 2 * h + odd))

    def pair(n):
        return pl.BlockSpec((n, 2 * head), lambda h, b: (0, h))

    return call(
        partial(attend_back_kernel, prompt),
        (heads, rows // tq),
        [
            row,
            row,
            row,
            pl.BlockSpec((1, 8, tq), lambda h, b: (h, 0, b)),
            column(rows, 0),
            column(rows, 1),
            column(far, 0),
            column(far, 1),
            pl.BlockSpec((far, 128), lambda h, b: (0, 0)),
            pl.BlockSpec((cont, 128), lambda h, b: (0, 0)),
            pl.BlockSpec((8, tq), lambda h, b: (0, jnp.maximum(b - first, 0))),
            pl.BlockSpec((tq, 384), lambda h, b: (b, 0)),
        ],
        [row, pair(rows), pair(prompt), pair(far - prompt)],
        [
            shape(rows, width),
            shape(rows, 2 * width, kind=F32),
            shape(prompt, 2 * width),
            shape(far - prompt, 2 * width),
        ],
        10 * rows * (rows + far) * width,
        2 * (4 * q.size + 4 * kv.size + 2 * kv_far.size),
        rows * (rows + far) * heads,
        [pltpu.VMEM((rows + far, head), F32), pltpu.VMEM((rows + far, head), F32)],
        name="attend_back",
    )(
        q,
        do,
        o,
        stat,
        kv,
        kv,
        kv_far,
        kv_far,
        jnp.broadcast_to(bias[:, None], (far, 128)),
        jnp.broadcast_to(seg[prompt:, None], (cont, 128)),
        wide(seg[prompt:]),
        table,
    )


def mixed_kernel(a_ref, h_ref, wa_ref, wh_ref, o_ref):
    for i in range(a_ref.shape[0] // ROWS):
        at = pl.ds(i * ROWS, ROWS)
        o_ref[at, :] = (mul(a_ref[at, :], wa_ref[...], NT) + mul(h_ref[at, :], wh_ref[...], NT)).astype(BF16)


def mixed_sum(attended, activated, w_out, w_contract, tile=512):
    rows = attended.shape[0]
    deep, deeper = attended.shape[1], activated.shape[1]
    width = w_out.shape[0]
    return call(
        mixed_kernel,
        (width // tile,),
        [
            pl.BlockSpec((rows, deep), lambda j: (0, 0)),
            pl.BlockSpec((rows, deeper), lambda j: (0, 0)),
            pl.BlockSpec((tile, deep), lambda j: (j, 0)),
            pl.BlockSpec((tile, deeper), lambda j: (j, 0)),
        ],
        pl.BlockSpec((rows, tile), lambda j: (0, j)),
        shape(rows, width),
        2 * rows * width * (deep + deeper),
        2 * (rows + width) * (deep + deeper) + 2 * rows * width,
        name="mixed_sum",
    )(attended, activated, w_out, w_contract)


def grads_kernel(g_ref, wo_ref, wc_ref, d_ref, do_ref, gp_ref, sum_ref):
    @pl.when(pl.program_id(0) == 0)
    def _():
        for i in range(g_ref.shape[0] // ROWS):
            at = pl.ds(i * ROWS, ROWS)
            do_ref[at, :] = mul(g_ref[at, :], wo_ref[...], NN).astype(BF16)

    total = 0.0
    for i in range(g_ref.shape[0] // ROWS):
        at = pl.ds(i * ROWS, ROWS)
        grad = (mul(g_ref[at, :], wc_ref[...], NN) * d_ref[at, :].astype(F32)).astype(BF16)
        gp_ref[at, :] = grad
        total += jnp.sum(grad.astype(F32), 0, keepdims=True)
    sum_ref[...] = jnp.broadcast_to(total, sum_ref.shape)


def branch_grads(g, w_out, w_contract, slope, tile=512):
    rows, depth = g.shape
    deep, cols = w_out.shape[1], w_contract.shape[1]
    tall = pl.BlockSpec((rows, tile), lambda j: (0, j))
    return call(
        grads_kernel,
        (cols // tile,),
        [
            pl.BlockSpec((rows, depth), lambda j: (0, 0)),
            pl.BlockSpec((depth, deep), lambda j: (0, 0)),
            pl.BlockSpec((depth, tile), lambda j: (0, j)),
            tall,
        ],
        [pl.BlockSpec((rows, deep), lambda j: (0, 0)), tall, pl.BlockSpec((8, tile), lambda j: (0, j))],
        [shape(rows, deep), shape(rows, cols), shape(8, cols, kind=F32)],
        2 * rows * depth * (deep + cols),
        2 * (rows * depth + depth * (deep + cols) + 2 * rows * cols),
        name="branch_grads",
    )(g, w_out, w_contract, slope)


def pack_kernel(prompt_blocks, q_ref, own_ref, near_ref, far_ref, table_ref, o_ref, sum_ref):
    block = pl.program_id(1)
    head = q_ref.shape[1]
    theirs = near_ref[...].astype(F32) + far_ref[...].astype(F32)
    both = own_ref[...] + jnp.where(block < prompt_blocks, theirs, 0.0)
    out = [q_ref[...], turn(both[:, :head], table_ref[...], -1.0).astype(BF16), both[:, head:].astype(BF16)]

    @pl.when(block == 0)
    def _():
        sum_ref[...] = jnp.zeros_like(sum_ref)

    for i, part in enumerate(out):
        o_ref[:, i * head : (i + 1) * head] = part
        sum_ref[:, i * head : (i + 1) * head] += jnp.sum(part.astype(F32), 0, keepdims=True)


def pack(dq, own, near, far, table, prompt):
    rows, width = dq.shape
    head = HEAD
    heads = width // head
    tq = ROWS
    blocks = prompt // tq
    theirs = pl.BlockSpec((tq, 2 * head), lambda h, b: (jnp.minimum(b, blocks - 1), h))
    return call(
        partial(pack_kernel, blocks),
        (heads, rows // tq),
        [
            pl.BlockSpec((tq, head), lambda h, b: (b, h)),
            pl.BlockSpec((tq, 2 * head), lambda h, b: (b, h)),
            theirs,
            theirs,
            pl.BlockSpec((tq, 384), lambda h, b: (b, 0)),
        ],
        [pl.BlockSpec((tq, 3 * head), lambda h, b: (b, h)), pl.BlockSpec((8, 3 * head), lambda h, b: (0, h))],
        [shape(rows, 3 * width), shape(8, 3 * width, kind=F32)],
        10 * rows * width,
        16 * rows * width,
        name="pack",
    )(dq, own, near, far, table)


def unit_grad_kernel(gp_ref, gh_ref, wa_ref, we_ref, x_ref, stat_ref, gain_ref, e_ref, sum_ref):
    sums = [0.0] * 4
    for i in range(gp_ref.shape[0] // ROWS):
        at = pl.ds(i * ROWS, ROWS)
        first = mul(gp_ref[at, :], wa_ref[...], NT)
        second = mul(gh_ref[at, :], we_ref[...], NT)
        e_ref[at, :] = (first * gain_ref[0:1] + second * gain_ref[2:3]).astype(BF16)
        unit = (x_ref[at, :].astype(F32) - stat_ref[at, 0:1]) * stat_ref[at, 1:2]
        for j, v in enumerate((first * unit, first, second * unit, second)):
            sums[j] += jnp.sum(v, 0, keepdims=True)
    for j in range(4):
        sum_ref[j : j + 1] = sums[j]
    sum_ref[4:] = jnp.zeros_like(sum_ref[4:])


def unit_grads(gp, gh, w_attend, w_expand, x, stat, gains, tile=512):
    rows, width = x.shape
    deep, deeper = gp.shape[1], gh.shape[1]
    col = pl.BlockSpec((rows, tile), lambda j: (0, j))
    row = pl.BlockSpec((8, tile), lambda j: (0, j))
    return call(
        unit_grad_kernel,
        (width // tile,),
        [
            pl.BlockSpec((rows, deep), lambda j: (0, 0)),
            pl.BlockSpec((rows, deeper), lambda j: (0, 0)),
            pl.BlockSpec((tile, deep), lambda j: (j, 0)),
            pl.BlockSpec((tile, deeper), lambda j: (j, 0)),
            col,
            pl.BlockSpec((rows, 128), lambda j: (0, 0)),
            row,
        ],
        [col, row],
        [shape(rows, width), shape(8, width, kind=F32)],
        2 * rows * width * (deep + deeper),
        2 * (rows + width) * (deep + deeper) + 4 * rows * width,
        name="unit_grads",
    )(gp, gh, w_attend, w_expand, x, stat, gains)


def far_kernel(a_ref, b_ref, o_ref):
    for i in range(o_ref.shape[0] // ROWS):
        o_ref[pl.ds(i * ROWS, ROWS), :] = mul(a_ref[:, pl.ds(i * ROWS, ROWS)], b_ref[...], TN).astype(BF16)


def far_product(a, b, tile=512):
    tokens, width = a.shape
    half = width // 2
    cols = b.shape[1]
    return call(
        far_kernel,
        (cols // tile,),
        [pl.BlockSpec((tokens, half), lambda j: (0, 1)), pl.BlockSpec((tokens, tile), lambda j: (0, j))],
        pl.BlockSpec((half, tile), lambda j: (0, j)),
        shape(half, cols),
        2 * tokens * half * cols,
        2 * (tokens * half + tokens * cols + half * cols),
        name="far_product",
    )(a, b)


def near_kernel(a_ref, b_ref, r_ref, *outs):
    size = a_ref.shape[1] // len(outs)
    for i, out in enumerate(outs):
        at = pl.ds(i * size, size)
        out[...] = (mul(a_ref[:, at], b_ref[...], TN) + r_ref[at, :].astype(F32)).astype(out.dtype)


def near_product(a, b, received, tile=512):
    tokens, width = a.shape
    half = width // 2
    cols = b.shape[1]
    size = half // 4
    out = pl.BlockSpec((size, tile), lambda j: (0, j))
    return call(
        near_kernel,
        (cols // tile,),
        [
            pl.BlockSpec((tokens, half), lambda j: (0, 0)),
            pl.BlockSpec((tokens, tile), lambda j: (0, j)),
            pl.BlockSpec((half, tile), lambda j: (0, j)),
        ],
        [out] * 4,
        [shape(size, cols, kind=F32)] + [shape(size, cols)] * 3,
        2 * tokens * half * cols,
        2 * (tokens * half + tokens * cols + 2 * half * cols),
        name="near_product",
    )(a, b, received)


class SquareLinks:
    order = ((0, 0, 0), (1, 0, 0), (0, 1, 0), (1, 1, 0), (0, 0, 1), (1, 0, 1), (0, 1, 1), (1, 1, 1))

    def x_hop(self, v):
        return lax.ppermute(v, "fsdp", [(0, 1), (1, 0)])

    def y_hop(self, v):
        return lax.ppermute(v, "ctx", [(0, 2), (2, 0), (1, 3), (3, 1)])

    def core_hop(self, v):
        return lax.ppermute(v, "ctx", [(0, 1), (1, 0), (2, 3), (3, 2)])

    def place(self, bits):
        f, c = lax.axis_index("fsdp"), lax.axis_index("ctx")
        a, b, d = bits
        return ((f ^ a) * 2 + ((c // 2) ^ b)) * 2 + ((c % 2) ^ d)

    def spot(self, p):
        f, c = lax.axis_index("fsdp"), lax.axis_index("ctx")
        a, b, d = f ^ (p // 4), (c // 2) ^ (p // 2 % 2), (c % 2) ^ (p % 2)
        return d * 4 + b * 2 + a

    def to_relative(self, v):
        return reorder(v, [partial(self.place, bits) for bits in self.order])

    def to_whole(self, v):
        return reorder(v, [partial(self.spot, p) for p in range(8)])

    def gather(self, block):
        rows = block.shape[0]
        half = rows // 2
        from_x, from_y = self.x_hop(block), self.y_hop(block)
        corner = (self.x_hop(from_y[:half]), self.y_hop(from_x[half:]))
        near = jnp.concatenate([block, from_x, from_y, *corner], 0)
        return jnp.concatenate([near, self.core_hop(near)], 0)

    def scatter_far(self, left, right):
        return self.core_hop(far_product(left, right))

    def scatter_near(self, left, right, far):
        return near_product(left, right, far)

    def scatter_end(self, own, to_x, to_y, corner):
        half = corner.shape[0] // 2
        via_x, via_y = self.x_hop(corner[:half]), self.y_hop(corner[half:])
        to_y = jnp.concatenate([to_y[:half] + via_x, to_y[half:]], 0)
        to_x = jnp.concatenate([to_x[:half], to_x[half:] + via_y], 0)
        return own + self.x_hop(to_x).astype(F32) + self.y_hop(to_y).astype(F32)

    def others(self, v):
        c = lax.axis_index("ctx")
        return jnp.stack([v[c ^ bits] for bits in (2, 1, 3)])

    def gather_others(self, block):
        from_y = self.y_hop(block)
        return jnp.concatenate([from_y, self.core_hop(jnp.concatenate([block, from_y], 0))], 0)

    def scatter_others(self, near, far):
        theirs = self.core_hop(far)
        rows = near.shape[0]
        return theirs, lambda token: self.y_hop(after(theirs[rows:], token) + near)

    def sum_rows(self, v):
        v = v + self.core_hop(v)
        v = v + self.x_hop(v)
        return v + self.y_hop(v)


class AnyLinks:
    def to_relative(self, v):
        return v

    def to_whole(self, v):
        return v

    def gather(self, block):
        return lax.all_gather(block, ("fsdp", "ctx"), axis=0, tiled=True)

    def scatter_far(self, left, right):
        return None

    def scatter_near(self, left, right, far):
        return (jnp.einsum("tc,tk->ck", left, right, preferred_element_type=F32).astype(BF16),)

    def scatter_end(self, whole):
        return lax.psum_scatter(whole, ("fsdp", "ctx"), scatter_dimension=0, tiled=True).astype(F32)

    def others(self, v):
        return jnp.roll(v, -lax.axis_index("ctx"), 0)[1:]

    def gather_others(self, block):
        rows = block.shape[0]
        whole = lax.all_gather(block, "ctx", axis=0, tiled=True)
        return jnp.roll(whole, -rows * lax.axis_index("ctx"), 0)[rows:]

    def scatter_others(self, near, far):
        rows = near.shape[0]
        whole = jnp.concatenate([jnp.zeros_like(near), near, far], 0)
        whole = jnp.roll(whole, rows * lax.axis_index("ctx"), 0)
        theirs = lax.psum_scatter(whole, "ctx", scatter_dimension=0, tiled=True)
        return theirs, lambda token: jnp.zeros_like(theirs)

    def sum_rows(self, v):
        return lax.psum(v, ("fsdp", "ctx"))


def sum_tp(v):
    size = lax.axis_size("tp")
    if size & (size - 1):
        return lax.psum(v, "tp")
    step = 1
    while step < size:
        v = v + lax.ppermute(v, "tp", [(i, i ^ step) for i in range(size)])
        step *= 2
    return v


def end_kernel(x_ref, g_ref, e_ref, o_ref):
    x = x_ref[...].astype(F32)
    center = x - jnp.mean(x, -1, keepdims=True)
    scale = lax.rsqrt(jnp.mean(center * center, -1, keepdims=True) + EPS)
    unit = center * scale
    e = e_ref[...].astype(F32)
    rest = e - jnp.mean(e, -1, keepdims=True) - unit * jnp.mean(e * unit, -1, keepdims=True)
    o_ref[...] = g_ref[...].astype(F32) + scale * rest


def input_grads(x, g, e):
    rows, width = x.shape
    block = pl.BlockSpec((64, width), lambda i: (i, 0))
    return call(
        end_kernel, (rows // 64,), [block] * 3, block, shape(rows, width, kind=F32), 15 * x.size, 10 * x.size, name="input_grads"
    )(x, g, e)


def shards(
    stream_in,
    stream_grad,
    segments,
    positions,
    first_gain,
    first_shift,
    second_gain,
    second_shift,
    attend_weight,
    attend_bias,
    output_weight,
    expand_weight,
    expand_bias,
    contract_weight,
    output_bias,
):
    square = lax.axis_size("fsdp") == 2 and lax.axis_size("ctx") == 4
    links = SquareLinks() if square else AnyLinks()
    local_rows = attend_weight.shape[0]
    heads = attend_bias.shape[0]
    holders = lax.axis_size("ctx")
    holder = lax.axis_index("ctx")
    prompt = PROMPT // holders

    in_part = links.to_relative(stream_in)
    rows_in = lax.all_gather(in_part, "tp", axis=0, tiled=True)
    grad_part = links.to_relative(stream_grad)
    grad_late, rows_in = lax.optimization_barrier((grad_part, rows_in))
    rows_grad = lax.all_gather(grad_late, "tp", axis=0, tiled=True)
    row_count = rows_in.shape[0]

    attend_all = links.gather(attend_weight.reshape(local_rows, -1))
    expand_all = links.gather(expand_weight)
    contract_all = links.gather(contract_weight)
    output_all = links.gather(output_weight)

    gains = jnp.concatenate([jnp.stack([first_gain, first_shift, second_gain, second_shift]), jnp.zeros((4, first_gain.shape[0]), F32)])
    gains = links.to_relative(gains)
    row_pos = lax.dynamic_slice_in_dim(positions, holder * row_count, row_count)
    row_seg = lax.dynamic_slice_in_dim(segments, holder * row_count, row_count)
    starts = positions.reshape(holders, row_count)[:, 0]
    bias = jnp.where(links.others(starts) < row_pos[0], 0.0, -1e30).astype(F32)
    bias = jnp.repeat(bias, prompt)
    table = turn_table(row_pos)

    first_norm, second_norm, stat = norms(rows_in, gains)
    queries, pairs = project(first_norm, attend_all, attend_bias.reshape(-1), table, heads)
    pairs_far = links.gather_others(pairs[:prompt])
    activated, slope = expand(after(second_norm, pairs), expand_all, expand_bias)
    attended, row_sums = attend(after(queries, activated), pairs, pairs_far, bias, row_seg, prompt)
    mixed = mixed_sum(attended, activated, output_all, contract_all)
    branches = lax.psum_scatter(mixed, "tp", scatter_dimension=0, tiled=True)

    rows_grad = after(rows_grad, mixed)
    grad_attended, grad_pre, expand_sums = branch_grads(rows_grad, output_all, contract_all, slope)
    grad_queries, pair_own, pair_near, pair_far = attend_back(
        queries, grad_attended, attended, row_sums, pairs, pairs_far, bias, row_seg, prompt, table
    )
    core_part, y_part = links.scatter_others(pair_near, pair_far)
    far_c = links.scatter_far(rows_grad, after(activated, pair_own))
    y_part = y_part(pair_own)
    near_c = links.scatter_near(rows_grad, activated, far_c)
    far_e = links.scatter_far(second_norm, after(grad_pre, near_c[0]))
    grad_flat, attend_sums = pack(grad_queries, after(pair_own, near_c[0]), y_part, core_part, table, prompt)
    grad_unit, vector_parts = unit_grads(grad_flat, grad_pre, attend_all, expand_all, rows_in, stat, gains)
    unit_part = lax.psum_scatter(grad_unit, "tp", scatter_dimension=0, tiled=True)

    near_e = links.scatter_near(after(second_norm, grad_unit), grad_pre, far_e)
    far_a = links.scatter_far(first_norm, after(grad_flat, near_e[0]))
    far_o = links.scatter_far(rows_grad, after(attended, near_e[0]))
    near_a = links.scatter_near(first_norm, grad_flat, far_a)
    near_o = links.scatter_near(rows_grad, after(attended, near_a[0]), far_o)
    contract_weight_grad = links.scatter_end(*near_c)
    expand_weight_grad = links.scatter_end(*near_e)
    attend_weight_grad = links.scatter_end(*near_a).reshape(attend_weight.shape)
    output_weight_grad = links.scatter_end(*near_o)

    bias_sums = links.sum_rows(jnp.concatenate([attend_sums[0], expand_sums[0]]))
    attend_bias_grad = bias_sums[: grad_flat.shape[1]].reshape(attend_bias.shape)
    expand_bias_grad = bias_sums[grad_flat.shape[1] :]
    row_sum = jnp.sum(grad_part.astype(F32), 0)
    vectors = jnp.concatenate([vector_parts[:4], row_sum[None], jnp.zeros((3, row_sum.shape[0]), F32)])
    norm_sums = sum_tp(links.sum_rows(links.to_whole(vectors)))

    stream_out = links.to_whole((in_part.astype(F32) + branches.astype(F32))) + output_bias
    stream_out = stream_out.astype(BF16)
    input_grad = links.to_whole(input_grads(in_part, grad_part, unit_part))
    return (
        stream_out,
        input_grad,
        norm_sums[0],
        norm_sums[1],
        norm_sums[2],
        norm_sums[3],
        attend_weight_grad,
        attend_bias_grad,
        output_weight_grad,
        expand_weight_grad,
        expand_bias_grad,
        contract_weight_grad,
        norm_sums[4],
    )


def solution(mesh):
    tokens = P(("fsdp", "ctx", "tp"), None)
    weight = P(("fsdp", "ctx"), "tp")
    heads = P(("fsdp", "ctx"), "tp", None)
    return jax.shard_map(
        shards,
        mesh=mesh,
        in_specs=(
            tokens,
            tokens,
            P("fsdp"),
            P("fsdp"),
            P(),
            P(),
            P(),
            P(),
            heads,
            P("tp", None),
            weight,
            weight,
            P("tp"),
            weight,
            P(),
        ),
        out_specs=(
            tokens,
            tokens,
            P(),
            P(),
            P(),
            P(),
            heads,
            P("tp", None),
            weight,
            weight,
            P("tp"),
            weight,
            P(),
        ),
        check_vma=False,
    )
```

time: 636 us -> 523 us (0.82)
  matrix products: 230 us -> 0 us
  Pallas kernels: 0 us -> 197 us
  other arithmetic: 68.8 us -> 24.4 us
  local copies, waits for them, and re-layouts: 99.9 us -> 74.7 us
    dot_general x21 -> x0, matrix products: 216 us -> none  [the longest x4 61.2 us: dot(): return jnp.dot(left, right, preferred_element_type=F32)]
    pallas_call x0 -> x24, Pallas kernels: none -> 197 us  [the longest x4 26.4 us: far_product(): call(far_kernel, (cols // tile,), [pl.BlockSpec((tokens, half), lambda j:...]
    convert_element_type x4 -> x1, other arithmetic: 26.8 us -> 0.01 us  [turn_table(): angles = where_at.astype(F32)[:, None] * frequency[None, :]]
    ppermute x18, waiting for transfers between devices: 71.4 us -> 47.2 us  [x_hop(): return lax.ppermute(v, 'fsdp', [(0, 1), (1, 0)])]
    unnamed x206 -> x100, local copies, waits for them, and re-layouts: 58.1 us -> 37.6 us
    ppermute x20, waiting for transfers between devices: 81.5 us -> 98.4 us  [y_hop(): return lax.ppermute(v, 'ctx', [(0, 2), (2, 0), (1, 3), (3, 1)])]
    sub x1 -> x0, matrix products: 13.6 us -> none  [attention_probs(): exponent = jnp.exp(scores - row_top)]
    reduce_sum x7 -> x1, other arithmetic: 11.9 us -> 1.39 us  [shards(): row_sum = jnp.sum(grad_part.astype(F32), 0)]
  transfers between devices with their start and end apart: 56 -> 56, of which waited for: 21 -> 24; matrix products, arithmetic and copies ran while one was open for 54% -> 15% of each run, Pallas kernels for 0% -> 38%
where the time goes in v2:
time: 523 us; the launch traced here: 517 us
  Pallas kernels  197 us (38%)
  waiting for transfers between devices  157 us (30%)
  local copies, waits for them, and re-layouts  74.7 us (14%)
  starting transfers between devices  48.8 us (9%)
  other arithmetic  24.4 us (5%)
  between operations  14.8 us (3%)
    ppermute x20, waiting for transfers between devices, y_hop(): return lax.ppermute(v, 'ctx', [(0, 2), (2, 0), (1, 3), (3, 1)])  98.4 us
    ppermute x18, waiting for transfers between devices, x_hop(): return lax.ppermute(v, 'fsdp', [(0, 1), (1, 0)])  47.2 us
    unnamed x100, local copies, waits for them, and re-layouts  37.6 us
    pallas_call x4, Pallas kernels, far_product(): call(far_kernel, (cols // tile,), [pl.BlockSpec((tokens, half), lambda j:...  26.4 us
    pallas_call x4, Pallas kernels, near_product(): call(near_kernel, (cols // tile,), [pl.BlockSpec((tokens, half), lambda j...  25.9 us
    ppermute x20, starting transfers between devices, y_hop(): return lax.ppermute(v, 'ctx', [(0, 2), (2, 0), (1, 3), (3, 1)])  24 us
    pallas_call x1, Pallas kernels, attend_back(): call(partial(attend_back_kernel, prompt), (heads, rows // tq), [row, row,...  23 us
    pallas_call x1, Pallas kernels, unit_grads(): call(unit_grad_kernel, (width // tile,), [pl.BlockSpec((rows, deep), lamb...  22.2 us
  transfers between devices with their start and end apart: 56, of which 24 were waited for; matrix products, arithmetic and copies ran while one was open for 15% of the time, Pallas kernels for 38%

profile of v2, /device:TPU:0, one launch (start us, length us, event | category | flops | bytes accessed | tf_op | source)
XLA Modules:
  0.0 516.5 jit_solution(17915710154293953418)
XLA Ops:
  10.9 3.0 collective-permute-start.1
  18.9 13.3 %collective-permute-done.1 = bf16[256,1536]{1,0:T(8,128)(2,1)S(1)} collective-permute-done((bf16[256,1536]{1,0:T(8,128)(2,1)S(1)}, bf16[256,1536]{1,0:T(8,128)(2,1)S(1)}, u32[]{:S(2)}, u32[]{:S(2)}) %collective-permute-start.1) | collective-permute-done | bytes 786464 | tf_op jit(solution)/shard_map/ppermute | solution.py:555
  32.2 2.1 collective-permute-start.18
  39.2 15.5 %collective-permute-done.6 = bf16[256,2048]{1,0:T(8,128)(2,1)S(1)} collective-permute-done((bf16[256,2048]{1,0:T(8,128)(2,1)S(1)}, bf16[256,2048]{1,0:T(8,128)(2,1)S(1)}, u32[]{:S(2)}, u32[]{:S(2)}) %collective-permute-start.6) | collective-permute-done | bytes 1048608 | tf_op jit(solution)/shard_map/ppermute | solution.py:555
  59.4 17.7 %collective-permute-done.18 = bf16[256,2048]{1,0:T(8,128)(2,1)S(1)} collective-permute-done((bf16[256,2048]{1,0:T(8,128)(2,1)S(1)}, bf16[256,2048]{1,0:T(8,128)(2,1)S(1)}, u32[]{:S(2)}, u32[]{:S(2)}) %collective-permute-start.18) | collective-permute-done | bytes 1048608 | tf_op jit(solution)/shard_map/ppermute | solution.py:555
  80.9 6.8 %collective-permute-done.2 = bf16[128,1536]{1,0:T(8,128)(2,1)S(1)} collective-permute-done((bf16[128,1536]{1,0:T(8,128)(2,1)S(1)}, bf16[128,1536]{1,0:T(8,128)(2,1)S(1)}, u32[]{:S(2)}, u32[]{:S(2)}) %collective-permute-start.2) | collective-permute-done | bytes 393248 | tf_op jit(solution)/shard_map/ppermute | solution.py:552
  94.5 4.4 collective-permute-done.7
  100.8 8.0 %collective-permute-done.19 = bf16[128,2048]{1,0:T(8,128)(2,1)S(1)} collective-permute-done((bf16[128,2048]{1,0:T(8,128)(2,1)S(1)}, bf16[128,2048]{1,0:T(8,128)(2,1)S(1)}, u32[]{:S(2)}, u32[]{:S(2)}) %collective-permute-start.19) | collective-permute-done | bytes 524320 | tf_op jit(solution)/shard_map/ppermute | solution.py:552
  110.5 3.3 copy-done.27
  122.5 4.4 concatenate.73.table_ref
  126.9 4.3 constant_dynamic-update-slice_fusion.5.w_ref.wa_ref
  131.2 8.4 %norms.1 = (bf16[1024,2048]{1,0:T(8,128)(2,1)S(1)}, bf16[1024,2048]{1,0:T(8,128)(2,1)}, f32[1024,128]{1,0:T(8,128)S(1)}) custom-call(bf16[1024,2048]{1,0:T(8,128)(2,1)} %all-gather.3.cloned.1.call-done.x_ref, f32[8,2048]{1,0:T(8,128)S(1)} %reorder.8.gain_ref), custom_call_target="tpu_custom_call" | custom-call | flops 20971520 | bytes 12582912 | tf_op jit(solution)/shard_map/norms/pallas_call | solution.py:96
  142.5 10.4 %project.1 = (bf16[1024,512]{1,0:T(8,128)(2,1)S(1)}, bf16[1024,1024]{1,0:T(8,128)(2,1)S(1)}) custom-call(bf16[1024,2048]{1,0:T(8,128)(2,1)} %copy-done.13, bf16[2048,1536]{1,0:T(8,128)(2,1)} %constant_dynamic-update-slice_fusion.5.w_ref.wa_ref, f32[8,1536]{1,0:T(8,128)S(1)} %broadcast_in_dim.38.b_ref, f32[1024,384]{1,0:T(8,128)S(1)} %concatenate.73.table_ref), custom_call_target="tpu_custom_call" | custom-call | flops 6442450944 | bytes 13631488 | tf_op jit(solution)/shard_map/project/pallas_call | solution.py:122
  163.0 17.2 %collective-permute-done.15 = bf16[128,512]{1,0:T(8,128)(2,1)S(1)} collective-permute-done((bf16[128,512]{1,0:T(8,128)(2,1)S(1)}, bf16[128,512]{1,0:T(8,128)(2,1)S(1)}, u32[]{:S(2)}, u32[]{:S(2)}) %collective-permute-start.15) | collective-permute-done | bytes 131104 | tf_op jit(solution)/shard_map/ppermute | solution.py:555
  184.0 2.7 compare_select_fusion
  188.1 5.6 %constant_dynamic-update-slice_fusion.16.w_ref.we_ref = bf16[2048,2048]{1,0:T(8,128)(2,1)} fusion(bf16[2048,2048]{1,0:T(8,128)(2,1)} %copy-done.28, bf16[1024,2048]{1,0:T(8,128)(2,1)} %collective-permute-done.9), kind=kLoop, calls=%fused_computation.43 | loop fusion | bytes 8388608 | tf_op jit(solution)/shard_map/concatenate | solution.py:582
  193.7 4.7 constant_dynamic-update-slice_fusion.40.wh_ref.wc_ref
  198.5 16.7 %expand.1 = (bf16[1024,2048]{1,0:T(8,128)(2,1)S(1)}, bf16[1024,2048]{1,0:T(8,128)(2,1)}) custom-call(bf16[1024,2048]{1,0:T(8,128)(2,1)} %get-tuple-element.89.n_ref.a_ref, bf16[2048,2048]{1,0:T(8,128)(2,1)} %constant_dynamic-update-slice_fusion.16.w_ref.we_ref, f32[8,2048]{1,0:T(8,128)S(1)} %broadcast_in_dim.41.b_ref), custom_call_target="tpu_custom_call" | custom-call | flops 8589934592 | bytes 20971520 | tf_op jit(solution)/shard_map/expand/pallas_call | solution.py:152
  220.9 16.6 %attend.1 = (bf16[1024,512]{1,0:T(8,128)(2,1)S(1)}, f32[2,8,1024]{2,1,0:T(8,128)S(1)}) custom-call(bf16[1024,512]{1,0:T(8,128)(2,1)S(1)} %copy-done.19, bf16[1024,1024]{1,0:T(8,128)(2,1)S(1)} %copy-done.9, bf16[1024,1024]{1,0:T(8,128)(2,1)S(1)} %copy-done.9, bf16[1536,1024]{1,0:T(8,128)(2,1)} %copy-done.26, bf16[1536,1024]{1,0:T(8,128)(2,1)} %copy-done.26, ...), custom_call_target="tpu_custom_call" | custom-call | flops 5368709120 | bytes 7340032 | tf_op jit(solution)/shard_map/attend/pallas_call | solution.py:210
  237.5 16.0 %mixed_sum.1 = bf16[1024,2048]{1,0:T(8,128)(2,1)} custom-call(bf16[1024,512]{1,0:T(8,128)(2,1)S(1)} %get-tuple-element.100.a_ref.o_ref.b_ref, bf16[1024,2048]{1,0:T(8,128)(2,1)} %copy-done.17, bf16[2048,512]{1,0:T(8,128)(2,1)S(1)} %copy-done.11, bf16[2048,2048]{1,0:T(8,128)(2,1)} %constant_dynamic-update-slice_fusion.40.wh_ref.wc_ref), custom_call_target="tpu_custom_call" | custom-call | flops 10737418240 | bytes 19922944 | tf_op jit(solution)/shard_map/mixed_sum/pallas_call | solution.py:363
  255.2 17.0 %branch_grads.1 = (bf16[1024,512]{1,0:T(8,128)(2,1)S(1)}, bf16[1024,2048]{1,0:T(8,128)(2,1)}, f32[8,2048]{1,0:T(8,128)S(1)}) custom-call(bf16[1024,2048]{1,0:T(8,128)(2,1)} %all-gather.5.cloned.1.call-done.g_ref.a_ref, bf16[2048,512]{1,0:T(8,128)(2,1)S(1)} %copy-done.12, bf16[2048,2048]{1,0:T(8,128)(2,1)} %constant_dynamic-update-slice_fusion.40.wh_ref.wc_ref, ...), custom_call_target="tpu_custom_call" | custom-call | flops 10737418240 | bytes 23068672 | tf_op jit(solution)/shard_map/branch_grads/pallas_call | solution.py:400
  272.4 23.0 %attend_back.1 = (bf16[1024,512]{1,0:T(8,128)(2,1)S(1)}, f32[1024,1024]{1,0:T(8,128)}, bf16[512,1024]{1,0:T(8,128)(2,1)S(1)}, bf16[1024,1024]{1,0:T(8,128)(2,1)}) custom-call(bf16[1024,512]{1,0:T(8,128)(2,1)S(1)} %copy-done.20, bf16[1024,512]{1,0:T(8,128)(2,1)S(1)} %get-tuple-element.74.do_ref, bf16[1024,512]{1,0:T(8,128)(2,1)} %copy-done.2, ...), custom_call_target="tpu_custom_call" | custom-call | flops 13421772800 | bytes 18874368 | tf_op jit(solution)/shard_map/attend_back/pallas_call | solution.py:308
  295.4 7.5 %far_product.4 = bf16[1024,2048]{1,0:T(8,128)(2,1)S(1)} custom-call(bf16[1024,2048]{1,0:T(8,128)(2,1)} %all-gather.5.cloned.1.call-done.g_ref.a_ref, bf16[1024,2048]{1,0:T(8,128)(2,1)} %copy-done.17), custom_call_target="tpu_custom_call" | custom-call | flops 4294967296 | bytes 10485760 | tf_op jit(solution)/shard_map/far_product/pallas_call | solution.py:507
  303.5 9.3 %collective-permute-done.23.far_ref = bf16[1024,1024]{1,0:T(8,128)(2,1)S(1)} collective-permute-done((bf16[1024,1024]{1,0:T(8,128)(2,1)S(1)}, bf16[1024,1024]{1,0:T(8,128)(2,1)S(1)}, u32[]{:S(2)}, u32[]{:S(2)}) %collective-permute-start.23) | collective-permute-done | bytes 2097184 | tf_op jit(solution)/shard_map/ppermute | solution.py:558
  316.3 8.1 %near_product.4 = (f32[256,2048]{1,0:T(8,128)S(1)}, bf16[256,2048]{1,0:T(8,128)(2,1)S(1)}, bf16[256,2048]{1,0:T(8,128)(2,1)S(1)}, bf16[256,2048]{1,0:T(8,128)(2,1)S(1)}) custom-call(bf16[1024,2048]{1,0:T(8,128)(2,1)} %all-gather.5.cloned.1.call-done.g_ref.a_ref, bf16[1024,2048]{1,0:T(8,128)(2,1)} %copy-done.17, bf16[1024,2048]{1,0:T(8,128)(2,1)} %collective-permute-done.22.r_ref), custom_call_target="tpu_custom_call" | custom-call | flops 4294967296 | bytes 14680064 | tf_op jit(solution)/shard_map/near_product/pallas_call | solution.py:532
  325.3 8.8 %far_product.5 = bf16[1024,2048]{1,0:T(8,128)(2,1)} custom-call(bf16[1024,2048]{1,0:T(8,128)(2,1)} %get-tuple-element.89.n_ref.a_ref, bf16[1024,2048]{1,0:T(8,128)(2,1)} %get-tuple-element.90.gh_ref.b_ref), custom_call_target="tpu_custom_call" | custom-call | flops 4294967296 | bytes 10485760 | tf_op jit(solution)/shard_map/far_product/pallas_call | solution.py:507
  334.2 4.6 collective-permute-done.24.near_ref
  338.8 7.2 %pack.1 = (bf16[1024,1536]{1,0:T(8,128)(2,1)}, f32[8,1536]{1,0:T(8,128)S(1)}) custom-call(bf16[1024,512]{1,0:T(8,128)(2,1)S(1)} %get-tuple-element.76.q_ref, f32[1024,1024]{1,0:T(8,128)} %get-tuple-element.80.own_ref, bf16[512,1024]{1,0:T(8,128)(2,1)S(1)} %collective-permute-done.24.near_ref, bf16[1024,1024]{1,0:T(8,128)(2,1)S(1)} %collective-permute-done.23.far_ref, ...), custom_call_target="tpu_custom_call" | custom-call | flops 5242880 | bytes 8388608 | tf_op jit(solution)/shard_map/pack/pallas_call | solution.py:440
  347.9 22.2 %unit_grads.1 = (bf16[1024,2048]{1,0:T(8,128)(2,1)}, f32[8,2048]{1,0:T(8,128)S(1)}) custom-call(bf16[1024,1536]{1,0:T(8,128)(2,1)S(1)} %copy-done.14, bf16[1024,2048]{1,0:T(8,128)(2,1)} %get-tuple-element.90.gh_ref.b_ref, bf16[2048,1536]{1,0:T(8,128)(2,1)} %constant_dynamic-update-slice_fusion.5.w_ref.wa_ref, ...), custom_call_target="tpu_custom_call" | custom-call | flops 15032385536 | bytes 30408704 | tf_op jit(solution)/shard_map/unit_grads/pallas_call | solution.py:478
  372.4 3.5 collective-permute-done.26
  377.4 2.8 collective-permute-done.27
  384.6 3.4 collective-permute-start.29
  388.5 3.5 collective-permute-done.37
  400.5 6.1 %collective-permute-done.50 = bf16[128,2048]{1,0:T(8,128)(2,1)} collective-permute-done((bf16[128,2048]{1,0:T(8,128)(2,1)}, bf16[128,2048]{1,0:T(8,128)(2,1)}, u32[]{:S(2)}, u32[]{:S(2)}) %collective-permute-start.50) | collective-permute-done | bytes 524320 | tf_op jit(solution)/shard_map/ppermute | solution.py:552
  410.1 8.1 %near_product.5 = (f32[256,2048]{1,0:T(8,128)S(1)}, bf16[256,2048]{1,0:T(8,128)(2,1)S(1)}, bf16[256,2048]{1,0:T(8,128)(2,1)S(1)}, bf16[256,2048]{1,0:T(8,128)(2,1)S(1)}) custom-call(bf16[1024,2048]{1,0:T(8,128)(2,1)} %get-tuple-element.89.n_ref.a_ref, bf16[1024,2048]{1,0:T(8,128)(2,1)} %get-tuple-element.90.gh_ref.b_ref, ...), custom_call_target="tpu_custom_call" | custom-call | flops 4294967296 | bytes 14680064 | tf_op jit(solution)/shard_map/near_product/pallas_call | solution.py:532
  418.2 7.2 %far_product.6 = bf16[1024,1536]{1,0:T(8,128)(2,1)} custom-call(bf16[1024,2048]{1,0:T(8,128)(2,1)} %copy-done.13, bf16[1024,1536]{1,0:T(8,128)(2,1)} %get-tuple-element.92.gp_ref.b_ref), custom_call_target="tpu_custom_call" | custom-call | flops 3221225472 | bytes 8388608 | tf_op jit(solution)/shard_map/far_product/pallas_call | solution.py:507
  428.7 3.3 convert_add_fusion
  432.7 2.9 far_product.7
  435.7 5.6 %collective-permute-done.44 = bf16[128,2048]{1,0:T(8,128)(2,1)S(1)} collective-permute-done((bf16[128,2048]{1,0:T(8,128)(2,1)S(1)}, bf16[128,2048]{1,0:T(8,128)(2,1)S(1)}, u32[]{:S(2)}, u32[]{:S(2)}) %collective-permute-start.44) | collective-permute-done | bytes 524320 | tf_op jit(solution)/shard_map/ppermute | solution.py:555
  442.3 4.4 collective-permute-done.46
  447.1 6.9 %near_product.6 = (f32[256,1536]{1,0:T(8,128)S(1)}, bf16[256,1536]{1,0:T(8,128)(2,1)S(1)}, bf16[256,1536]{1,0:T(8,128)(2,1)S(1)}, bf16[256,1536]{1,0:T(8,128)(2,1)S(1)}) custom-call(bf16[1024,2048]{1,0:T(8,128)(2,1)} %copy-done.13, bf16[1024,1536]{1,0:T(8,128)(2,1)} %get-tuple-element.92.gp_ref.b_ref, bf16[1024,1536]{1,0:T(8,128)(2,1)} %collective-permute-done.31.r_ref), custom_call_target="tpu_custom_call" | custom-call | flops 3221225472 | bytes 11534336 | tf_op jit(solution)/shard_map/near_product/pallas_call | solution.py:532
  454.0 2.9 near_product.7
  459.9 16.0 %collective-permute-done.40 = bf16[128,512]{1,0:T(8,128)(2,1)S(1)} collective-permute-done((bf16[128,512]{1,0:T(8,128)(2,1)S(1)}, bf16[128,512]{1,0:T(8,128)(2,1)S(1)}, u32[]{:S(2)}, u32[]{:S(2)}) %collective-permute-start.40) | collective-permute-done | bytes 131104 | tf_op jit(solution)/shard_map/ppermute | solution.py:555
  478.1 4.0 collective-permute-done.32
  482.9 3.9 collective-permute-done.34
  494.6 3.4 input_grads.1.x_ref
  499.5 5.5 %collective-permute-done.33 = bf16[256,1536]{1,0:T(8,128)(2,1)S(1)} collective-permute-done((bf16[256,1536]{1,0:T(8,128)(2,1)S(1)}, bf16[256,1536]{1,0:T(8,128)(2,1)S(1)}, u32[]{:S(2)}, u32[]{:S(2)}) %collective-permute-start.33) | collective-permute-done | bytes 786464 | tf_op jit(solution)/shard_map/ppermute | solution.py:552
  507.6 2.2 reshape.56
  (287 shorter events, 117.5 us)
Async XLA Ops:
  7.2 109.8 %all-gather.3.cloned.1.call-start = ((), (), s32[]{:S(2)}) async-start(), calls=%async_computation.2 | async-start | bytes 5242880 | tf_op jit(solution)/shard_map/all_gather | solution.py:709
  9.6 244.0 %all-gather.5.cloned.1.call-start = ((), (), s32[]{:S(2)}) async-start(), calls=%async_computation.4 | async-start | bytes 5242880 | tf_op jit(solution)/shard_map/all_gather | solution.py:712
  10.9 21.4 %collective-permute-start.1 = (bf16[256,1536]{1,0:T(8,128)(2,1)S(1)}, bf16[256,1536]{1,0:T(8,128)(2,1)S(1)}, u32[]{:S(2)}, u32[]{:S(2)}) collective-permute-start(bf16[256,1536]{1,0:T(8,128)(2,1)S(1)} %bitcast.17), channel_id=1, source_target_pairs={{0,8},{8,0},{4,12},{12,4},{1,9},{9,1},{5,13},{13,5},{2,10},{10,2},... | collective-permute-start | bytes 2359304 | tf_op jit(solution)/shard_map/ppermute | solution.py:555
  13.9 22.7 %collective-permute-start = (bf16[256,1536]{1,0:T(8,128)(2,1)S(1)}, bf16[256,1536]{1,0:T(8,128)(2,1)S(1)}, u32[]{:S(2)}, u32[]{:S(2)}) collective-permute-start(bf16[256,1536]{1,0:T(8,128)(2,1)S(1)} %bitcast.18), channel_id=1, source_target_pairs={{0,16},{16,0},{1,17},{17,1},{2,18},{18,2},{3,19},{19,3},{4,20},{20... | collective-permute-start | bytes 2359304 | tf_op jit(solution)/shard_map/ppermute | solution.py:552
  15.4 42.5 %collective-permute-start.5 = (bf16[256,2048]{1,0:T(8,128)(2,1)S(1)}, bf16[256,2048]{1,0:T(8,128)(2,1)S(1)}, u32[]{:S(2)}, u32[]{:S(2)}) collective-permute-start(bf16[256,2048]{1,0:T(8,128)(2,1)S(1)} %copy-done.23), channel_id=1, source_target_pairs={{0,16},{16,0},{1,17},{17,1},{2,18},{18,2},{3,19},{19,3},{4,20},{20... | collective-permute-start | bytes 3145736 | tf_op jit(solution)/shard_map/ppermute | solution.py:552
  15.9 38.8 %collective-permute-start.6 = (bf16[256,2048]{1,0:T(8,128)(2,1)S(1)}, bf16[256,2048]{1,0:T(8,128)(2,1)S(1)}, u32[]{:S(2)}, u32[]{:S(2)}) collective-permute-start(bf16[256,2048]{1,0:T(8,128)(2,1)S(1)} %copy-done.23), channel_id=1, source_target_pairs={{0,8},{8,0},{4,12},{12,4},{1,9},{9,1},{5,13},{13,5},{2,10},{10,2},... | collective-permute-start | bytes 3145736 | tf_op jit(solution)/shard_map/ppermute | solution.py:555
  16.0 63.3 %collective-permute-start.17 = (bf16[256,2048]{1,0:T(8,128)(2,1)S(1)}, bf16[256,2048]{1,0:T(8,128)(2,1)S(1)}, u32[]{:S(2)}, u32[]{:S(2)}) collective-permute-start(bf16[256,2048]{1,0:T(8,128)(2,1)S(1)} %copy-done.24), channel_id=1, source_target_pairs={{0,16},{16,0},{1,17},{17,1},{2,18},{18,2},{3,19},{19,3},{4,20},{20... | collective-permute-start | bytes 3145736 | tf_op jit(solution)/shard_map/ppermute | solution.py:552
  32.2 44.9 %collective-permute-start.18 = (bf16[256,2048]{1,0:T(8,128)(2,1)S(1)}, bf16[256,2048]{1,0:T(8,128)(2,1)S(1)}, u32[]{:S(2)}, u32[]{:S(2)}) collective-permute-start(bf16[256,2048]{1,0:T(8,128)(2,1)S(1)} %copy-done.24), channel_id=1, source_target_pairs={{0,8},{8,0},{4,12},{12,4},{1,9},{9,1},{5,13},{13,5},{2,10},{10,2},... | collective-permute-start | bytes 3145736 | tf_op jit(solution)/shard_map/ppermute | solution.py:555
  36.6 51.1 %collective-permute-start.2 = (bf16[128,1536]{1,0:T(8,128)(2,1)S(1)}, bf16[128,1536]{1,0:T(8,128)(2,1)S(1)}, u32[]{:S(2)}, u32[]{:S(2)}) collective-permute-start(bf16[128,1536]{1,0:T(8,128)(2,1)S(1)} %slice.199), channel_id=1, source_target_pairs={{0,16},{16,0},{1,17},{17,1},{2,18},{18,2},{3,19},{19,3},{4,20},{20... | collective-permute-start | bytes 1179656 | tf_op jit(solution)/shard_map/ppermute | solution.py:552
  54.7 33.8 %collective-permute-start.3 = (bf16[128,1536]{1,0:T(8,128)(2,1)S(1)}, bf16[128,1536]{1,0:T(8,128)(2,1)S(1)}, u32[]{:S(2)}, u32[]{:S(2)}) collective-permute-start(bf16[128,1536]{1,0:T(8,128)(2,1)S(1)} %slice.200), channel_id=1, source_target_pairs={{0,8},{8,0},{4,12},{12,4},{1,9},{9,1},{5,13},{13,5},{2,10},{10,2},... | collective-permute-start | bytes 1179656 | tf_op jit(solution)/shard_map/ppermute | solution.py:555
  57.8 41.1 %collective-permute-start.7 = (bf16[128,2048]{1,0:T(8,128)(2,1)S(1)}, bf16[128,2048]{1,0:T(8,128)(2,1)S(1)}, u32[]{:S(2)}, u32[]{:S(2)}) collective-permute-start(bf16[128,2048]{1,0:T(8,128)(2,1)S(1)} %slice.201), channel_id=1, source_target_pairs={{0,16},{16,0},{1,17},{17,1},{2,18},{18,2},{3,19},{19,3},{4,20},{20... | collective-permute-start | bytes 1572872 | tf_op jit(solution)/shard_map/ppermute | solution.py:552
  77.2 22.7 %collective-permute-start.8 = (bf16[128,2048]{1,0:T(8,128)(2,1)S(1)}, bf16[128,2048]{1,0:T(8,128)(2,1)S(1)}, u32[]{:S(2)}, u32[]{:S(2)}) collective-permute-start(bf16[128,2048]{1,0:T(8,128)(2,1)S(1)} %slice.202), channel_id=1, source_target_pairs={{0,8},{8,0},{4,12},{12,4},{1,9},{9,1},{5,13},{13,5},{2,10},{10,2},... | collective-permute-start | bytes 1572872 | tf_op jit(solution)/shard_map/ppermute | solution.py:555
  79.3 29.4 %collective-permute-start.19 = (bf16[128,2048]{1,0:T(8,128)(2,1)S(1)}, bf16[128,2048]{1,0:T(8,128)(2,1)S(1)}, u32[]{:S(2)}, u32[]{:S(2)}) collective-permute-start(bf16[128,2048]{1,0:T(8,128)(2,1)S(1)} %slice.206), channel_id=1, source_target_pairs={{0,16},{16,0},{1,17},{17,1},{2,18},{18,2},{3,19},{19,3},{4,20},{20... | collective-permute-start | bytes 1572872 | tf_op jit(solution)/shard_map/ppermute | solution.py:552
  87.7 21.9 %collective-permute-start.20 = (bf16[128,2048]{1,0:T(8,128)(2,1)S(1)}, bf16[128,2048]{1,0:T(8,128)(2,1)S(1)}, u32[]{:S(2)}, u32[]{:S(2)}) collective-permute-start(bf16[128,2048]{1,0:T(8,128)(2,1)S(1)} %slice.207), channel_id=1, source_target_pairs={{0,8},{8,0},{4,12},{12,4},{1,9},{9,1},{5,13},{13,5},{2,10},{10,2},... | collective-permute-start | bytes 1572872 | tf_op jit(solution)/shard_map/ppermute | solution.py:555
  89.3 37.6 %collective-permute-start.4 = (bf16[1024,1536]{1,0:T(8,128)(2,1)}, bf16[1024,1536]{1,0:T(8,128)(2,1)}, u32[]{:S(2)}, u32[]{:S(2)}) collective-permute-start(bf16[1024,1536]{1,0:T(8,128)(2,1)} %get-tuple-element.157), channel_id=1, source_target_pairs={{0,4},{4,0},{8,12},{12,8},{1,5},{5,1},{9,13},{13,9},{2,6},{6,2},{1... | collective-permute-start | bytes 9437192 | tf_op jit(solution)/shard_map/ppermute | solution.py:558
  100.8 87.4 %collective-permute-start.9 = (bf16[1024,2048]{1,0:T(8,128)(2,1)}, bf16[1024,2048]{1,0:T(8,128)(2,1)}, u32[]{:S(2)}, u32[]{:S(2)}) collective-permute-start(bf16[1024,2048]{1,0:T(8,128)(2,1)} %get-tuple-element.153), channel_id=1, source_target_pairs={{0,4},{4,0},{8,12},{12,8},{1,5},{5,1},{9,13},{13,9},{2,6},{6,2},{1... | collective-permute-start | bytes 12582920 | tf_op jit(solution)/shard_map/ppermute | solution.py:558
  110.5 83.2 %collective-permute-start.21 = (bf16[1024,2048]{1,0:T(8,128)(2,1)}, bf16[1024,2048]{1,0:T(8,128)(2,1)}, u32[]{:S(2)}, u32[]{:S(2)}) collective-permute-start(bf16[1024,2048]{1,0:T(8,128)(2,1)} %get-tuple-element.149), channel_id=1, source_target_pairs={{0,4},{4,0},{8,12},{12,8},{1,5},{5,1},{9,13},{13,9},{2,6},{6,2},{1... | collective-permute-start | bytes 12582920 | tf_op jit(solution)/shard_map/ppermute | solution.py:558
  113.8 44.2 %collective-permute-start.12 = (bf16[256,512]{1,0:T(8,128)(2,1)}, bf16[256,512]{1,0:T(8,128)(2,1)}, u32[]{:S(2)}, u32[]{:S(2)}) collective-permute-start(bf16[256,512]{1,0:T(8,128)(2,1)} %param.25), channel_id=1, source_target_pairs={{0,16},{16,0},{1,17},{17,1},{2,18},{18,2},{3,19},{19,3},{4,20},{20... | collective-permute-start | bytes 786440 | tf_op jit(solution)/shard_map/ppermute | solution.py:552
  115.3 42.0 %collective-permute-start.13 = (bf16[256,512]{1,0:T(8,128)(2,1)}, bf16[256,512]{1,0:T(8,128)(2,1)S(1)}, u32[]{:S(2)}, u32[]{:S(2)}) collective-permute-start(bf16[256,512]{1,0:T(8,128)(2,1)} %param.25), channel_id=1, source_target_pairs={{0,8},{8,0},{4,12},{12,4},{1,9},{9,1},{5,13},{13,5},{2,10},{10,2},... | collective-permute-start | bytes 786440 | tf_op jit(solution)/shard_map/ppermute | solution.py:555
  117.0 290.9 %reduce-scatter.3.cloned.1.call-start = ((), (), s32[]{:S(2)}) async-start(), calls=%async_computation.3 | async-start | bytes 5242880 | tf_op jit(solution)/shard_map/reduce_scatter | solution.py:735
  154.0 26.8 %collective-permute-start.10 = (bf16[512,1024]{1,0:T(8,128)(2,1)S(1)}, bf16[512,1024]{1,0:T(8,128)(2,1)S(1)}, u32[]{:S(2)}, u32[]{:S(2)}) collective-permute-start(bf16[512,1024]{1,0:T(8,128)(2,1)S(1)} %slice.156), channel_id=1, source_target_pairs={{0,8},{8,0},{4,12},{12,4},{1,9},{9,1},{5,13},{13,5},{2,10},{10,2},... | collective-permute-start | bytes 3145736 | tf_op jit(solution)/shard_map/ppermute | solution.py:555
  159.0 21.2 %collective-permute-start.15 = (bf16[128,512]{1,0:T(8,128)(2,1)S(1)}, bf16[128,512]{1,0:T(8,128)(2,1)S(1)}, u32[]{:S(2)}, u32[]{:S(2)}) collective-permute-start(bf16[128,512]{1,0:T(8,128)(2,1)S(1)} %slice.205), channel_id=1, source_target_pairs={{0,8},{8,0},{4,12},{12,4},{1,9},{9,1},{5,13},{13,5},{2,10},{10,2},... | collective-permute-start | bytes 393224 | tf_op jit(solution)/shard_map/ppermute | solution.py:555
  182.5 34.9 %collective-permute-start.11 = (bf16[1024,1024]{1,0:T(8,128)(2,1)}, bf16[1024,1024]{1,0:T(8,128)(2,1)}, u32[]{:S(2)}, u32[]{:S(2)}) collective-permute-start(bf16[1024,1024]{1,0:T(8,128)(2,1)} %pad_maximum_fusion), channel_id=1, source_target_pairs={{0,4},{4,0},{8,12},{12,8},{1,5},{5,1},{9,13},{13,9},{2,6},{6,2},{1... | collective-permute-start | bytes 6291464 | tf_op jit(solution)/shard_map/ppermute | solution.py:558
  253.6 239.8 %reduce-scatter.5.cloned.1.call-start = ((), (), s32[]{:S(2)}) async-start(), calls=%async_computation.5 | async-start | bytes 5242880 | tf_op jit(solution)/shard_map/reduce_scatter | solution.py:749
  302.9 13.3 %collective-permute-start.22 = (bf16[1024,2048]{1,0:T(8,128)(2,1)S(1)}, bf16[1024,2048]{1,0:T(8,128)(2,1)}, u32[]{:S(2)}, u32[]{:S(2)}) collective-permute-start(bf16[1024,2048]{1,0:T(8,128)(2,1)S(1)} %far_product.4), channel_id=1, source_target_pairs={{0,4},{4,0},{8,12},{12,8},{1,5},{5,1},{9,13},{13,9},{2,6},{6,2},{1... | collective-permute-start | bytes 12582920 | tf_op jit(solution)/shard_map/ppermute | solution.py:558
  303.0 9.8 %collective-permute-start.23 = (bf16[1024,1024]{1,0:T(8,128)(2,1)S(1)}, bf16[1024,1024]{1,0:T(8,128)(2,1)S(1)}, u32[]{:S(2)}, u32[]{:S(2)}) collective-permute-start(bf16[1024,1024]{1,0:T(8,128)(2,1)S(1)} %copy-done.40), channel_id=1, source_target_pairs={{0,4},{4,0},{8,12},{12,8},{1,5},{5,1},{9,13},{13,9},{2,6},{6,2},{1... | collective-permute-start | bytes 6291464 | tf_op jit(solution)/shard_map/ppermute | solution.py:558
  313.3 25.5 %collective-permute-start.24 = (bf16[512,1024]{1,0:T(8,128)(2,1)S(1)}, bf16[512,1024]{1,0:T(8,128)(2,1)S(1)}, u32[]{:S(2)}, u32[]{:S(2)}) collective-permute-start(bf16[512,1024]{1,0:T(8,128)(2,1)S(1)} %add.110), channel_id=1, source_target_pairs={{0,8},{8,0},{4,12},{12,4},{1,9},{9,1},{5,13},{13,5},{2,10},{10,2},... | collective-permute-start | bytes 3145736 | tf_op jit(solution)/shard_map/ppermute | solution.py:555
  334.1 75.9 %collective-permute-start.30 = (bf16[1024,2048]{1,0:T(8,128)(2,1)}, bf16[1024,2048]{1,0:T(8,128)(2,1)}, u32[]{:S(2)}, u32[]{:S(2)}) collective-permute-start(bf16[1024,2048]{1,0:T(8,128)(2,1)} %far_product.5), channel_id=1, source_target_pairs={{0,4},{4,0},{8,12},{12,8},{1,5},{5,1},{9,13},{13,9},{2,6},{6,2},{1... | collective-permute-start | bytes 12582920 | tf_op jit(solution)/shard_map/ppermute | solution.py:558
  377.4 10.5 %collective-permute-start.36 = (f32[3584]{0:T(1024)S(1)}, f32[3584]{0:T(1024)S(1)}, u32[]{:S(2)}, u32[]{:S(2)}) collective-permute-start(f32[3584]{0:T(1024)S(1)} %pad_maximum_fusion.9), channel_id=1, source_target_pairs={{0,4},{4,0},{8,12},{12,8},{1,5},{5,1},{9,13},{13,9},{2,6},{6,2},{1... | collective-permute-start | bytes 43016 | tf_op jit(solution)/shard_map/ppermute | solution.py:558
  382.9 14.7 %collective-permute-start.48 = (bf16[128,2048]{1,0:T(8,128)(2,1)}, bf16[128,2048]{1,0:T(8,128)(2,1)}, u32[]{:S(2)}, u32[]{:S(2)}) collective-permute-start(bf16[128,2048]{1,0:T(8,128)(2,1)} %get-tuple-element.115), channel_id=1, source_target_pairs={{0,8},{8,0},{4,12},{12,4},{1,9},{9,1},{5,13},{13,5},{2,10},{10,2},... | collective-permute-start | bytes 1572872 | tf_op jit(solution)/shard_map/ppermute | solution.py:555
  384.6 12.3 %collective-permute-start.29 = (f32[8,2048]{1,0:T(8,128)S(1)}, f32[8,2048]{1,0:T(8,128)S(1)}, u32[]{:S(2)}, u32[]{:S(2)}) collective-permute-start(f32[8,2048]{1,0:T(8,128)S(1)} %add.114), channel_id=1, source_target_pairs={{0,2},{1,3},{2,0},{3,1},{4,6},{5,7},{6,4},{7,5},{8,10},{9,11},{10,... | collective-permute-start | bytes 196616 | tf_op jit(solution)/shard_map/ppermute | solution.py:660
  393.3 13.3 %collective-permute-start.50 = (bf16[128,2048]{1,0:T(8,128)(2,1)}, bf16[128,2048]{1,0:T(8,128)(2,1)}, u32[]{:S(2)}, u32[]{:S(2)}) collective-permute-start(bf16[128,2048]{1,0:T(8,128)(2,1)} %get-tuple-element.116), channel_id=1, source_target_pairs={{0,16},{16,0},{1,17},{17,1},{2,18},{18,2},{3,19},{19,3},{4,20},{20... | collective-permute-start | bytes 1572872 | tf_op jit(solution)/shard_map/ppermute | solution.py:552
  400.4 28.2 %collective-permute-start.49 = (bf16[256,2048]{1,0:T(8,128)(2,1)}, bf16[256,2048]{1,0:T(8,128)(2,1)}, u32[]{:S(2)}, u32[]{:S(2)}) collective-permute-start(bf16[256,2048]{1,0:T(8,128)(2,1)} %pad_maximum_fusion.3), channel_id=1, source_target_pairs={{0,16},{16,0},{1,17},{17,1},{2,18},{18,2},{3,19},{19,3},{4,20},{20... | collective-permute-start | bytes 3145736 | tf_op jit(solution)/shard_map/ppermute | solution.py:552
  407.9 20.8 %collective-permute-start.51 = (bf16[256,2048]{1,0:T(8,128)(2,1)S(1)}, bf16[256,2048]{1,0:T(8,128)(2,1)}, u32[]{:S(2)}, u32[]{:S(2)}) collective-permute-start(bf16[256,2048]{1,0:T(8,128)(2,1)S(1)} %pad_maximum_fusion.4), channel_id=1, source_target_pairs={{0,8},{8,0},{4,12},{12,4},{1,9},{9,1},{5,13},{13,5},{2,10},{10,2},... | collective-permute-start | bytes 3145736 | tf_op jit(solution)/shard_map/ppermute | solution.py:555
  425.3 21.7 %collective-permute-start.31 = (bf16[1024,1536]{1,0:T(8,128)(2,1)}, bf16[1024,1536]{1,0:T(8,128)(2,1)}, u32[]{:S(2)}, u32[]{:S(2)}) collective-permute-start(bf16[1024,1536]{1,0:T(8,128)(2,1)} %far_product.6), channel_id=1, source_target_pairs={{0,4},{4,0},{8,12},{12,8},{1,5},{5,1},{9,13},{13,9},{2,6},{6,2},{1... | collective-permute-start | bytes 9437192 | tf_op jit(solution)/shard_map/ppermute | solution.py:558
  426.6 14.6 %collective-permute-start.44 = (bf16[128,2048]{1,0:T(8,128)(2,1)S(1)}, bf16[128,2048]{1,0:T(8,128)(2,1)S(1)}, u32[]{:S(2)}, u32[]{:S(2)}) collective-permute-start(bf16[128,2048]{1,0:T(8,128)(2,1)S(1)} %get-tuple-element.121), channel_id=1, source_target_pairs={{0,8},{8,0},{4,12},{12,4},{1,9},{9,1},{5,13},{13,5},{2,10},{10,2},... | collective-permute-start | bytes 1572872 | tf_op jit(solution)/shard_map/ppermute | solution.py:555
  431.9 14.8 %collective-permute-start.46 = (bf16[128,2048]{1,0:T(8,128)(2,1)S(1)}, bf16[128,2048]{1,0:T(8,128)(2,1)S(1)}, u32[]{:S(2)}, u32[]{:S(2)}) collective-permute-start(bf16[128,2048]{1,0:T(8,128)(2,1)S(1)} %get-tuple-element.122), channel_id=1, source_target_pairs={{0,16},{16,0},{1,17},{17,1},{2,18},{18,2},{3,19},{19,3},{4,20},{20... | collective-permute-start | bytes 1572872 | tf_op jit(solution)/shard_map/ppermute | solution.py:552
  435.6 18.4 %collective-permute-start.39 = (bf16[1024,512]{1,0:T(8,128)(2,1)S(1)}, bf16[1024,512]{1,0:T(8,128)(2,1)S(1)}, u32[]{:S(2)}, u32[]{:S(2)}) collective-permute-start(bf16[1024,512]{1,0:T(8,128)(2,1)S(1)} %far_product.7), channel_id=1, source_target_pairs={{0,4},{4,0},{8,12},{12,8},{1,5},{5,1},{9,13},{13,9},{2,6},{6,2},{1... | collective-permute-start | bytes 3145736 | tf_op jit(solution)/shard_map/ppermute | solution.py:558
  441.4 47.4 %collective-permute-start.45 = (bf16[256,2048]{1,0:T(8,128)(2,1)S(1)}, bf16[256,2048]{1,0:T(8,128)(2,1)S(1)}, u32[]{:S(2)}, u32[]{:S(2)}) collective-permute-start(bf16[256,2048]{1,0:T(8,128)(2,1)S(1)} %pad_maximum_fusion.1), channel_id=1, source_target_pairs={{0,16},{16,0},{1,17},{17,1},{2,18},{18,2},{3,19},{19,3},{4,20},{20... | collective-permute-start | bytes 3145736 | tf_op jit(solution)/shard_map/ppermute | solution.py:552
  446.9 43.0 %collective-permute-start.47 = (bf16[256,2048]{1,0:T(8,128)(2,1)S(1)}, bf16[256,2048]{1,0:T(8,128)(2,1)S(1)}, u32[]{:S(2)}, u32[]{:S(2)}) collective-permute-start(bf16[256,2048]{1,0:T(8,128)(2,1)S(1)} %pad_maximum_fusion.2), channel_id=1, source_target_pairs={{0,8},{8,0},{4,12},{12,4},{1,9},{9,1},{5,13},{13,5},{2,10},{10,2},... | collective-permute-start | bytes 3145736 | tf_op jit(solution)/shard_map/ppermute | solution.py:555
  456.9 19.0 %collective-permute-start.40 = (bf16[128,512]{1,0:T(8,128)(2,1)S(1)}, bf16[128,512]{1,0:T(8,128)(2,1)S(1)}, u32[]{:S(2)}, u32[]{:S(2)}) collective-permute-start(bf16[128,512]{1,0:T(8,128)(2,1)S(1)} %get-tuple-element.163), channel_id=1, source_target_pairs={{0,8},{8,0},{4,12},{12,4},{1,9},{9,1},{5,13},{13,5},{2,10},{10,2},... | collective-permute-start | bytes 393224 | tf_op jit(solution)/shard_map/ppermute | solution.py:555
  458.8 17.9 %collective-permute-start.42 = (bf16[128,512]{1,0:T(8,128)(2,1)S(1)}, bf16[128,512]{1,0:T(8,128)(2,1)S(1)}, u32[]{:S(2)}, u32[]{:S(2)}) collective-permute-start(bf16[128,512]{1,0:T(8,128)(2,1)S(1)} %get-tuple-element.164), channel_id=1, source_target_pairs={{0,16},{16,0},{1,17},{17,1},{2,18},{18,2},{3,19},{19,3},{4,20},{20... | collective-permute-start | bytes 393224 | tf_op jit(solution)/shard_map/ppermute | solution.py:552
  459.7 22.4 %collective-permute-start.32 = (bf16[128,1536]{1,0:T(8,128)(2,1)S(1)}, bf16[128,1536]{1,0:T(8,128)(2,1)S(1)}, u32[]{:S(2)}, u32[]{:S(2)}) collective-permute-start(bf16[128,1536]{1,0:T(8,128)(2,1)S(1)} %get-tuple-element.139), channel_id=1, source_target_pairs={{0,8},{8,0},{4,12},{12,4},{1,9},{9,1},{5,13},{13,5},{2,10},{10,2},... | collective-permute-start | bytes 1179656 | tf_op jit(solution)/shard_map/ppermute | solution.py:555
  475.9 11.0 %collective-permute-start.34 = (bf16[128,1536]{1,0:T(8,128)(2,1)S(1)}, bf16[128,1536]{1,0:T(8,128)(2,1)S(1)}, u32[]{:S(2)}, u32[]{:S(2)}) collective-permute-start(bf16[128,1536]{1,0:T(8,128)(2,1)S(1)} %get-tuple-element.140), channel_id=1, source_target_pairs={{0,16},{16,0},{1,17},{17,1},{2,18},{18,2},{3,19},{19,3},{4,20},{20... | collective-permute-start | bytes 1179656 | tf_op jit(solution)/shard_map/ppermute | solution.py:552
  476.7 15.8 %collective-permute-start.41 = (bf16[256,512]{1,0:T(8,128)(2,1)S(1)}, bf16[256,512]{1,0:T(8,128)(2,1)S(1)}, u32[]{:S(2)}, u32[]{:S(2)}) collective-permute-start(bf16[256,512]{1,0:T(8,128)(2,1)S(1)} %pad_maximum_fusion.7), channel_id=1, source_target_pairs={{0,16},{16,0},{1,17},{17,1},{2,18},{18,2},{3,19},{19,3},{4,20},{20... | collective-permute-start | bytes 786440 | tf_op jit(solution)/shard_map/ppermute | solution.py:552
  482.1 10.4 %collective-permute-start.43 = (bf16[256,512]{1,0:T(8,128)(2,1)S(1)}, bf16[256,512]{1,0:T(8,128)(2,1)S(1)}, u32[]{:S(2)}, u32[]{:S(2)}) collective-permute-start(bf16[256,512]{1,0:T(8,128)(2,1)S(1)} %pad_maximum_fusion.8), channel_id=1, source_target_pairs={{0,8},{8,0},{4,12},{12,4},{1,9},{9,1},{5,13},{13,5},{2,10},{10,2},... | collective-permute-start | bytes 786440 | tf_op jit(solution)/shard_map/ppermute | solution.py:555
  486.8 18.2 %collective-permute-start.33 = (bf16[256,1536]{1,0:T(8,128)(2,1)S(1)}, bf16[256,1536]{1,0:T(8,128)(2,1)S(1)}, u32[]{:S(2)}, u32[]{:S(2)}) collective-permute-start(bf16[256,1536]{1,0:T(8,128)(2,1)S(1)} %pad_maximum_fusion.5), channel_id=1, source_target_pairs={{0,16},{16,0},{1,17},{17,1},{2,18},{18,2},{3,19},{19,3},{4,20},{20... | collective-permute-start | bytes 2359304 | tf_op jit(solution)/shard_map/ppermute | solution.py:552
  488.8 17.1 %collective-permute-start.35 = (bf16[256,1536]{1,0:T(8,128)(2,1)}, bf16[256,1536]{1,0:T(8,128)(2,1)}, u32[]{:S(2)}, u32[]{:S(2)}) collective-permute-start(bf16[256,1536]{1,0:T(8,128)(2,1)} %pad_maximum_fusion.6), channel_id=1, source_target_pairs={{0,8},{8,0},{4,12},{12,4},{1,9},{9,1},{5,13},{13,5},{2,10},{10,2},... | collective-permute-start | bytes 2359304 | tf_op jit(solution)/shard_map/ppermute | solution.py:555
  (50 other events, 479.3 us)
Sparse Core Ops, SparseCore 0:
  9.7 83.4 all-gather.2
  117.2 81.0 all-gather.4
  253.7 77.0 reduce-scatter.2
  394.1 74.3 reduce-scatter.4

commit v3 on v2

--- a/solution.py
+++ b/solution.py
@@ -78,29 +78,34 @@
     return call(partial(reorder_kernel, places), (), [block], block, shape(rows, cols, kind=x.dtype), 0, 4 * rows * cols, name="reorder")(x)
 
 
-def norm_kernel(x_ref, gain_ref, first_ref, second_ref, stat_ref):
+def norm_kernel(places, x_ref, gain_ref, first_ref, second_ref, x_out, stat_ref):
     x = x_ref[...].astype(F32)
     mean = jnp.mean(x, -1, keepdims=True)
     center = x - mean
     scale = lax.rsqrt(jnp.mean(center * center, -1, keepdims=True) + EPS)
-    unit = center * scale
-    first_ref[...] = (unit * gain_ref[0:1] + gain_ref[1:2]).astype(BF16)
-    second_ref[...] = (unit * gain_ref[2:3] + gain_ref[3:4]).astype(BF16)
+    size = x_ref.shape[1] // len(places)
+    for i, place in enumerate(places):
+        at, to = pl.ds(pl.multiple_of(place() * size, size), size), pl.ds(i * size, size)
+        part = x_ref[:, at]
+        x_out[:, to] = part
+        unit = (part.astype(F32) - mean) * scale
+        first_ref[:, to] = (unit * gain_ref[0:1, at] + gain_ref[1:2, at]).astype(BF16)
+        second_ref[:, to] = (unit * gain_ref[2:3, at] + gain_ref[3:4, at]).astype(BF16)
     lane = lax.broadcasted_iota(jnp.int32, stat_ref.shape, 1)
     stat_ref[...] = jnp.where(lane == 0, mean, scale)
 
 
-def norms(x, gains):
+def norms(x, gains, places):
     rows, width = x.shape
     block = pl.BlockSpec((128, width), lambda i: (i, 0))
     return call(
-        norm_kernel,
+        partial(norm_kernel, places),
         (rows // 128,),
         [block, pl.BlockSpec((8, width), lambda i: (0, 0))],
-        [block, block, pl.BlockSpec((128, 128), lambda i: (i, 0))],
-        [shape(rows, width), shape(rows, width), shape(rows, 128, kind=F32)],
+        [block, block, block, pl.BlockSpec((128, 128), lambda i: (i, 0))],
+        [shape(rows, width)] * 3 + [shape(rows, 128, kind=F32)],
         10 * rows * width,
-        6 * rows * width,
+        8 * rows * width,
         name="norms",
     )(x, gains)
 
@@ -377,41 +382,51 @@
     )(attended, activated, w_out, w_contract)
 
 
-def grads_kernel(g_ref, wo_ref, wc_ref, d_ref, do_ref, gp_ref, sum_ref):
-    @pl.when(pl.program_id(0) == 0)
-    def _():
-        for i in range(g_ref.shape[0] // ROWS):
-            at = pl.ds(i * ROWS, ROWS)
-            do_ref[at, :] = mul(g_ref[at, :], wo_ref[...], NN).astype(BF16)
-
+def attended_grad_kernel(g_ref, w_ref, o_ref):
+    for i in range(g_ref.shape[0] // ROWS):
+        at = pl.ds(i * ROWS, ROWS)
+        o_ref[at, :] = mul(g_ref[at, :], w_ref[...], NN).astype(BF16)
+
+
+def attended_grads(g, w, tile=256):
+    rows, depth = g.shape
+    cols = w.shape[1]
+    return call(
+        attended_grad_kernel,
+        (cols // tile,),
+        [pl.BlockSpec((rows, depth), lambda j: (0, 0)), pl.BlockSpec((depth, tile), lambda j: (0, j))],
+        pl.BlockSpec((rows, tile), lambda j: (0, j)),
+        shape(rows, cols),
+        2 * rows * depth * cols,
+        2 * (rows * depth + w.size + rows * cols),
+        name="attended_grads",
+    )(g, w)
+
+
+def hidden_grad_kernel(g_ref, w_ref, d_ref, gp_ref, sum_ref):
     total = 0.0
     for i in range(g_ref.shape[0] // ROWS):
         at = pl.ds(i * ROWS, ROWS)
-        grad = (mul(g_ref[at, :], wc_ref[...], NN) * d_ref[at, :].astype(F32)).astype(BF16)
+        grad = (mul(g_ref[at, :], w_ref[...], NN) * d_ref[at, :].astype(F32)).astype(BF16)
         gp_ref[at, :] = grad
         total += jnp.sum(grad.astype(F32), 0, keepdims=True)
     sum_ref[...] = jnp.broadcast_to(total, sum_ref.shape)
 
 
-def branch_grads(g, w_out, w_contract, slope, tile=512):
+def hidden_grads(g, w, slope, tile=512):
     rows, depth = g.shape
-    deep, cols = w_out.shape[1], w_contract.shape[1]
+    cols = w.shape[1]
     tall = pl.BlockSpec((rows, tile), lambda j: (0, j))
     return call(
-        grads_kernel,
+        hidden_grad_kernel,
         (cols // tile,),
-        [
-            pl.BlockSpec((rows, depth), lambda j: (0, 0)),
-            pl.BlockSpec((depth, deep), lambda j: (0, 0)),
-            pl.BlockSpec((depth, tile), lambda j: (0, j)),
-            tall,
-        ],
-        [pl.BlockSpec((rows, deep), lambda j: (0, 0)), tall, pl.BlockSpec((8, tile), lambda j: (0, j))],
-        [shape(rows, deep), shape(rows, cols), shape(8, cols, kind=F32)],
-        2 * rows * depth * (deep + cols),
-        2 * (rows * depth + depth * (deep + cols) + 2 * rows * cols),
-        name="branch_grads",
-    )(g, w_out, w_contract, slope)
+        [pl.BlockSpec((rows, depth), lambda j: (0, 0)), pl.BlockSpec((depth, tile), lambda j: (0, j)), tall],
+        [tall, pl.BlockSpec((8, tile), lambda j: (0, j))],
+        [shape(rows, cols), shape(8, cols, kind=F32)],
+        2 * rows * depth * cols,
+        2 * (rows * depth + w.size + 2 * rows * cols),
+        name="hidden_grads",
+    )(g, w, slope)
 
 
 def pack_kernel(prompt_blocks, q_ref, own_ref, near_ref, far_ref, table_ref, o_ref, sum_ref):
@@ -545,6 +560,134 @@
     )(a, b, received)
 
 
+class Hops:
+    def __init__(self, send, recv):
+        self.send, self.recv, self.count = send, recv, 0
+        f, c, t = (lax.axis_index(a) for a in ("fsdp", "ctx", "tp"))
+        ring = lax.axis_size("tp")
+        self.to = {
+            "x": {"fsdp": 1 - f},
+            "y": {"ctx": (c + 2) % 4},
+            "core": {"ctx": c + 1 - 2 * (c % 2)},
+            "up": {"tp": (t + 1) % ring},
+        }
+        self.back = {"tp": (t + ring - 1) % ring}
+
+    def greet(self):
+        barrier = pltpu.get_barrier_semaphore()
+        near = [*self.to.values(), self.back]
+        for device in near:
+            pl.semaphore_signal(barrier, inc=1, device_id=device, device_id_type=pl.DeviceIdType.MESH)
+        pl.semaphore_wait(barrier, len(near))
+
+    def copy(self, way, src, dst):
+        made = pltpu.make_async_remote_copy(
+            src, dst, self.send.at[self.count], self.recv.at[self.count],
+            device_id=self.to[way], device_id_type=pl.DeviceIdType.MESH,
+        )
+        self.count += 1
+        made.start()
+        return made
+
+
+def collect_kernel(n, x_ref, *refs):
+    parts, rows_ref, wholes = refs[:n], refs[n], refs[n + 1 : 2 * n + 1]
+    send, recv, local = refs[2 * n + 1 :]
+    hops = Hops(send, recv)
+    t, ring = lax.axis_index("tp"), lax.axis_size("tp")
+    rows = x_ref.shape[0]
+    chunk = rows // 2
+    own = [pltpu.make_async_copy(p, w.at[pl.ds(0, p.shape[0])], local.at[1 + i]) for i, (p, w) in enumerate(zip(parts, wholes))]
+    own.append(pltpu.make_async_copy(x_ref, rows_ref.at[pl.ds(t * rows, rows)], local.at[0]))
+    for copy in own:
+        copy.start()
+    hops.greet()
+    sent = []
+
+    def ring_hop(step, part):
+        at = pl.ds(((t + ring - step) % ring) * rows + part * chunk, chunk)
+        src = x_ref.at[pl.ds(part * chunk, chunk)] if step == 0 else rows_ref.at[at]
+        return hops.copy("up", src, rows_ref.at[at])
+
+    def first(i):
+        size = parts[i].shape[0]
+        return [hops.copy(way, parts[i], wholes[i].at[pl.ds(slot * size, size)]) for way, slot in (("x", 1), ("y", 2))]
+
+    def across(i, slots):
+        size = parts[i].shape[0]
+        for slot in slots:
+            src = parts[i] if slot == 0 else wholes[i].at[pl.ds(slot * size, size)]
+            sent.append(hops.copy("core", src, wholes[i].at[pl.ds((4 + slot) * size, size)]))
+
+    def corner(i):
+        size = parts[i].shape[0]
+        half = size // 2
+        top, low = pl.ds(3 * size, half), pl.ds(3 * size + half, half)
+        return [
+            hops.copy("x", wholes[i].at[pl.ds(2 * size, half)], wholes[i].at[top]),
+            hops.copy("y", wholes[i].at[pl.ds(size + half, half)], wholes[i].at[low]),
+        ]
+
+    def arrive(copies):
+        for copy in copies:
+            copy.wait_recv()
+        sent.extend(("sent", copy) for copy in copies)
+
+    firsts, corners, rings = {}, {}, {}
+    firsts[0] = first(0)
+    rings[0, 0], rings[0, 1] = ring_hop(0, 0), ring_hop(0, 1)
+    if n > 1:
+        firsts[1] = first(1)
+    for i in range(n):
+        across(i, [0])
+    plan = [("r", 0, 0), ("f", 0), ("r", 0, 1), ("r", 1, 0), ("f", 1), ("r", 1, 1), ("c", 0), ("f", 2), ("r", 2, 0), ("c", 1), ("r", 2, 1), ("c", 2)]
+    for kind, *which in plan:
+        if kind == "r":
+            step, part = which
+            arrive([rings[step, part]])
+            if step < ring - 2:
+                rings[step + 1, part] = ring_hop(step + 1, part)
+            continue
+        i = which[0]
+        if kind == "f":
+            arrive(firsts[i])
+            corners[i] = corner(i)
+            if i + 2 < n:
+                firsts[i + 2] = first(i + 2)
+            across(i, [1, 2])
+        else:
+            arrive(corners[i])
+            across(i, [3])
+    for copy in sent:
+        if isinstance(copy, tuple):
+            copy[1].wait_send()
+        else:
+            copy.wait()
+    for copy in own:
+        copy.wait()
+
+
+def collect(x, parts):
+    ring = lax.axis_size("tp")
+    n = len(parts)
+    copies = 2 * (ring - 1) + 8 * n
+    ref = pl.BlockSpec(memory_space=pl.ANY)
+    return pl.pallas_call(
+        partial(collect_kernel, n),
+        in_specs=[ref] * (n + 1),
+        out_specs=[ref] * (n + 1),
+        out_shape=[shape(ring * x.shape[0], x.shape[1])] + [shape(8 * p.shape[0], p.shape[1]) for p in parts],
+        scratch_shapes=[
+            pltpu.SemaphoreType.DMA((copies,)),
+            pltpu.SemaphoreType.DMA((copies,)),
+            pltpu.SemaphoreType.DMA((n + 1,)),
+        ],
+        compiler_params=pltpu.CompilerParams(collective_id=0, has_side_effects=True),
+        cost_estimate=pl.CostEstimate(flops=0, bytes_accessed=200 * 2**20, transcendentals=0),
+        name="collect",
+    )(x, *parts)
+
+
 class SquareLinks:
     order = ((0, 0, 0), (1, 0, 0), (0, 1, 0), (1, 1, 0), (0, 0, 1), (1, 0, 1), (0, 1, 1), (1, 1, 1))
 
@@ -567,11 +710,20 @@
         a, b, d = f ^ (p // 4), (c // 2) ^ (p // 2 % 2), (c % 2) ^ (p % 2)
         return d * 4 + b * 2 + a
 
+    def places(self):
+        return [partial(self.place, bits) for bits in self.order]
+
+    def spots(self):
+        return [partial(self.spot, p) for p in range(8)]
+
     def to_relative(self, v):
-        return reorder(v, [partial(self.place, bits) for bits in self.order])
+        return reorder(v, self.places())
 
     def to_whole(self, v):
-        return reorder(v, [partial(self.spot, p) for p in range(8)])
+        return reorder(v, self.spots())
+
+    def collect(self, x, parts):
+        return collect(x, parts)
 
     def gather(self, block):
         rows = block.shape[0]
@@ -605,7 +757,7 @@
     def scatter_others(self, near, far):
         theirs = self.core_hop(far)
         rows = near.shape[0]
-        return theirs, lambda token: self.y_hop(after(theirs[rows:], token) + near)
+        return theirs, lambda token: self.y_hop(after(theirs, token)[rows:] + near)
 
     def sum_rows(self, v):
         v = v + self.core_hop(v)
@@ -614,6 +766,15 @@
 
 
 class AnyLinks:
+    def places(self):
+        return [lambda: 0]
+
+    def spots(self):
+        return [lambda: 0]
+
+    def collect(self, x, parts):
+        return [lax.all_gather(x, "tp", axis=0, tiled=True)] + [self.gather(part) for part in parts]
+
     def to_relative(self, v):
         return v
 
@@ -662,21 +823,54 @@
     return v
 
 
-def end_kernel(x_ref, g_ref, e_ref, o_ref):
+def output_kernel(spots, x_ref, m_ref, b_ref, o_ref):
+    size = x_ref.shape[1] // len(spots)
+    for i, spot in enumerate(spots):
+        at, to = pl.ds(pl.multiple_of(spot() * size, size), size), pl.ds(i * size, size)
+        o_ref[:, to] = (x_ref[:, to].astype(F32) + m_ref[:, at].astype(F32) + b_ref[:1, to]).astype(BF16)
+
+
+def output_rows(x, mixed, bias, spots):
+    rows, width = x.shape
+    block = pl.BlockSpec((64, width), lambda i: (i, 0))
+    return call(
+        partial(output_kernel, spots),
+        (rows // 64,),
+        [block, block, pl.BlockSpec((8, width), lambda i: (0, 0))],
+        block,
+        shape(rows, width),
+        2 * x.size,
+        6 * x.size,
+        name="output_rows",
+    )(x, mixed, wide(bias))
+
+
+def end_kernel(spots, x_ref, g_ref, e_ref, o_ref, e_whole):
+    size = x_ref.shape[1] // len(spots)
+    for i, spot in enumerate(spots):
+        e_whole[:, i * size : (i + 1) * size] = e_ref[:, pl.ds(pl.multiple_of(spot() * size, size), size)].astype(F32)
     x = x_ref[...].astype(F32)
     center = x - jnp.mean(x, -1, keepdims=True)
     scale = lax.rsqrt(jnp.mean(center * center, -1, keepdims=True) + EPS)
     unit = center * scale
-    e = e_ref[...].astype(F32)
+    e = e_whole[...]
     rest = e - jnp.mean(e, -1, keepdims=True) - unit * jnp.mean(e * unit, -1, keepdims=True)
     o_ref[...] = g_ref[...].astype(F32) + scale * rest
 
 
-def input_grads(x, g, e):
+def input_grads(x, g, e, spots):
     rows, width = x.shape
     block = pl.BlockSpec((64, width), lambda i: (i, 0))
     return call(
-        end_kernel, (rows // 64,), [block] * 3, block, shape(rows, width, kind=F32), 15 * x.size, 10 * x.size, name="input_grads"
+        partial(end_kernel, spots),
+        (rows // 64,),
+        [block] * 3,
+        block,
+        shape(rows, width, kind=F32),
+        15 * x.size,
+        10 * x.size,
+        scratch=[pltpu.VMEM((64, width), F32)],
+        name="input_grads",
     )(x, g, e)
 
 
@@ -697,7 +891,7 @@
     contract_weight,
     output_bias,
 ):
-    square = lax.axis_size("fsdp") == 2 and lax.axis_size("ctx") == 4
+    square = (lax.axis_size("fsdp"), lax.axis_size("ctx"), lax.axis_size("tp")) == (2, 4, 4)
     links = SquareLinks() if square else AnyLinks()
     local_rows = attend_weight.shape[0]
     heads = attend_bias.shape[0]
@@ -705,20 +899,15 @@
     holder = lax.axis_index("ctx")
     prompt = PROMPT // holders
 
-    in_part = links.to_relative(stream_in)
-    rows_in = lax.all_gather(in_part, "tp", axis=0, tiled=True)
-    grad_part = links.to_relative(stream_grad)
-    grad_late, rows_in = lax.optimization_barrier((grad_part, rows_in))
-    rows_grad = lax.all_gather(grad_late, "tp", axis=0, tiled=True)
+    rows_in, attend_all, expand_all, output_all = links.collect(
+        stream_in, [attend_weight.reshape(local_rows, -1), expand_weight, output_weight]
+    )
     row_count = rows_in.shape[0]
-
-    attend_all = links.gather(attend_weight.reshape(local_rows, -1))
-    expand_all = links.gather(expand_weight)
-    contract_all = links.gather(contract_weight)
-    output_all = links.gather(output_weight)
+    rows_grad = lax.all_gather(links.to_relative(after(stream_grad, rows_in)), "tp", axis=0, tiled=True)
+    contract_all = links.gather(after(contract_weight, rows_in))
 
     gains = jnp.concatenate([jnp.stack([first_gain, first_shift, second_gain, second_shift]), jnp.zeros((4, first_gain.shape[0]), F32)])
-    gains = links.to_relative(gains)
+    own_gains = links.to_relative(gains)
     row_pos = lax.dynamic_slice_in_dim(positions, holder * row_count, row_count)
     row_seg = lax.dynamic_slice_in_dim(segments, holder * row_count, row_count)
     starts = positions.reshape(holders, row_count)[:, 0]
@@ -726,7 +915,7 @@
     bias = jnp.repeat(bias, prompt)
     table = turn_table(row_pos)
 
-    first_norm, second_norm, stat = norms(rows_in, gains)
+    first_norm, second_norm, rows_in, stat = norms(rows_in, gains, links.places())
     queries, pairs = project(first_norm, attend_all, attend_bias.reshape(-1), table, heads)
     pairs_far = links.gather_others(pairs[:prompt])
     activated, slope = expand(after(second_norm, pairs), expand_all, expand_bias)
@@ -735,20 +924,21 @@
     branches = lax.psum_scatter(mixed, "tp", scatter_dimension=0, tiled=True)
 
     rows_grad = after(rows_grad, mixed)
-    grad_attended, grad_pre, expand_sums = branch_grads(rows_grad, output_all, contract_all, slope)
+    grad_attended = attended_grads(rows_grad, output_all)
     grad_queries, pair_own, pair_near, pair_far = attend_back(
         queries, grad_attended, attended, row_sums, pairs, pairs_far, bias, row_seg, prompt, table
     )
     core_part, y_part = links.scatter_others(pair_near, pair_far)
     far_c = links.scatter_far(rows_grad, after(activated, pair_own))
-    y_part = y_part(pair_own)
-    near_c = links.scatter_near(rows_grad, activated, far_c)
-    far_e = links.scatter_far(second_norm, after(grad_pre, near_c[0]))
+    y_part = y_part(pair_own if far_c is None else far_c)
+    grad_pre, expand_sums = hidden_grads(after(rows_grad, y_part), contract_all, slope)
+    near_c = links.scatter_near(rows_grad, after(activated, grad_pre), far_c)
     grad_flat, attend_sums = pack(grad_queries, after(pair_own, near_c[0]), y_part, core_part, table, prompt)
-    grad_unit, vector_parts = unit_grads(grad_flat, grad_pre, attend_all, expand_all, rows_in, stat, gains)
+    grad_unit, vector_parts = unit_grads(grad_flat, grad_pre, attend_all, expand_all, rows_in, stat, own_gains)
     unit_part = lax.psum_scatter(grad_unit, "tp", scatter_dimension=0, tiled=True)
 
-    near_e = links.scatter_near(after(second_norm, grad_unit), grad_pre, far_e)
+    far_e = links.scatter_far(second_norm, after(grad_pre, grad_unit))
+    near_e = links.scatter_near(second_norm, grad_pre, far_e)
     far_a = links.scatter_far(first_norm, after(grad_flat, near_e[0]))
     far_o = links.scatter_far(rows_grad, after(attended, near_e[0]))
     near_a = links.scatter_near(first_norm, grad_flat, far_a)
@@ -761,13 +951,12 @@
     bias_sums = links.sum_rows(jnp.concatenate([attend_sums[0], expand_sums[0]]))
     attend_bias_grad = bias_sums[: grad_flat.shape[1]].reshape(attend_bias.shape)
     expand_bias_grad = bias_sums[grad_flat.shape[1] :]
-    row_sum = jnp.sum(grad_part.astype(F32), 0)
-    vectors = jnp.concatenate([vector_parts[:4], row_sum[None], jnp.zeros((3, row_sum.shape[0]), F32)])
-    norm_sums = sum_tp(links.sum_rows(links.to_whole(vectors)))
-
-    stream_out = links.to_whole((in_part.astype(F32) + branches.astype(F32))) + output_bias
-    stream_out = stream_out.astype(BF16)
-    input_grad = links.to_whole(input_grads(in_part, grad_part, unit_part))
+    row_sum = jnp.sum(stream_grad.astype(F32), 0)
+    vectors = jnp.concatenate([links.to_whole(vector_parts)[:4], row_sum[None]])
+    norm_sums = sum_tp(links.sum_rows(vectors))
+
+    stream_out = output_rows(stream_in, branches, output_bias, links.spots())
+    input_grad = input_grads(stream_in, stream_grad, unit_part, links.spots())
     return (
         stream_out,
         input_grad,

time: 523 us -> 563 us (1.076)
  Pallas kernels: 197 us -> 297 us
  local copies, waits for them, and re-layouts: 74.7 us -> 53.9 us
  waiting for transfers between devices: 157 us -> 140 us
  starting transfers between devices: 48.8 us -> 31.9 us
    pallas_call x3 -> x6, Pallas kernels: 28.8 us -> 129 us  [the longest x1 97 us: collect(): pl.pallas_call(partial(collect_kernel, n), in_specs=[ref] * (n + 1), out_...]
    ppermute x18 -> x12, waiting for transfers between devices: 47.2 us -> 32.3 us  [x_hop(): return lax.ppermute(v, 'fsdp', [(0, 1), (1, 0)])]
    concatenate x4 -> x1, local copies, waits for them, and re-layouts: 15.9 us -> 5.15 us  [gather(): return jnp.concatenate([near, self.core_hop(near)], 0)]
    unnamed x100 -> x98, local copies, waits for them, and re-layouts: 37.6 us -> 28.1 us
    ppermute x20 -> x14, waiting for transfers between devices: 98.4 us -> 89.2 us  [y_hop(): return lax.ppermute(v, 'ctx', [(0, 2), (2, 0), (1, 3), (3, 1)])]
    ppermute x20 -> x14, starting transfers between devices: 24 us -> 15.9 us  [y_hop(): return lax.ppermute(v, 'ctx', [(0, 2), (2, 0), (1, 3), (3, 1)])]
    ppermute x18 -> x12, starting transfers between devices: 18.4 us -> 10.4 us  [x_hop(): return lax.ppermute(v, 'fsdp', [(0, 1), (1, 0)])]
    ppermute x12 -> x9, waiting for transfers between devices: 10.5 us -> 16.1 us  [core_hop(): return lax.ppermute(v, 'ctx', [(0, 1), (1, 0), (2, 3), (3, 2)])]
  transfers between devices with their start and end apart: 56 -> 40, of which waited for: 24 -> 20; matrix products, arithmetic and copies ran while one was open for 15% -> 9% of each run, Pallas kernels for 38% -> 29%
where the time goes in v3:
time: 563 us; the launch traced here: 558 us
  Pallas kernels  297 us (53%)
  waiting for transfers between devices  140 us (25%)
  local copies, waits for them, and re-layouts  53.9 us (10%)
  starting transfers between devices  31.9 us (6%)
  other arithmetic  19.5 us (3%)
  between operations  14.7 us (3%)
    pallas_call x1, Pallas kernels, collect(): pl.pallas_call(partial(collect_kernel, n), in_specs=[ref] * (n + 1), out_...  97 us
    ppermute x14, waiting for transfers between devices, y_hop(): return lax.ppermute(v, 'ctx', [(0, 2), (2, 0), (1, 3), (3, 1)])  89.2 us
    ppermute x12, waiting for transfers between devices, x_hop(): return lax.ppermute(v, 'fsdp', [(0, 1), (1, 0)])  32.3 us
    unnamed x98, local copies, waits for them, and re-layouts  28.1 us
    pallas_call x4, Pallas kernels, far_product(): call(far_kernel, (cols // tile,), [pl.BlockSpec((tokens, half), lambda j:...  27.7 us
    pallas_call x4, Pallas kernels, near_product(): call(near_kernel, (cols // tile,), [pl.BlockSpec((tokens, half), lambda j...  27.1 us
    pallas_call x1, Pallas kernels, attend_back(): call(partial(attend_back_kernel, prompt), (heads, rows // tq), [row, row,...  23 us
    pallas_call x1, Pallas kernels, unit_grads(): call(unit_grad_kernel, (width // tile,), [pl.BlockSpec((rows, deep), lamb...  22.2 us
  transfers between devices with their start and end apart: 40, of which 20 were waited for; matrix products, arithmetic and copies ran while one was open for 9% of the time, Pallas kernels for 29%

profile of v3, /device:TPU:0, one launch (start us, length us, event | category | flops | bytes accessed | tf_op | source)
XLA Modules:
  0.0 557.9 jit_solution(9330284015675138839)
XLA Ops:
  7.2 2.2 copy.29
  9.4 97.0 %collect.1 = (bf16[1024,2048]{1,0:T(8,128)(2,1)}, bf16[2048,1536]{1,0:T(8,128)(2,1)}, bf16[2048,2048]{1,0:T(8,128)(2,1)}, bf16[2048,512]{1,0:T(8,128)(2,1)}) custom-call(bf16[256,2048]{1,0:T(8,128)(2,1)} %x_ref.6, bf16[256,1536]{1,0:T(8,128)(2,1)} %bitcast.17, bf16[256,2048]{1,0:T(8,128)(2,1)} %refs_1_.1, bf16[256,512]{1,0:T(8,128)(2,1)} %refs_2_.1), custom_call_target="tpu_custom_call" | custom-call | bytes 209715200 | tf_op jit(solution)/shard_map/collect/pallas_call | solution.py:675
  106.4 3.0 collective-permute-start.3
  112.4 1.9 multiply_sine_fusion
  116.8 5.0 concatenate.50.table_ref
  121.8 9.3 %norms.1 = (bf16[1024,2048]{1,0:T(8,128)(2,1)S(1)}, bf16[1024,2048]{1,0:T(8,128)(2,1)}, bf16[1024,2048]{1,0:T(8,128)(2,1)}, f32[1024,128]{1,0:T(8,128)S(1)}) custom-call(bf16[1024,2048]{1,0:T(8,128)(2,1)} %get-tuple-element.67.x_ref, f32[8,2048]{1,0:T(8,128)S(1)} %concatenate.49.gain_ref.x_ref), custom_call_target="tpu_custom_call" | custom-call | flops 20971520 | bytes 16777216 | tf_op jit(solution)/shard_map/norms/pallas_call | solution.py:101
  131.1 3.6 constant_dynamic-update-slice_fusion.6
  138.5 2.8 constant_dynamic-update-slice_fusion.5
  141.3 3.0 constant_dynamic-update-slice_fusion.4
  144.3 4.6 collective-permute-done.4
  151.4 10.4 %project.1 = (bf16[1024,512]{1,0:T(8,128)(2,1)S(1)}, bf16[1024,1024]{1,0:T(8,128)(2,1)S(1)}) custom-call(bf16[1024,2048]{1,0:T(8,128)(2,1)} %copy-done.24, bf16[2048,1536]{1,0:T(8,128)(2,1)} %get-tuple-element.69.w_ref.wa_ref, f32[8,1536]{1,0:T(8,128)S(1)} %broadcast_in_dim.38.b_ref, f32[1024,384]{1,0:T(8,128)S(1)} %copy-done.2), custom_call_target="tpu_custom_call" | custom-call | flops 6442450944 | bytes 13631488 | tf_op jit(solution)/shard_map/project/pallas_call | solution.py:127
  162.7 24.9 %collective-permute-done = bf16[512,1024]{1,0:T(8,128)(2,1)S(1)} collective-permute-done((bf16[512,1024]{1,0:T(8,128)(2,1)S(1)}, bf16[512,1024]{1,0:T(8,128)(2,1)S(1)}, u32[]{:S(2)}, u32[]{:S(2)}) %collective-permute-start) | collective-permute-done | bytes 1048608 | tf_op jit(solution)/shard_map/ppermute | solution.py:698
  189.2 16.7 %expand.1 = (bf16[1024,2048]{1,0:T(8,128)(2,1)S(1)}, bf16[1024,2048]{1,0:T(8,128)(2,1)}) custom-call(bf16[1024,2048]{1,0:T(8,128)(2,1)} %get-tuple-element.73.n_ref.a_ref, bf16[2048,2048]{1,0:T(8,128)(2,1)} %get-tuple-element.74.w_ref.we_ref, f32[8,2048]{1,0:T(8,128)S(1)} %broadcast_in_dim.41.b_ref), custom_call_target="tpu_custom_call" | custom-call | flops 8589934592 | bytes 20971520 | tf_op jit(solution)/shard_map/expand/pallas_call | solution.py:157
  205.8 2.0 copy-done.31
  208.8 2.7 compare_select_fusion
  215.3 16.4 %attend.1 = (bf16[1024,512]{1,0:T(8,128)(2,1)S(1)}, f32[2,8,1024]{2,1,0:T(8,128)S(1)}) custom-call(bf16[1024,512]{1,0:T(8,128)(2,1)S(1)} %get-tuple-element.76.q_ref, bf16[1024,1024]{1,0:T(8,128)(2,1)S(1)} %copy-done.23, bf16[1024,1024]{1,0:T(8,128)(2,1)S(1)} %copy-done.23, bf16[1536,1024]{1,0:T(8,128)(2,1)} %copy-done.35, bf16[1536,1024]{1,0:T(8,128)(2,1)} %copy-done.35, ...), custom_call_target="tpu_custom_call" | custom-call | flops 5368709120 | bytes 7340032 | tf_op jit(solution)/shard_map/attend/pallas_call | solution.py:215
  231.7 5.2 constant_dynamic-update-slice_fusion.7.wh_ref.w_ref
  236.9 15.7 %mixed_sum.1 = bf16[1024,2048]{1,0:T(8,128)(2,1)} custom-call(bf16[1024,512]{1,0:T(8,128)(2,1)S(1)} %get-tuple-element.110.a_ref.o_ref.b_ref, bf16[1024,2048]{1,0:T(8,128)(2,1)} %copy-done.31, bf16[2048,512]{1,0:T(8,128)(2,1)S(1)} %copy-done.26, bf16[2048,2048]{1,0:T(8,128)(2,1)} %constant_dynamic-update-slice_fusion.7.wh_ref.w_ref), custom_call_target="tpu_custom_call" | custom-call | flops 10737418240 | bytes 19922944 | tf_op jit(solution)/shard_map/mixed_sum/pallas_call | solution.py:368
  254.2 4.9 attended_grads.1.do_ref
  259.4 23.0 %attend_back.1 = (bf16[1024,512]{1,0:T(8,128)(2,1)S(1)}, f32[1024,1024]{1,0:T(8,128)}, bf16[512,1024]{1,0:T(8,128)(2,1)S(1)}, bf16[1024,1024]{1,0:T(8,128)(2,1)}) custom-call(bf16[1024,512]{1,0:T(8,128)(2,1)S(1)} %copy-done.33, bf16[1024,512]{1,0:T(8,128)(2,1)S(1)} %attended_grads.1.do_ref, bf16[1024,512]{1,0:T(8,128)(2,1)} %copy-done.4, ...), custom_call_target="tpu_custom_call" | custom-call | flops 13421772800 | bytes 18874368 | tf_op jit(solution)/shard_map/attend_back/pallas_call | solution.py:313
  282.4 8.5 %far_product.4 = bf16[1024,2048]{1,0:T(8,128)(2,1)} custom-call(bf16[1024,2048]{1,0:T(8,128)(2,1)} %all-gather.2.cloned.1.call-done.g_ref.a_ref, bf16[1024,2048]{1,0:T(8,128)(2,1)} %copy-done.31), custom_call_target="tpu_custom_call" | custom-call | flops 4294967296 | bytes 10485760 | tf_op jit(solution)/shard_map/far_product/pallas_call | solution.py:522
  291.5 10.0 %collective-permute-done.7.far_ref = bf16[1024,1024]{1,0:T(8,128)(2,1)} collective-permute-done((bf16[1024,1024]{1,0:T(8,128)(2,1)}, bf16[1024,1024]{1,0:T(8,128)(2,1)}, u32[]{:S(2)}, u32[]{:S(2)}) %collective-permute-start.7) | collective-permute-done | bytes 2097184 | tf_op jit(solution)/shard_map/ppermute | solution.py:701
  303.7 24.8 %collective-permute-done.9.near_ref = bf16[512,1024]{1,0:T(8,128)(2,1)S(1)} collective-permute-done((bf16[512,1024]{1,0:T(8,128)(2,1)S(1)}, bf16[512,1024]{1,0:T(8,128)(2,1)S(1)}, u32[]{:S(2)}, u32[]{:S(2)}) %collective-permute-start.9) | collective-permute-done | bytes 1048608 | tf_op jit(solution)/shard_map/ppermute | solution.py:698
  328.4 13.6 %hidden_grads.1 = (bf16[1024,2048]{1,0:T(8,128)(2,1)S(1)}, f32[8,2048]{1,0:T(8,128)S(1)}) custom-call(bf16[1024,2048]{1,0:T(8,128)(2,1)} %all-gather.2.cloned.1.call-done.g_ref.a_ref, bf16[2048,2048]{1,0:T(8,128)(2,1)} %constant_dynamic-update-slice_fusion.7.wh_ref.w_ref, bf16[1024,2048]{1,0:T(8,128)(2,1)} %get-tuple-element.90.d_ref), custom_call_target="tpu_custom_call" | custom-call | flops 8589934592 | bytes 20971520 | tf_op jit(solution)/shard_map/hidden_grads/pallas_call | solution.py:420
  342.0 9.6 %near_product.4 = (f32[256,2048]{1,0:T(8,128)S(1)}, bf16[256,2048]{1,0:T(8,128)(2,1)S(1)}, bf16[256,2048]{1,0:T(8,128)(2,1)S(1)}, bf16[256,2048]{1,0:T(8,128)(2,1)S(1)}) custom-call(bf16[1024,2048]{1,0:T(8,128)(2,1)} %all-gather.2.cloned.1.call-done.g_ref.a_ref, bf16[1024,2048]{1,0:T(8,128)(2,1)} %copy-done.31, bf16[1024,2048]{1,0:T(8,128)(2,1)} %collective-permute-done.8.r_ref), custom_call_target="tpu_custom_call" | custom-call | flops 4294967296 | bytes 14680064 | tf_op jit(solution)/shard_map/near_product/pallas_call | solution.py:547
  353.9 7.8 %pack.1 = (bf16[1024,1536]{1,0:T(8,128)(2,1)}, f32[8,1536]{1,0:T(8,128)S(1)}) custom-call(bf16[1024,512]{1,0:T(8,128)(2,1)S(1)} %get-tuple-element.83.q_ref, f32[1024,1024]{1,0:T(8,128)} %get-tuple-element.94.own_ref, bf16[512,1024]{1,0:T(8,128)(2,1)S(1)} %collective-permute-done.9.near_ref, bf16[1024,1024]{1,0:T(8,128)(2,1)} %collective-permute-done.7.far_ref, ...), custom_call_target="tpu_custom_call" | custom-call | flops 5242880 | bytes 8388608 | tf_op jit(solution)/shard_map/pack/pallas_call | solution.py:455
  361.7 1.9 copy-done.25
  363.6 22.2 %unit_grads.1 = (bf16[1024,2048]{1,0:T(8,128)(2,1)}, f32[8,2048]{1,0:T(8,128)S(1)}) custom-call(bf16[1024,1536]{1,0:T(8,128)(2,1)S(1)} %copy-done.25, bf16[1024,2048]{1,0:T(8,128)(2,1)} %copy-done.30, bf16[2048,1536]{1,0:T(8,128)(2,1)} %get-tuple-element.69.w_ref.wa_ref, bf16[2048,2048]{1,0:T(8,128)(2,1)} %get-tuple-element.74.w_ref.we_ref, ...), custom_call_target="tpu_custom_call" | custom-call | flops 15032385536 | bytes 30408704 | tf_op jit(solution)/shard_map/unit_grads/pallas_call | solution.py:493
  385.8 8.6 %far_product.5 = bf16[1024,2048]{1,0:T(8,128)(2,1)} custom-call(bf16[1024,2048]{1,0:T(8,128)(2,1)} %get-tuple-element.73.n_ref.a_ref, bf16[1024,2048]{1,0:T(8,128)(2,1)} %copy-done.30), custom_call_target="tpu_custom_call" | custom-call | flops 4294967296 | bytes 10485760 | tf_op jit(solution)/shard_map/far_product/pallas_call | solution.py:522
  395.2 6.1 %collective-permute-done.10 = f32[5,2048]{1,0:T(8,128)S(1)} collective-permute-done((f32[5,2048]{1,0:T(8,128)S(1)}, f32[5,2048]{1,0:T(8,128)S(1)}, u32[]{:S(2)}, u32[]{:S(2)}) %collective-permute-start.10) | collective-permute-done | bytes 40992 | tf_op jit(solution)/shard_map/ppermute | solution.py:701
  406.6 12.8 %collective-permute-done.12 = f32[5,2048]{1,0:T(8,128)S(1)} collective-permute-done((f32[5,2048]{1,0:T(8,128)S(1)}, f32[5,2048]{1,0:T(8,128)S(1)}, u32[]{:S(2)}, u32[]{:S(2)}) %collective-permute-start.12) | collective-permute-done | bytes 40992 | tf_op jit(solution)/shard_map/ppermute | solution.py:698
  421.1 2.7 collective-permute-done.13
  423.8 2.6 collective-permute-start.14
  427.1 3.3 collective-permute-done.22
  431.7 2.4 collective-permute-done.23
  437.1 9.0 %collective-permute-done.35 = bf16[128,2048]{1,0:T(8,128)(2,1)} collective-permute-done((bf16[128,2048]{1,0:T(8,128)(2,1)}, bf16[128,2048]{1,0:T(8,128)(2,1)}, u32[]{:S(2)}, u32[]{:S(2)}) %collective-permute-start.35) | collective-permute-done | bytes 524320 | tf_op jit(solution)/shard_map/ppermute | solution.py:695
  448.9 8.0 %near_product.5 = (f32[256,2048]{1,0:T(8,128)S(1)}, bf16[256,2048]{1,0:T(8,128)(2,1)S(1)}, bf16[256,2048]{1,0:T(8,128)(2,1)S(1)}, bf16[256,2048]{1,0:T(8,128)(2,1)S(1)}) custom-call(bf16[1024,2048]{1,0:T(8,128)(2,1)} %get-tuple-element.73.n_ref.a_ref, bf16[1024,2048]{1,0:T(8,128)(2,1)} %copy-done.30, bf16[1024,2048]{1,0:T(8,128)(2,1)} %collective-permute-done.15.r_ref), custom_call_target="tpu_custom_call" | custom-call | flops 4294967296 | bytes 14680064 | tf_op jit(solution)/shard_map/near_product/pallas_call | solution.py:547
  459.2 7.6 %far_product.6 = bf16[1024,1536]{1,0:T(8,128)(2,1)} custom-call(bf16[1024,2048]{1,0:T(8,128)(2,1)} %copy-done.24, bf16[1024,1536]{1,0:T(8,128)(2,1)} %get-tuple-element.102.gp_ref.b_ref), custom_call_target="tpu_custom_call" | custom-call | flops 3221225472 | bytes 8388608 | tf_op jit(solution)/shard_map/far_product/pallas_call | solution.py:522
  474.9 2.9 far_product.7
  477.8 5.5 collective-permute-done.29
  485.1 3.8 collective-permute-done.31
  490.6 6.6 %near_product.6 = (f32[256,1536]{1,0:T(8,128)S(1)}, bf16[256,1536]{1,0:T(8,128)(2,1)S(1)}, bf16[256,1536]{1,0:T(8,128)(2,1)S(1)}, bf16[256,1536]{1,0:T(8,128)(2,1)S(1)}) custom-call(bf16[1024,2048]{1,0:T(8,128)(2,1)} %copy-done.24, bf16[1024,1536]{1,0:T(8,128)(2,1)} %get-tuple-element.102.gp_ref.b_ref, bf16[1024,1536]{1,0:T(8,128)(2,1)} %collective-permute-done.16.r_ref), custom_call_target="tpu_custom_call" | custom-call | flops 3221225472 | bytes 11534336 | tf_op jit(solution)/shard_map/near_product/pallas_call | solution.py:547
  498.4 2.9 near_product.7
  504.0 14.1 %collective-permute-done.25 = bf16[128,512]{1,0:T(8,128)(2,1)S(1)} collective-permute-done((bf16[128,512]{1,0:T(8,128)(2,1)S(1)}, bf16[128,512]{1,0:T(8,128)(2,1)S(1)}, u32[]{:S(2)}, u32[]{:S(2)}) %collective-permute-start.25) | collective-permute-done | bytes 131104 | tf_op jit(solution)/shard_map/ppermute | solution.py:698
  520.3 4.0 collective-permute-done.17
  535.7 2.8 input_grads.1
  538.5 8.7 %collective-permute-done.18 = bf16[256,1536]{1,0:T(8,128)(2,1)S(1)} collective-permute-done((bf16[256,1536]{1,0:T(8,128)(2,1)}, bf16[256,1536]{1,0:T(8,128)(2,1)S(1)}, u32[]{:S(2)}, u32[]{:S(2)}) %collective-permute-start.18) | collective-permute-done | bytes 786464 | tf_op jit(solution)/shard_map/ppermute | solution.py:695
  549.0 2.2 reshape.56
  (236 shorter events, 74.0 us)
Async XLA Ops:
  7.2 103.8 %copy-start.1 = (bf16[256,2048]{1,0:T(8,128)(2,1)S(1)}, bf16[256,2048]{1,0:T(8,128)(2,1)}, u32[]{:S(2)}) copy-start(bf16[256,2048]{1,0:T(8,128)(2,1)} %g_ref.1) | copy-start | bytes 3145732
  7.2 245.4 %all-gather.2.cloned.1.call-start = ((), (), s32[]{:S(2)}) async-start(), calls=%async_computation.3 | async-start | bytes 5242880 | tf_op jit(solution)/shard_map/all_gather | solution.py:906
  9.4 102.8 %copy-start.45 = (f32[2,768]{1,0:T(2,128)S(1)}, f32[2,768]{1,0:T(2,128)}, u32[]{:S(2)}) copy-start(f32[2,768]{1,0:T(2,128)} %param.24) | copy-start | bytes 18436
  9.4 102.8 %copy-start.39 = (f32[2048]{0:T(1024)S(1)}, f32[2048]{0:T(1024)}, u32[]{:S(2)}) copy-start(f32[2048]{0:T(1024)} %param.19) | copy-start | bytes 24580
  9.4 102.8 %copy-start.40 = (f32[2048]{0:T(1024)S(1)}, f32[2048]{0:T(1024)}, u32[]{:S(2)}) copy-start(f32[2048]{0:T(1024)} %param.20) | copy-start | bytes 24580
  9.4 102.8 %copy-start.41 = (f32[2048]{0:T(1024)S(1)}, f32[2048]{0:T(1024)}, u32[]{:S(2)}) copy-start(f32[2048]{0:T(1024)} %param.21) | copy-start | bytes 24580
  9.4 102.8 %copy-start.42 = (f32[2048]{0:T(1024)S(1)}, f32[2048]{0:T(1024)}, u32[]{:S(2)}) copy-start(f32[2048]{0:T(1024)} %param.22) | copy-start | bytes 24580
  9.4 102.9 %copy-start.38 = (s32[4096]{0:T(1024)S(1)}, s32[4096]{0:T(1024)}, u32[]{:S(2)}) copy-start(s32[4096]{0:T(1024)} %param.18) | copy-start | bytes 49156
  106.4 28.3 %collective-permute-start.3 = (bf16[256,2048]{1,0:T(8,128)(2,1)}, bf16[256,2048]{1,0:T(8,128)(2,1)}, u32[]{:S(2)}, u32[]{:S(2)}) collective-permute-start(bf16[256,2048]{1,0:T(8,128)(2,1)} %param.28), channel_id=1, source_target_pairs={{0,8},{8,0},{4,12},{12,4},{1,9},{9,1},{5,13},{13,5},{2,10},{10,2},... | collective-permute-start | bytes 3145736 | tf_op jit(solution)/shard_map/ppermute | solution.py:698
  109.5 26.9 %collective-permute-start.2 = (bf16[256,2048]{1,0:T(8,128)(2,1)}, bf16[256,2048]{1,0:T(8,128)(2,1)}, u32[]{:S(2)}, u32[]{:S(2)}) collective-permute-start(bf16[256,2048]{1,0:T(8,128)(2,1)} %param.28), channel_id=1, source_target_pairs={{0,16},{16,0},{1,17},{17,1},{2,18},{18,2},{3,19},{19,3},{4,20},{20... | collective-permute-start | bytes 3145736 | tf_op jit(solution)/shard_map/ppermute | solution.py:695
  112.1 358.9 %reduce-scatter.3.cloned.1.call-start = ((), (), s32[]{:S(2)}) async-start(), calls=%async_computation.2 | async-start | bytes 5242880 | tf_op jit(solution)/shard_map/reduce_scatter | solution.py:924
  135.8 13.1 %collective-permute-start.4 = (bf16[128,2048]{1,0:T(8,128)(2,1)S(1)}, bf16[128,2048]{1,0:T(8,128)(2,1)S(1)}, u32[]{:S(2)}, u32[]{:S(2)}) collective-permute-start(bf16[128,2048]{1,0:T(8,128)(2,1)S(1)} %slice.176), channel_id=1, source_target_pairs={{0,16},{16,0},{1,17},{17,1},{2,18},{18,2},{3,19},{19,3},{4,20},{20... | collective-permute-start | bytes 1572872 | tf_op jit(solution)/shard_map/ppermute | solution.py:695
  137.4 12.9 %collective-permute-start.5 = (bf16[128,2048]{1,0:T(8,128)(2,1)S(1)}, bf16[128,2048]{1,0:T(8,128)(2,1)S(1)}, u32[]{:S(2)}, u32[]{:S(2)}) collective-permute-start(bf16[128,2048]{1,0:T(8,128)(2,1)S(1)} %slice.177), channel_id=1, source_target_pairs={{0,8},{8,0},{4,12},{12,4},{1,9},{9,1},{5,13},{13,5},{2,10},{10,2},... | collective-permute-start | bytes 1572872 | tf_op jit(solution)/shard_map/ppermute | solution.py:698
  151.4 80.3 %collective-permute-start.6 = (bf16[1024,2048]{1,0:T(8,128)(2,1)}, bf16[1024,2048]{1,0:T(8,128)(2,1)}, u32[]{:S(2)}, u32[]{:S(2)}) collective-permute-start(bf16[1024,2048]{1,0:T(8,128)(2,1)} %get-tuple-element.147), channel_id=1, source_target_pairs={{0,4},{4,0},{8,12},{12,8},{1,5},{5,1},{9,13},{13,9},{2,6},{6,2},{1... | collective-permute-start | bytes 12582920 | tf_op jit(solution)/shard_map/ppermute | solution.py:701
  161.9 51.9 %copy-start.32 = (bf16[1024,512]{1,0:T(8,128)(2,1)}, bf16[1024,512]{1,0:T(8,128)(2,1)S(1)}, u32[]{:S(2)}) copy-start(bf16[1024,512]{1,0:T(8,128)(2,1)S(1)} %get-tuple-element.76.q_ref) | copy-start | bytes 3145732
  162.0 25.7 %collective-permute-start = (bf16[512,1024]{1,0:T(8,128)(2,1)S(1)}, bf16[512,1024]{1,0:T(8,128)(2,1)S(1)}, u32[]{:S(2)}, u32[]{:S(2)}) collective-permute-start(bf16[512,1024]{1,0:T(8,128)(2,1)S(1)} %slice.134), channel_id=1, source_target_pairs={{0,8},{8,0},{4,12},{12,4},{1,9},{9,1},{5,13},{13,5},{2,10},{10,2},... | collective-permute-start | bytes 3145736 | tf_op jit(solution)/shard_map/ppermute | solution.py:698
  189.1 22.6 %collective-permute-start.1 = (bf16[1024,1024]{1,0:T(8,128)(2,1)}, bf16[1024,1024]{1,0:T(8,128)(2,1)}, u32[]{:S(2)}, u32[]{:S(2)}) collective-permute-start(bf16[1024,1024]{1,0:T(8,128)(2,1)} %pad_maximum_fusion), channel_id=1, source_target_pairs={{0,4},{4,0},{8,12},{12,8},{1,5},{5,1},{9,13},{13,9},{2,6},{6,2},{1... | collective-permute-start | bytes 6291464 | tf_op jit(solution)/shard_map/ppermute | solution.py:701
  290.9 10.6 %collective-permute-start.8 = (bf16[1024,2048]{1,0:T(8,128)(2,1)}, bf16[1024,2048]{1,0:T(8,128)(2,1)}, u32[]{:S(2)}, u32[]{:S(2)}) collective-permute-start(bf16[1024,2048]{1,0:T(8,128)(2,1)} %far_product.4), channel_id=1, source_target_pairs={{0,4},{4,0},{8,12},{12,8},{1,5},{5,1},{9,13},{13,9},{2,6},{6,2},{1... | collective-permute-start | bytes 12582920 | tf_op jit(solution)/shard_map/ppermute | solution.py:701
  291.4 10.1 %collective-permute-start.7 = (bf16[1024,1024]{1,0:T(8,128)(2,1)}, bf16[1024,1024]{1,0:T(8,128)(2,1)}, u32[]{:S(2)}, u32[]{:S(2)}) collective-permute-start(bf16[1024,1024]{1,0:T(8,128)(2,1)} %get-tuple-element.85), channel_id=1, source_target_pairs={{0,4},{4,0},{8,12},{12,8},{1,5},{5,1},{9,13},{13,9},{2,6},{6,2},{1... | collective-permute-start | bytes 6291464 | tf_op jit(solution)/shard_map/ppermute | solution.py:701
  291.5 243.0 %reduce-scatter.5.cloned.1.call-start = ((), (), s32[]{:S(2)}) async-start(), calls=%async_computation.4 | async-start | bytes 5242880 | tf_op jit(solution)/shard_map/reduce_scatter | solution.py:938
  302.9 25.5 %collective-permute-start.9 = (bf16[512,1024]{1,0:T(8,128)(2,1)S(1)}, bf16[512,1024]{1,0:T(8,128)(2,1)S(1)}, u32[]{:S(2)}, u32[]{:S(2)}) collective-permute-start(bf16[512,1024]{1,0:T(8,128)(2,1)S(1)} %slice_add_fusion), channel_id=1, source_target_pairs={{0,8},{8,0},{4,12},{12,4},{1,9},{9,1},{5,13},{13,5},{2,10},{10,2},... | collective-permute-start | bytes 3145736 | tf_op jit(solution)/shard_map/ppermute | solution.py:698
  394.4 54.4 %collective-permute-start.15 = (bf16[1024,2048]{1,0:T(8,128)(2,1)}, bf16[1024,2048]{1,0:T(8,128)(2,1)}, u32[]{:S(2)}, u32[]{:S(2)}) collective-permute-start(bf16[1024,2048]{1,0:T(8,128)(2,1)} %far_product.5), channel_id=1, source_target_pairs={{0,4},{4,0},{8,12},{12,8},{1,5},{5,1},{9,13},{13,9},{2,6},{6,2},{1... | collective-permute-start | bytes 12582920 | tf_op jit(solution)/shard_map/ppermute | solution.py:701
  394.7 6.6 %collective-permute-start.10 = (f32[5,2048]{1,0:T(8,128)S(1)}, f32[5,2048]{1,0:T(8,128)S(1)}, u32[]{:S(2)}, u32[]{:S(2)}) collective-permute-start(f32[5,2048]{1,0:T(8,128)S(1)} %pad_maximum_fusion.9), channel_id=1, source_target_pairs={{0,4},{4,0},{8,12},{12,8},{1,5},{5,1},{9,13},{13,9},{2,6},{6,2},{1... | collective-permute-start | bytes 122888 | tf_op jit(solution)/shard_map/ppermute | solution.py:701
  401.3 4.4 collective-permute-start.11
  403.9 31.4 %collective-permute-start.33 = (bf16[128,2048]{1,0:T(8,128)(2,1)}, bf16[128,2048]{1,0:T(8,128)(2,1)}, u32[]{:S(2)}, u32[]{:S(2)}) collective-permute-start(bf16[128,2048]{1,0:T(8,128)(2,1)} %get-tuple-element.125), channel_id=1, source_target_pairs={{0,8},{8,0},{4,12},{12,4},{1,9},{9,1},{5,13},{13,5},{2,10},{10,2},... | collective-permute-start | bytes 1572872 | tf_op jit(solution)/shard_map/ppermute | solution.py:698
  405.8 13.7 %collective-permute-start.12 = (f32[5,2048]{1,0:T(8,128)S(1)}, f32[5,2048]{1,0:T(8,128)S(1)}, u32[]{:S(2)}, u32[]{:S(2)}) collective-permute-start(f32[5,2048]{1,0:T(8,128)S(1)} %add.98), channel_id=1, source_target_pairs={{0,8},{8,0},{4,12},{12,4},{1,9},{9,1},{5,13},{13,5},{2,10},{10,2},... | collective-permute-start | bytes 122888 | tf_op jit(solution)/shard_map/ppermute | solution.py:698
  419.5 4.3 collective-permute-start.13
  421.1 5.4 collective-permute-start.21
  423.8 11.5 %collective-permute-start.14 = (f32[5,2048]{1,0:T(8,128)S(1)}, f32[5,2048]{1,0:T(8,128)S(1)}, u32[]{:S(2)}, u32[]{:S(2)}) collective-permute-start(f32[5,2048]{1,0:T(8,128)S(1)} %add.100), channel_id=1, source_target_pairs={{0,2},{1,3},{2,0},{3,1},{4,6},{5,7},{6,4},{7,5},{8,10},{9,11},{10,... | collective-permute-start | bytes 122888 | tf_op jit(solution)/shard_map/ppermute | solution.py:821
  426.5 3.9 collective-permute-start.22
  430.3 3.7 collective-permute-start.23
  430.9 15.2 %collective-permute-start.35 = (bf16[128,2048]{1,0:T(8,128)(2,1)}, bf16[128,2048]{1,0:T(8,128)(2,1)}, u32[]{:S(2)}, u32[]{:S(2)}) collective-permute-start(bf16[128,2048]{1,0:T(8,128)(2,1)} %get-tuple-element.126), channel_id=1, source_target_pairs={{0,16},{16,0},{1,17},{17,1},{2,18},{18,2},{3,19},{19,3},{4,20},{20... | collective-permute-start | bytes 1572872 | tf_op jit(solution)/shard_map/ppermute | solution.py:695
  436.6 32.7 %collective-permute-start.34 = (bf16[256,2048]{1,0:T(8,128)(2,1)S(1)}, bf16[256,2048]{1,0:T(8,128)(2,1)S(1)}, u32[]{:S(2)}, u32[]{:S(2)}) collective-permute-start(bf16[256,2048]{1,0:T(8,128)(2,1)S(1)} %pad_maximum_fusion.3), channel_id=1, source_target_pairs={{0,16},{16,0},{1,17},{17,1},{2,18},{18,2},{3,19},{19,3},{4,20},{20... | collective-permute-start | bytes 3145736 | tf_op jit(solution)/shard_map/ppermute | solution.py:695
  447.4 21.9 %collective-permute-start.36 = (bf16[256,2048]{1,0:T(8,128)(2,1)S(1)}, bf16[256,2048]{1,0:T(8,128)(2,1)S(1)}, u32[]{:S(2)}, u32[]{:S(2)}) collective-permute-start(bf16[256,2048]{1,0:T(8,128)(2,1)S(1)} %pad_maximum_fusion.4), channel_id=1, source_target_pairs={{0,8},{8,0},{4,12},{12,4},{1,9},{9,1},{5,13},{13,5},{2,10},{10,2},... | collective-permute-start | bytes 3145736 | tf_op jit(solution)/shard_map/ppermute | solution.py:698
  466.9 23.7 %collective-permute-start.16 = (bf16[1024,1536]{1,0:T(8,128)(2,1)}, bf16[1024,1536]{1,0:T(8,128)(2,1)}, u32[]{:S(2)}, u32[]{:S(2)}) collective-permute-start(bf16[1024,1536]{1,0:T(8,128)(2,1)} %far_product.6), channel_id=1, source_target_pairs={{0,4},{4,0},{8,12},{12,8},{1,5},{5,1},{9,13},{13,9},{2,6},{6,2},{1... | collective-permute-start | bytes 9437192 | tf_op jit(solution)/shard_map/ppermute | solution.py:701
  468.7 14.6 %collective-permute-start.29 = (bf16[128,2048]{1,0:T(8,128)(2,1)}, bf16[128,2048]{1,0:T(8,128)(2,1)}, u32[]{:S(2)}, u32[]{:S(2)}) collective-permute-start(bf16[128,2048]{1,0:T(8,128)(2,1)} %get-tuple-element.131), channel_id=1, source_target_pairs={{0,8},{8,0},{4,12},{12,4},{1,9},{9,1},{5,13},{13,5},{2,10},{10,2},... | collective-permute-start | bytes 1572872 | tf_op jit(solution)/shard_map/ppermute | solution.py:698
  474.1 14.8 %collective-permute-start.31 = (bf16[128,2048]{1,0:T(8,128)(2,1)S(1)}, bf16[128,2048]{1,0:T(8,128)(2,1)S(1)}, u32[]{:S(2)}, u32[]{:S(2)}) collective-permute-start(bf16[128,2048]{1,0:T(8,128)(2,1)S(1)} %copy-done.34), channel_id=1, source_target_pairs={{0,16},{16,0},{1,17},{17,1},{2,18},{18,2},{3,19},{19,3},{4,20},{20... | collective-permute-start | bytes 1572872 | tf_op jit(solution)/shard_map/ppermute | solution.py:695
  477.7 20.7 %collective-permute-start.24 = (bf16[1024,512]{1,0:T(8,128)(2,1)S(1)}, bf16[1024,512]{1,0:T(8,128)(2,1)S(1)}, u32[]{:S(2)}, u32[]{:S(2)}) collective-permute-start(bf16[1024,512]{1,0:T(8,128)(2,1)S(1)} %far_product.7), channel_id=1, source_target_pairs={{0,4},{4,0},{8,12},{12,8},{1,5},{5,1},{9,13},{13,9},{2,6},{6,2},{1... | collective-permute-start | bytes 3145736 | tf_op jit(solution)/shard_map/ppermute | solution.py:701
  484.6 45.4 %collective-permute-start.30 = (bf16[256,2048]{1,0:T(8,128)(2,1)S(1)}, bf16[256,2048]{1,0:T(8,128)(2,1)S(1)}, u32[]{:S(2)}, u32[]{:S(2)}) collective-permute-start(bf16[256,2048]{1,0:T(8,128)(2,1)S(1)} %pad_maximum_fusion.1), channel_id=1, source_target_pairs={{0,16},{16,0},{1,17},{17,1},{2,18},{18,2},{3,19},{19,3},{4,20},{20... | collective-permute-start | bytes 3145736 | tf_op jit(solution)/shard_map/ppermute | solution.py:695
  489.1 42.2 %collective-permute-start.32 = (bf16[256,2048]{1,0:T(8,128)(2,1)S(1)}, bf16[256,2048]{1,0:T(8,128)(2,1)S(1)}, u32[]{:S(2)}, u32[]{:S(2)}) collective-permute-start(bf16[256,2048]{1,0:T(8,128)(2,1)S(1)} %pad_maximum_fusion.2), channel_id=1, source_target_pairs={{0,8},{8,0},{4,12},{12,4},{1,9},{9,1},{5,13},{13,5},{2,10},{10,2},... | collective-permute-start | bytes 3145736 | tf_op jit(solution)/shard_map/ppermute | solution.py:698
  501.3 16.8 %collective-permute-start.25 = (bf16[128,512]{1,0:T(8,128)(2,1)S(1)}, bf16[128,512]{1,0:T(8,128)(2,1)S(1)}, u32[]{:S(2)}, u32[]{:S(2)}) collective-permute-start(bf16[128,512]{1,0:T(8,128)(2,1)S(1)} %get-tuple-element.153), channel_id=1, source_target_pairs={{0,8},{8,0},{4,12},{12,4},{1,9},{9,1},{5,13},{13,5},{2,10},{10,2},... | collective-permute-start | bytes 393224 | tf_op jit(solution)/shard_map/ppermute | solution.py:698
  502.0 16.8 %collective-permute-start.27 = (bf16[128,512]{1,0:T(8,128)(2,1)S(1)}, bf16[128,512]{1,0:T(8,128)(2,1)S(1)}, u32[]{:S(2)}, u32[]{:S(2)}) collective-permute-start(bf16[128,512]{1,0:T(8,128)(2,1)S(1)} %get-tuple-element.154), channel_id=1, source_target_pairs={{0,16},{16,0},{1,17},{17,1},{2,18},{18,2},{3,19},{19,3},{4,20},{20... | collective-permute-start | bytes 393224 | tf_op jit(solution)/shard_map/ppermute | solution.py:695
  502.7 21.6 %collective-permute-start.17 = (bf16[128,1536]{1,0:T(8,128)(2,1)S(1)}, bf16[128,1536]{1,0:T(8,128)(2,1)S(1)}, u32[]{:S(2)}, u32[]{:S(2)}) collective-permute-start(bf16[128,1536]{1,0:T(8,128)(2,1)S(1)} %get-tuple-element.143), channel_id=1, source_target_pairs={{0,8},{8,0},{4,12},{12,4},{1,9},{9,1},{5,13},{13,5},{2,10},{10,2},... | collective-permute-start | bytes 1179656 | tf_op jit(solution)/shard_map/ppermute | solution.py:698
  518.1 9.9 %collective-permute-start.19 = (bf16[128,1536]{1,0:T(8,128)(2,1)S(1)}, bf16[128,1536]{1,0:T(8,128)(2,1)S(1)}, u32[]{:S(2)}, u32[]{:S(2)}) collective-permute-start(bf16[128,1536]{1,0:T(8,128)(2,1)S(1)} %get-tuple-element.144), channel_id=1, source_target_pairs={{0,16},{16,0},{1,17},{17,1},{2,18},{18,2},{3,19},{19,3},{4,20},{20... | collective-permute-start | bytes 1179656 | tf_op jit(solution)/shard_map/ppermute | solution.py:695
  518.8 14.7 %collective-permute-start.26 = (bf16[256,512]{1,0:T(8,128)(2,1)S(1)}, bf16[256,512]{1,0:T(8,128)(2,1)S(1)}, u32[]{:S(2)}, u32[]{:S(2)}) collective-permute-start(bf16[256,512]{1,0:T(8,128)(2,1)S(1)} %pad_maximum_fusion.7), channel_id=1, source_target_pairs={{0,16},{16,0},{1,17},{17,1},{2,18},{18,2},{3,19},{19,3},{4,20},{20... | collective-permute-start | bytes 786440 | tf_op jit(solution)/shard_map/ppermute | solution.py:695
  524.3 9.3 %collective-permute-start.28 = (bf16[256,512]{1,0:T(8,128)(2,1)S(1)}, bf16[256,512]{1,0:T(8,128)(2,1)S(1)}, u32[]{:S(2)}, u32[]{:S(2)}) collective-permute-start(bf16[256,512]{1,0:T(8,128)(2,1)S(1)} %pad_maximum_fusion.8), channel_id=1, source_target_pairs={{0,8},{8,0},{4,12},{12,4},{1,9},{9,1},{5,13},{13,5},{2,10},{10,2},... | collective-permute-start | bytes 786440 | tf_op jit(solution)/shard_map/ppermute | solution.py:698
  527.9 19.3 %collective-permute-start.18 = (bf16[256,1536]{1,0:T(8,128)(2,1)}, bf16[256,1536]{1,0:T(8,128)(2,1)S(1)}, u32[]{:S(2)}, u32[]{:S(2)}) collective-permute-start(bf16[256,1536]{1,0:T(8,128)(2,1)} %pad_maximum_fusion.5), channel_id=1, source_target_pairs={{0,16},{16,0},{1,17},{17,1},{2,18},{18,2},{3,19},{19,3},{4,20},{20... | collective-permute-start | bytes 2359304 | tf_op jit(solution)/shard_map/ppermute | solution.py:695
  529.9 17.7 %collective-permute-start.20 = (bf16[256,1536]{1,0:T(8,128)(2,1)}, bf16[256,1536]{1,0:T(8,128)(2,1)}, u32[]{:S(2)}, u32[]{:S(2)}) collective-permute-start(bf16[256,1536]{1,0:T(8,128)(2,1)} %pad_maximum_fusion.6), channel_id=1, source_target_pairs={{0,8},{8,0},{4,12},{12,4},{1,9},{9,1},{5,13},{13,5},{2,10},{10,2},... | collective-permute-start | bytes 2359304 | tf_op jit(solution)/shard_map/ppermute | solution.py:698
  (39 other events, 292.9 us)
Sparse Core Ops, SparseCore 0:
  112.3 80.1 all-gather.1
  291.6 77.2 reduce-scatter.2
  431.8 75.9 reduce-scatter.4

commit v4 on v3

--- a/solution.py
+++ b/solution.py
@@ -562,7 +562,7 @@
 
 class Hops:
     def __init__(self, send, recv):
-        self.send, self.recv, self.count = send, recv, 0
+        self.send, self.recv, self.made = send, recv, []
         f, c, t = (lax.axis_index(a) for a in ("fsdp", "ctx", "tp"))
         ring = lax.axis_size("tp")
         self.to = {
@@ -581,111 +581,343 @@
         pl.semaphore_wait(barrier, len(near))
 
     def copy(self, way, src, dst):
-        made = pltpu.make_async_remote_copy(
-            src, dst, self.send.at[self.count], self.recv.at[self.count],
-            device_id=self.to[way], device_id_type=pl.DeviceIdType.MESH,
+        i = len(self.made)
+        self.made.append(
+            pltpu.make_async_remote_copy(
+                src,
+                dst,
+                self.send.at[i],
+                self.recv.at[i],
+                device_id=self.to[way],
+                device_id_type=pl.DeviceIdType.MESH,
+            )
         )
-        self.count += 1
-        made.start()
-        return made
-
-
-def collect_kernel(n, x_ref, *refs):
-    parts, rows_ref, wholes = refs[:n], refs[n], refs[n + 1 : 2 * n + 1]
-    send, recv, local = refs[2 * n + 1 :]
+        return self.made[-1]
+
+    def end(self):
+        for copy in self.made:
+            copy.wait_send()
+
+
+class Block:
+    def __init__(self, hops, part, whole, halves=1):
+        size = part.shape[0]
+        half, piece = size // 2, size // halves
+
+        def at(slot, start=0, rows=size):
+            return whole.at[pl.ds(slot * size + start, rows)]
+
+        self.first = [
+            [
+                hops.copy(way, part.at[pl.ds(i * piece, piece)], at(slot, i * piece, piece))
+                for way, slot in (("x", 1), ("y", 2))
+            ]
+            for i in range(halves)
+        ]
+        self.corner = [
+            hops.copy("x", at(2, 0, half), at(3, 0, half)),
+            hops.copy("y", at(1, half, half), at(3, half, half)),
+        ]
+        self.core = [hops.copy("core", part if slot == 0 else at(slot), at(4 + slot)) for slot in range(4)]
+
+
+def start(copies):
+    for copy in copies:
+        copy.start()
+
+
+def arrive(copies):
+    for copy in copies:
+        copy.wait_recv()
+
+
+def table_kernel(pos_ref, freq_ref, o_ref):
+    angle = pos_ref[...] * freq_ref[:1]
+    c, s = jnp.cos(angle), jnp.sin(angle)
+    lane = lax.broadcasted_iota(jnp.int32, angle.shape, 1)
+    half = ROT // 2
+    o_ref[:, :128] = jnp.where(lane < ROT, c, 1.0)
+    o_ref[:, 128:256] = jnp.where(lane < half, -s, 0.0)
+    o_ref[:, 256:] = jnp.where((lane >= half) & (lane < ROT), s, 0.0)
+
+
+def norm_block_kernel(x_ref, gain_ref, first_ref, second_ref, stat_ref):
+    x = x_ref[...].astype(F32)
+    mean = jnp.mean(x, -1, keepdims=True)
+    center = x - mean
+    scale = lax.rsqrt(jnp.mean(center * center, -1, keepdims=True) + EPS)
+    unit = center * scale
+    first_ref[...] = (unit * gain_ref[0:1] + gain_ref[1:2]).astype(BF16)
+    second_ref[...] = (unit * gain_ref[2:3] + gain_ref[3:4]).astype(BF16)
+    lane = lax.broadcasted_iota(jnp.int32, stat_ref.shape, 1)
+    stat_ref[...] = jnp.where(lane == 0, mean, scale)
+
+
+def project_block_kernel(n_ref, w_ref, b_ref, table_ref, q_ref, kv_ref):
+    head = q_ref.shape[1]
+    out = mul(n_ref[...], w_ref[...], NN) + b_ref[:1]
+    q_ref[...] = turn(out[:, :head], table_ref[...], 1.0).astype(BF16)
+    kv_ref[:, :head] = turn(out[:, head : 2 * head], table_ref[...], 1.0).astype(BF16)
+    kv_ref[:, head:] = out[:, 2 * head :].astype(BF16)
+
+
+def expand_block_kernel(n_ref, w_ref, b_ref, h_ref, d_ref):
+    pre = mul(n_ref[...], w_ref[...], NN) + b_ref[:1]
+    below = 0.5 + 0.5 * lax.erf(pre * math.sqrt(0.5))
+    h_ref[...] = (pre * below).astype(BF16)
+    d_ref[...] = (below + pre * jnp.exp(-0.5 * pre * pre) * (1.0 / math.sqrt(2 * math.pi))).astype(BF16)
+
+
+def forward_kernel(places, prompt, *refs):
+    (
+        x_ref, g_ref, wa, we, wo, wc, gain_ref, bias_a, bias_e, far_bias, segc, segr, pos_ref, freq_ref,
+        rows_in, rows_grad, gains, attend_all, expand_all, output_all, contract_all,
+        first, second, stat, table, queries, pairs, pairs_far, activated, slope, attended, row_sums, mixed,
+        send, recv, local, held_x, held_g, held_gains, *held,
+    ) = refs
     hops = Hops(send, recv)
     t, ring = lax.axis_index("tp"), lax.axis_size("tp")
-    rows = x_ref.shape[0]
+    rows, width = x_ref.shape
+    total = rows * ring
+    block = width // len(places)
     chunk = rows // 2
-    own = [pltpu.make_async_copy(p, w.at[pl.ds(0, p.shape[0])], local.at[1 + i]) for i, (p, w) in enumerate(zip(parts, wholes))]
-    own.append(pltpu.make_async_copy(x_ref, rows_ref.at[pl.ds(t * rows, rows)], local.at[0]))
-    for copy in own:
-        copy.start()
+
+    here = pl.ds(t * rows, rows)
+    moves = [(x_ref, held_x, rows_in.at[here]), (gain_ref, held_gains, gains), (g_ref, held_g, rows_grad.at[here])]
+    loads, stores, count = [], [], 0
+    for src, mid, dst in moves:
+        loads.append([])
+        for i, place in enumerate(places):
+            at = pl.ds(pl.multiple_of(place() * block, block), block)
+            loads[-1].append(pltpu.make_async_copy(src.at[:, at], mid.at[:, pl.ds(i * block, block)], local.at[count]))
+            count += 1
+        stores.append(pltpu.make_async_copy(mid, dst, local.at[count]))
+        count += 1
+    for src, mid, whole in zip((wa, we, wo, wc), held, (attend_all, expand_all, output_all, contract_all)):
+        loads.append([pltpu.make_async_copy(src, mid, local.at[count])])
+        stores.append(pltpu.make_async_copy(mid, whole.at[pl.ds(0, src.shape[0])], local.at[count + 1]))
+        count += 2
+
+    def rings(ref, held_rows):
+        made = {}
+        for step in range(ring - 1):
+            for half in range(2):
+                at = ref.at[pl.ds(((t + ring - step) % ring) * rows + half * chunk, chunk)]
+                src = held_rows.at[pl.ds(half * chunk, chunk)] if step == 0 else at
+                made[step, half] = hops.copy("up", src, at)
+        return made
+
+    ring_x, ring_g = rings(rows_in, held_x), rings(rows_grad, held_g)
+    a, e, o = (Block(hops, part, whole) for part, whole in ((wa, attend_all), (we, expand_all), (wo, output_all)))
+    c = Block(hops, wc, contract_all, 2)
+    own_pairs = pairs.at[pl.ds(0, prompt)]
+    far = [pairs_far.at[pl.ds(i * prompt, prompt)] for i in range(3)]
+    pair_y, pair_core = hops.copy("y", own_pairs, far[0]), hops.copy("core", own_pairs, far[1])
+    pair_corner = hops.copy("core", far[0], far[2])
+
+    def forward(copies, step, half):
+        arrive([copies[step, half]])
+        if step < ring - 2:
+            start([copies[step + 1, half]])
+
+    head = HEAD
+    heads = queries.shape[1] // head
+
+    def span(step):
+        return pl.ds(((t + ring - step) % ring) * rows, rows)
+
+    def norm(step):
+        tile = 128
+        row = pl.BlockSpec((tile, width), lambda i: (i, 0))
+        pltpu.emit_pipeline(
+            norm_block_kernel,
+            grid=(rows // tile,),
+            in_specs=[row, pl.BlockSpec((8, width), lambda i: (0, 0))],
+            out_specs=[row, row, pl.BlockSpec((tile, 128), lambda i: (i, 0))],
+        )(rows_in.at[span(step)], gains, first.at[span(step)], second.at[span(step)], stat.at[span(step)])
+
+    def project(step):
+        pltpu.emit_pipeline(
+            project_block_kernel,
+            grid=(heads,),
+            in_specs=[
+                pl.BlockSpec((rows, width), lambda h: (0, 0)),
+                pl.BlockSpec((width, 3 * head), lambda h: (0, h)),
+                pl.BlockSpec((8, 3 * head), lambda h: (0, h)),
+                pl.BlockSpec((rows, 384), lambda h: (0, 0)),
+            ],
+            out_specs=[pl.BlockSpec((rows, head), lambda h: (0, h)), pl.BlockSpec((rows, 2 * head), lambda h: (0, h))],
+        )(first.at[span(step)], attend_all, bias_a, table.at[span(step)], queries.at[span(step)], pairs.at[span(step)])
+
+    def expand(step):
+        tile = 512
+        out = pl.BlockSpec((rows, tile), lambda j: (0, j))
+        pltpu.emit_pipeline(
+            expand_block_kernel,
+            grid=(expand_all.shape[1] // tile,),
+            in_specs=[
+                pl.BlockSpec((rows, width), lambda j: (0, 0)),
+                pl.BlockSpec((width, tile), lambda j: (0, j)),
+                pl.BlockSpec((8, tile), lambda j: (0, j)),
+            ],
+            out_specs=[out, out],
+        )(second.at[span(step)], expand_all, bias_e, activated.at[span(step)], slope.at[span(step)])
+
+    for load in loads:
+        start(load)
     hops.greet()
-    sent = []
-
-    def ring_hop(step, part):
-        at = pl.ds(((t + ring - step) % ring) * rows + part * chunk, chunk)
-        src = x_ref.at[pl.ds(part * chunk, chunk)] if step == 0 else rows_ref.at[at]
-        return hops.copy("up", src, rows_ref.at[at])
-
-    def first(i):
-        size = parts[i].shape[0]
-        return [hops.copy(way, parts[i], wholes[i].at[pl.ds(slot * size, size)]) for way, slot in (("x", 1), ("y", 2))]
-
-    def across(i, slots):
-        size = parts[i].shape[0]
-        for slot in slots:
-            src = parts[i] if slot == 0 else wholes[i].at[pl.ds(slot * size, size)]
-            sent.append(hops.copy("core", src, wholes[i].at[pl.ds((4 + slot) * size, size)]))
-
-    def corner(i):
-        size = parts[i].shape[0]
-        half = size // 2
-        top, low = pl.ds(3 * size, half), pl.ds(3 * size + half, half)
-        return [
-            hops.copy("x", wholes[i].at[pl.ds(2 * size, half)], wholes[i].at[top]),
-            hops.copy("y", wholes[i].at[pl.ds(size + half, half)], wholes[i].at[low]),
-        ]
-
-    def arrive(copies):
-        for copy in copies:
-            copy.wait_recv()
-        sent.extend(("sent", copy) for copy in copies)
-
-    firsts, corners, rings = {}, {}, {}
-    firsts[0] = first(0)
-    rings[0, 0], rings[0, 1] = ring_hop(0, 0), ring_hop(0, 1)
-    if n > 1:
-        firsts[1] = first(1)
-    for i in range(n):
-        across(i, [0])
-    plan = [("r", 0, 0), ("f", 0), ("r", 0, 1), ("r", 1, 0), ("f", 1), ("r", 1, 1), ("c", 0), ("f", 2), ("r", 2, 0), ("c", 1), ("r", 2, 1), ("c", 2)]
-    for kind, *which in plan:
-        if kind == "r":
-            step, part = which
-            arrive([rings[step, part]])
-            if step < ring - 2:
-                rings[step + 1, part] = ring_hop(step + 1, part)
-            continue
-        i = which[0]
-        if kind == "f":
-            arrive(firsts[i])
-            corners[i] = corner(i)
-            if i + 2 < n:
-                firsts[i + 2] = first(i + 2)
-            across(i, [1, 2])
-        else:
-            arrive(corners[i])
-            across(i, [3])
-    for copy in sent:
-        if isinstance(copy, tuple):
-            copy[1].wait_send()
-        else:
+    start(a.first[0])
+    start([a.core[0]])
+    for i, (load, store) in enumerate(zip(loads, stores)):
+        for copy in load:
             copy.wait()
-    for copy in own:
-        copy.wait()
-
-
-def collect(x, parts):
+        store.start()
+        if i == 0:
+            start([ring_x[0, 0], ring_x[0, 1], e.core[0]])
+    for store in stores:
+        store.wait()
+    pltpu.emit_pipeline(
+        table_kernel,
+        grid=(total // rows,),
+        in_specs=[pl.BlockSpec((rows, 128), lambda i: (i, 0)), pl.BlockSpec((8, 128), lambda i: (0, 0))],
+        out_specs=[pl.BlockSpec((rows, 384), lambda i: (i, 0))],
+    )(pos_ref, freq_ref, table)
+    norm(0)
+    forward(ring_x, 0, 0)
+    start(e.first[0])
+    arrive(a.first[0])
+    start(a.corner + a.core[1:3])
+    forward(ring_x, 0, 1)
+    norm(1)
+    forward(ring_x, 1, 0)
+    arrive(a.corner)
+    start([a.core[3]])
+    arrive(e.first[0])
+    start(e.corner + e.core[1:3] + o.first[0] + [o.core[0]] + c.first[0] + [c.core[0]])
+    forward(ring_x, 1, 1)
+    start([ring_g[0, 0], ring_g[0, 1]])
+    norm(2)
+    arrive(a.core)
+    project(0)
+    forward(ring_x, 2, 0)
+    arrive(e.corner)
+    start([e.core[3]])
+    project(1)
+    project(2)
+    arrive(o.first[0])
+    start(o.core[1:3])
+    forward(ring_x, 2, 1)
+    norm(3)
+    project(3)
+    start([pair_y, pair_core] + o.corner)
+    arrive(e.core)
+    expand(0)
+    forward(ring_g, 0, 0)
+    arrive(c.first[0])
+    start(c.first[1])
+    expand(1)
+    arrive(o.corner)
+    start([o.core[3]])
+    expand(2)
+    forward(ring_g, 0, 1)
+    expand(3)
+    arrive([pair_y])
+    start([pair_corner])
+    arrive(c.first[1])
+    start(c.corner + c.core[1:3])
+    arrive([pair_core, pair_corner])
+
+    def attend_step(*args):
+        step = pl.program_id(0) * pl.num_programs(1) + pl.program_id(1)
+        pl.when(step == 2)(lambda: forward(ring_g, 1, 0))
+        pl.when(step == 7)(lambda: forward(ring_g, 1, 1))
+        attend_kernel(prompt, *args)
+
+    tq = ROWS
+    cont = total - prompt
+    n_far = far_bias.shape[1]
+    first_cont = prompt // tq
+    pltpu.emit_pipeline(
+        attend_step,
+        grid=(heads, total // tq),
+        in_specs=[
+            pl.BlockSpec((tq, head), lambda h, b: (b, h)),
+            pl.BlockSpec((total, head), lambda h, b: (0, 2 * h)),
+            pl.BlockSpec((total, head), lambda h, b: (0, 2 * h + 1)),
+            pl.BlockSpec((n_far, head), lambda h, b: (0, 2 * h)),
+            pl.BlockSpec((n_far, head), lambda h, b: (0, 2 * h + 1)),
+            pl.BlockSpec((8, n_far), lambda h, b: (0, 0)),
+            pl.BlockSpec((tq, 128), lambda h, b: (jnp.maximum(b - first_cont, 0), 0)),
+            pl.BlockSpec((8, cont), lambda h, b: (0, 0)),
+        ],
+        out_specs=[pl.BlockSpec((tq, head), lambda h, b: (b, h)), pl.BlockSpec((1, 8, tq), lambda h, b: (h, 0, b))],
+    )(queries, pairs, pairs, pairs_far, pairs_far, far_bias, segc, segr, attended, row_sums)
+
+    forward(ring_g, 2, 0)
+    arrive(c.corner)
+    start([c.core[3]])
+    arrive(o.core + c.core)
+    tile = 512
+    pltpu.emit_pipeline(
+        mixed_kernel,
+        grid=(width // tile,),
+        in_specs=[
+            pl.BlockSpec((total, attended.shape[1]), lambda j: (0, 0)),
+            pl.BlockSpec((total, activated.shape[1]), lambda j: (0, 0)),
+            pl.BlockSpec((tile, attended.shape[1]), lambda j: (j, 0)),
+            pl.BlockSpec((tile, activated.shape[1]), lambda j: (j, 0)),
+        ],
+        out_specs=[pl.BlockSpec((total, tile), lambda j: (0, j))],
+    )(attended, activated, output_all, contract_all, mixed)
+    forward(ring_g, 2, 1)
+    hops.end()
+
+
+def forward_pass(places, prompt, heads, x, g, weights, gains, bias_a, bias_e, far_bias, seg, where_at):
     ring = lax.axis_size("tp")
-    n = len(parts)
-    copies = 2 * (ring - 1) + 8 * n
+    rows, width = x.shape
+    total = ring * rows
+    wa, we, wo, wc = weights
+    head = HEAD
+    hidden = we.shape[1]
+    cont = total - prompt
+    far = far_bias.shape[0]
+    half = ROT // 2
+    lanes = jnp.arange(128) % half
+    freq = jnp.exp(lanes.astype(F32) * (-2.0 * math.log(10000.0) / ROT))
+    inputs = [
+        x, g, wa, we, wo, wc, gains, wide(bias_a), wide(bias_e), wide(far_bias),
+        jnp.broadcast_to(seg[prompt:, None], (cont, 128)), wide(seg[prompt:]),
+        jnp.broadcast_to(where_at.astype(F32)[:, None], (total, 128)), wide(freq),
+    ]
+    outs = [
+        shape(total, width), shape(total, width), shape(*gains.shape, kind=F32),
+        *(shape(8 * w.shape[0], w.shape[1]) for w in (wa, we, wo, wc)),
+        shape(total, width), shape(total, width), shape(total, 128, kind=F32), shape(total, 384, kind=F32),
+        shape(total, heads * head), shape(total, 2 * heads * head), shape(3 * prompt, 2 * heads * head),
+        shape(total, hidden), shape(total, hidden), shape(total, heads * head), shape(heads, 8, total, kind=F32),
+        shape(total, width),
+    ]
+    copies = 4 * (ring - 1) + 34 + 3
     ref = pl.BlockSpec(memory_space=pl.ANY)
     return pl.pallas_call(
-        partial(collect_kernel, n),
-        in_specs=[ref] * (n + 1),
-        out_specs=[ref] * (n + 1),
-        out_shape=[shape(ring * x.shape[0], x.shape[1])] + [shape(8 * p.shape[0], p.shape[1]) for p in parts],
+        partial(forward_kernel, places, prompt),
+        in_specs=[ref] * len(inputs),
+        out_specs=[ref] * len(outs),
+        out_shape=outs,
         scratch_shapes=[
             pltpu.SemaphoreType.DMA((copies,)),
             pltpu.SemaphoreType.DMA((copies,)),
-            pltpu.SemaphoreType.DMA((n + 1,)),
+            pltpu.SemaphoreType.DMA((3 * len(places) + 11,)),
+            pltpu.VMEM(x.shape, BF16),
+            pltpu.VMEM(g.shape, BF16),
+            pltpu.VMEM(gains.shape, F32),
+            *(pltpu.VMEM(w.shape, BF16) for w in weights),
         ],
-        compiler_params=pltpu.CompilerParams(collective_id=0, has_side_effects=True),
-        cost_estimate=pl.CostEstimate(flops=0, bytes_accessed=200 * 2**20, transcendentals=0),
-        name="collect",
-    )(x, *parts)
+        compiler_params=pltpu.CompilerParams(collective_id=0, has_side_effects=True, vmem_limit_bytes=56 * 2**20),
+        cost_estimate=pl.CostEstimate(flops=40 * 10**9, bytes_accessed=200 * 2**20, transcendentals=10**7),
+        name="forward_pass",
+    )(*inputs)
 
 
 class SquareLinks:
@@ -722,16 +954,6 @@
     def to_whole(self, v):
         return reorder(v, self.spots())
 
-    def collect(self, x, parts):
-        return collect(x, parts)
-
-    def gather(self, block):
-        rows = block.shape[0]
-        half = rows // 2
-        from_x, from_y = self.x_hop(block), self.y_hop(block)
-        corner = (self.x_hop(from_y[:half]), self.y_hop(from_x[half:]))
-        near = jnp.concatenate([block, from_x, from_y, *corner], 0)
-        return jnp.concatenate([near, self.core_hop(near)], 0)
 
     def scatter_far(self, left, right):
         return self.core_hop(far_product(left, right))
@@ -750,10 +972,6 @@
         c = lax.axis_index("ctx")
         return jnp.stack([v[c ^ bits] for bits in (2, 1, 3)])
 
-    def gather_others(self, block):
-        from_y = self.y_hop(block)
-        return jnp.concatenate([from_y, self.core_hop(jnp.concatenate([block, from_y], 0))], 0)
-
     def scatter_others(self, near, far):
         theirs = self.core_hop(far)
         rows = near.shape[0]
@@ -771,12 +989,6 @@
 
     def spots(self):
         return [lambda: 0]
-
-    def collect(self, x, parts):
-        return [lax.all_gather(x, "tp", axis=0, tiled=True)] + [self.gather(part) for part in parts]
-
-    def to_relative(self, v):
-        return v
 
     def to_whole(self, v):
         return v
@@ -899,31 +1111,36 @@
     holder = lax.axis_index("ctx")
     prompt = PROMPT // holders
 
-    rows_in, attend_all, expand_all, output_all = links.collect(
-        stream_in, [attend_weight.reshape(local_rows, -1), expand_weight, output_weight]
-    )
-    row_count = rows_in.shape[0]
-    rows_grad = lax.all_gather(links.to_relative(after(stream_grad, rows_in)), "tp", axis=0, tiled=True)
-    contract_all = links.gather(after(contract_weight, rows_in))
-
+    row_count = stream_in.shape[0] * lax.axis_size("tp")
     gains = jnp.concatenate([jnp.stack([first_gain, first_shift, second_gain, second_shift]), jnp.zeros((4, first_gain.shape[0]), F32)])
-    own_gains = links.to_relative(gains)
     row_pos = lax.dynamic_slice_in_dim(positions, holder * row_count, row_count)
     row_seg = lax.dynamic_slice_in_dim(segments, holder * row_count, row_count)
     starts = positions.reshape(holders, row_count)[:, 0]
     bias = jnp.where(links.others(starts) < row_pos[0], 0.0, -1e30).astype(F32)
     bias = jnp.repeat(bias, prompt)
-    table = turn_table(row_pos)
-
-    first_norm, second_norm, rows_in, stat = norms(rows_in, gains, links.places())
-    queries, pairs = project(first_norm, attend_all, attend_bias.reshape(-1), table, heads)
-    pairs_far = links.gather_others(pairs[:prompt])
-    activated, slope = expand(after(second_norm, pairs), expand_all, expand_bias)
-    attended, row_sums = attend(after(queries, activated), pairs, pairs_far, bias, row_seg, prompt)
-    mixed = mixed_sum(attended, activated, output_all, contract_all)
+    weights = (attend_weight.reshape(local_rows, -1), expand_weight, output_weight, contract_weight)
+
+    if square:
+        (
+            rows_in, rows_grad, own_gains, attend_all, expand_all, output_all, contract_all, first_norm, second_norm,
+            stat, table, queries, pairs, pairs_far, activated, slope, attended, row_sums, mixed,
+        ) = forward_pass(
+            links.places(), prompt, heads, stream_in, stream_grad, weights, gains, attend_bias.reshape(-1), expand_bias,
+            bias, row_seg, row_pos,
+        )
+    else:
+        own_gains = gains
+        rows_in, rows_grad = (lax.all_gather(v, "tp", axis=0, tiled=True) for v in (stream_in, stream_grad))
+        attend_all, expand_all, output_all, contract_all = (links.gather(v) for v in weights)
+        table = turn_table(row_pos)
+        first_norm, second_norm, rows_in, stat = norms(rows_in, gains, links.places())
+        queries, pairs = project(first_norm, attend_all, attend_bias.reshape(-1), table, heads)
+        pairs_far = links.gather_others(pairs[:prompt])
+        activated, slope = expand(second_norm, expand_all, expand_bias)
+        attended, row_sums = attend(queries, pairs, pairs_far, bias, row_seg, prompt)
+        mixed = mixed_sum(attended, activated, output_all, contract_all)
     branches = lax.psum_scatter(mixed, "tp", scatter_dimension=0, tiled=True)
 
-    rows_grad = after(rows_grad, mixed)
     grad_attended = attended_grads(rows_grad, output_all)
     grad_queries, pair_own, pair_near, pair_far = attend_back(
         queries, grad_attended, attended, row_sums, pairs, pairs_far, bias, row_seg, prompt, table

time: 563 us -> 514 us (0.913)
  waiting for transfers between devices: 140 us -> 103 us
  local copies, waits for them, and re-layouts: 53.9 us -> 30.8 us
  Pallas kernels: 297 us -> 316 us
  starting transfers between devices: 31.9 us -> 24.4 us
    ppermute x14 -> x11, waiting for transfers between devices: 89.2 us -> 58.6 us  [y_hop(): return lax.ppermute(v, 'ctx', [(0, 2), (2, 0), (1, 3), (3, 1)])]
    pallas_call x6 -> x1, Pallas kernels: 165 us -> 184 us  [forward_pass(): pl.pallas_call(partial(forward_kernel, places, prompt), in_specs=[ref] *...]
    unnamed x98 -> x69, local copies, waits for them, and re-layouts: 28.1 us -> 13.9 us
    concatenate x4 -> x0, local copies, waits for them, and re-layouts: 13.1 us -> none  [the longest x1 5.15 us: gather(): return jnp.concatenate([near, self.core_hop(near)], 0)]
    ppermute x12 -> x10, waiting for transfers between devices: 32.3 us -> 24.9 us  [x_hop(): return lax.ppermute(v, 'fsdp', [(0, 1), (1, 0)])]
    ppermute x14 -> x11, starting transfers between devices: 15.9 us -> 11.7 us  [y_hop(): return lax.ppermute(v, 'ctx', [(0, 2), (2, 0), (1, 3), (3, 1)])]
    ppermute x9 -> x7, waiting for transfers between devices: 16.1 us -> 16 us  [core_hop(): return lax.ppermute(v, 'ctx', [(0, 1), (1, 0), (2, 3), (3, 2)])]
  transfers between devices with their start and end apart: 40 -> 32, of which waited for: 20 -> 19; matrix products, arithmetic and copies ran while one was open for 9% -> 3% of each run, Pallas kernels for 29% -> 19%
where the time goes in v4:
time: 514 us; the launch traced here: 504 us
  Pallas kernels  316 us (61%)
  waiting for transfers between devices  103 us (20%)
  local copies, waits for them, and re-layouts  30.8 us (6%)
  starting transfers between devices  24.4 us (5%)
  other arithmetic  15 us (3%)
  between operations  15 us (3%)
    pallas_call x1, Pallas kernels, forward_pass(): pl.pallas_call(partial(forward_kernel, places, prompt), in_specs=[ref] *...  184 us
    ppermute x11, waiting for transfers between devices, y_hop(): return lax.ppermute(v, 'ctx', [(0, 2), (2, 0), (1, 3), (3, 1)])  58.6 us
    pallas_call x4, Pallas kernels, far_product(): call(far_kernel, (cols // tile,), [pl.BlockSpec((tokens, half), lambda j:...  27.9 us
    pallas_call x4, Pallas kernels, near_product(): call(near_kernel, (cols // tile,), [pl.BlockSpec((tokens, half), lambda j...  27.2 us
    ppermute x10, waiting for transfers between devices, x_hop(): return lax.ppermute(v, 'fsdp', [(0, 1), (1, 0)])  24.9 us
    pallas_call x1, Pallas kernels, attend_back(): call(partial(attend_back_kernel, prompt), (heads, rows // tq), [row, row,...  23 us
    pallas_call x1, Pallas kernels, unit_grads(): call(unit_grad_kernel, (width // tile,), [pl.BlockSpec((rows, deep), lamb...  22.3 us
    ppermute x7, waiting for transfers between devices, core_hop(): return lax.ppermute(v, 'ctx', [(0, 1), (1, 0), (2, 3), (3, 2)])  16 us
  transfers between devices with their start and end apart: 32, of which 19 were waited for; matrix products, arithmetic and copies ran while one was open for 3% of the time, Pallas kernels for 19%

profile of v4, /device:TPU:0, one launch (start us, length us, event | category | flops | bytes accessed | tf_op | source)
XLA Modules:
  0.0 504.0 jit_solution(9873028860249073211)
XLA Ops:
  7.3 2.1 copy.28
  12.5 2.7 compare_select_fusion
  16.0 1.4 concatenate.33.refs_6_
  18.0 1.3 broadcast_in_dim.39.refs_8_
  23.0 184.4 %forward_pass.1 = (bf16[1024,2048]{1,0:T(8,128)(2,1)}, bf16[1024,2048]{1,0:T(8,128)(2,1)}, f32[8,2048]{1,0:T(8,128)}, bf16[2048,1536]{1,0:T(8,128)(2,1)}, bf16[2...) custom-call(bf16[256,2048]{1,0:T(8,128)(2,1)} %x_ref.3, ...), custom_call_target="tpu_custom_call" | custom-call | flops 40000000000 | bytes 209715200 | tf_op jit(solution)/shard_map/forward_pass/pallas_call | solution.py:903
  207.4 1.6 copy-done.26
  209.0 5.0 attended_grads.1.do_ref
  214.3 23.0 %attend_back.1 = (bf16[1024,512]{1,0:T(8,128)(2,1)S(1)}, f32[1024,1024]{1,0:T(8,128)}, bf16[512,1024]{1,0:T(8,128)(2,1)S(1)}, bf16[1024,1024]{1,0:T(8,128)(2,1)}) custom-call(bf16[1024,512]{1,0:T(8,128)(2,1)S(1)} %copy-done.28, bf16[1024,512]{1,0:T(8,128)(2,1)S(1)} %attended_grads.1.do_ref, bf16[1024,512]{1,0:T(8,128)(2,1)} %get-tuple-element.110.o_ref.b_ref, ...), custom_call_target="tpu_custom_call" | custom-call | flops 13421772800 | bytes 18874368 | tf_op jit(solution)/shard_map/attend_back/pallas_call | solution.py:313
  238.3 8.5 %far_product.4 = bf16[1024,2048]{1,0:T(8,128)(2,1)} custom-call(bf16[1024,2048]{1,0:T(8,128)(2,1)} %get-tuple-element.83.g_ref.a_ref, bf16[1024,2048]{1,0:T(8,128)(2,1)} %get-tuple-element.87.b_ref), custom_call_target="tpu_custom_call" | custom-call | flops 4294967296 | bytes 10485760 | tf_op jit(solution)/shard_map/far_product/pallas_call | solution.py:522
  247.3 9.4 %collective-permute-done.far_ref = bf16[1024,1024]{1,0:T(8,128)(2,1)S(1)} collective-permute-done((bf16[1024,1024]{1,0:T(8,128)(2,1)}, bf16[1024,1024]{1,0:T(8,128)(2,1)S(1)}, u32[]{:S(2)}, u32[]{:S(2)}) %collective-permute-start) | collective-permute-done | bytes 2097184 | tf_op jit(solution)/shard_map/ppermute | solution.py:933
  257.3 1.3 slice_add_fusion
  259.6 24.3 %collective-permute-done.2.near_ref = bf16[512,1024]{1,0:T(8,128)(2,1)S(1)} collective-permute-done((bf16[512,1024]{1,0:T(8,128)(2,1)S(1)}, bf16[512,1024]{1,0:T(8,128)(2,1)S(1)}, u32[]{:S(2)}, u32[]{:S(2)}) %collective-permute-start.2) | collective-permute-done | bytes 1048608 | tf_op jit(solution)/shard_map/ppermute | solution.py:930
  283.9 13.5 %hidden_grads.1 = (bf16[1024,2048]{1,0:T(8,128)(2,1)S(1)}, f32[8,2048]{1,0:T(8,128)S(1)}) custom-call(bf16[1024,2048]{1,0:T(8,128)(2,1)} %get-tuple-element.83.g_ref.a_ref, bf16[2048,2048]{1,0:T(8,128)(2,1)} %get-tuple-element.84.w_ref, bf16[1024,2048]{1,0:T(8,128)(2,1)} %get-tuple-element.85.d_ref), custom_call_target="tpu_custom_call" | custom-call | flops 8589934592 | bytes 20971520 | tf_op jit(solution)/shard_map/hidden_grads/pallas_call | solution.py:420
  297.3 9.7 %near_product.4 = (f32[256,2048]{1,0:T(8,128)S(1)}, bf16[256,2048]{1,0:T(8,128)(2,1)S(1)}, bf16[256,2048]{1,0:T(8,128)(2,1)S(1)}, bf16[256,2048]{1,0:T(8,128)(2,1)S(1)}) custom-call(bf16[1024,2048]{1,0:T(8,128)(2,1)} %get-tuple-element.83.g_ref.a_ref, bf16[1024,2048]{1,0:T(8,128)(2,1)} %get-tuple-element.87.b_ref, ...), custom_call_target="tpu_custom_call" | custom-call | flops 4294967296 | bytes 14680064 | tf_op jit(solution)/shard_map/near_product/pallas_call | solution.py:547
  307.0 1.3 copy-done.3
  308.4 7.9 %pack.1 = (bf16[1024,1536]{1,0:T(8,128)(2,1)}, f32[8,1536]{1,0:T(8,128)S(1)}) custom-call(bf16[1024,512]{1,0:T(8,128)(2,1)S(1)} %get-tuple-element.76.q_ref, f32[1024,1024]{1,0:T(8,128)} %get-tuple-element.89.own_ref, bf16[512,1024]{1,0:T(8,128)(2,1)S(1)} %collective-permute-done.2.near_ref, bf16[1024,1024]{1,0:T(8,128)(2,1)S(1)} %collective-permute-done.far_ref, ...), custom_call_target="tpu_custom_call" | custom-call | flops 5242880 | bytes 8388608 | tf_op jit(solution)/shard_map/pack/pallas_call | solution.py:455
  316.3 1.9 copy-done.25
  318.1 22.3 %unit_grads.1 = (bf16[1024,2048]{1,0:T(8,128)(2,1)}, f32[8,2048]{1,0:T(8,128)S(1)}) custom-call(bf16[1024,1536]{1,0:T(8,128)(2,1)S(1)} %copy-done.25, bf16[1024,2048]{1,0:T(8,128)(2,1)} %copy-done.27, bf16[2048,1536]{1,0:T(8,128)(2,1)} %get-tuple-element.91.wa_ref, bf16[2048,2048]{1,0:T(8,128)(2,1)} %get-tuple-element.92.we_ref, ...), custom_call_target="tpu_custom_call" | custom-call | flops 15032385536 | bytes 30408704 | tf_op jit(solution)/shard_map/unit_grads/pallas_call | solution.py:493
  340.4 8.6 %far_product.5 = bf16[1024,2048]{1,0:T(8,128)(2,1)} custom-call(bf16[1024,2048]{1,0:T(8,128)(2,1)} %get-tuple-element.99.a_ref, bf16[1024,2048]{1,0:T(8,128)(2,1)} %copy-done.27), custom_call_target="tpu_custom_call" | custom-call | flops 4294967296 | bytes 10485760 | tf_op jit(solution)/shard_map/far_product/pallas_call | solution.py:522
  349.9 6.1 %collective-permute-done.3 = f32[5,2048]{1,0:T(8,128)S(1)} collective-permute-done((f32[5,2048]{1,0:T(8,128)S(1)}, f32[5,2048]{1,0:T(8,128)S(1)}, u32[]{:S(2)}, u32[]{:S(2)}) %collective-permute-start.3) | collective-permute-done | bytes 40992 | tf_op jit(solution)/shard_map/ppermute | solution.py:933
  359.2 1.3 collective-permute-done.4
  361.4 3.4 collective-permute-done.5
  365.3 3.8 collective-permute-done.6
  370.2 2.9 collective-permute-done.15
  373.9 1.2 collective-permute-start.26
  375.1 1.8 collective-permute-done.16
  379.4 9.7 %collective-permute-done.26 = bf16[128,2048]{1,0:T(8,128)(2,1)S(1)} collective-permute-done((bf16[128,2048]{1,0:T(8,128)(2,1)}, bf16[128,2048]{1,0:T(8,128)(2,1)S(1)}, u32[]{:S(2)}, u32[]{:S(2)}) %collective-permute-start.26) | collective-permute-done | bytes 524320 | tf_op jit(solution)/shard_map/ppermute | solution.py:930
  390.4 8.0 %near_product.5 = (f32[256,2048]{1,0:T(8,128)S(1)}, bf16[256,2048]{1,0:T(8,128)(2,1)S(1)}, bf16[256,2048]{1,0:T(8,128)(2,1)S(1)}, bf16[256,2048]{1,0:T(8,128)(2,1)S(1)}) custom-call(bf16[1024,2048]{1,0:T(8,128)(2,1)} %get-tuple-element.99.a_ref, bf16[1024,2048]{1,0:T(8,128)(2,1)} %copy-done.27, bf16[1024,2048]{1,0:T(8,128)(2,1)} %collective-permute-done.8.r_ref), custom_call_target="tpu_custom_call" | custom-call | flops 4294967296 | bytes 14680064 | tf_op jit(solution)/shard_map/near_product/pallas_call | solution.py:547
  398.5 1.3 copy-done.5
  400.7 7.7 %far_product.6 = bf16[1024,1536]{1,0:T(8,128)(2,1)} custom-call(bf16[1024,2048]{1,0:T(8,128)(2,1)} %get-tuple-element.98.a_ref, bf16[1024,1536]{1,0:T(8,128)(2,1)} %get-tuple-element.102.gp_ref.b_ref), custom_call_target="tpu_custom_call" | custom-call | flops 3221225472 | bytes 8388608 | tf_op jit(solution)/shard_map/far_product/pallas_call | solution.py:522
  411.4 1.8 convert_add_fusion
  413.2 1.3 copy-done.11
  414.5 1.7 output_rows.1
  416.2 3.0 far_product.7
  420.7 4.3 collective-permute-done.24
  425.0 1.2 slice_add_fusion.3
  427.4 6.8 %collective-permute-done.22 = bf16[128,2048]{1,0:T(8,128)(2,1)S(1)} collective-permute-done((bf16[128,2048]{1,0:T(8,128)(2,1)S(1)}, bf16[128,2048]{1,0:T(8,128)(2,1)S(1)}, u32[]{:S(2)}, u32[]{:S(2)}) %collective-permute-start.22) | collective-permute-done | bytes 524320 | tf_op jit(solution)/shard_map/ppermute | solution.py:930
  435.5 6.7 %near_product.6 = (f32[256,1536]{1,0:T(8,128)S(1)}, bf16[256,1536]{1,0:T(8,128)(2,1)S(1)}, bf16[256,1536]{1,0:T(8,128)(2,1)S(1)}, bf16[256,1536]{1,0:T(8,128)(2,1)S(1)}) custom-call(bf16[1024,2048]{1,0:T(8,128)(2,1)} %get-tuple-element.98.a_ref, bf16[1024,1536]{1,0:T(8,128)(2,1)} %get-tuple-element.102.gp_ref.b_ref, ...), custom_call_target="tpu_custom_call" | custom-call | flops 3221225472 | bytes 11534336 | tf_op jit(solution)/shard_map/near_product/pallas_call | solution.py:547
  443.4 2.9 near_product.7
  449.5 14.0 %collective-permute-done.20 = bf16[128,512]{1,0:T(8,128)(2,1)S(1)} collective-permute-done((bf16[128,512]{1,0:T(8,128)(2,1)S(1)}, bf16[128,512]{1,0:T(8,128)(2,1)S(1)}, u32[]{:S(2)}, u32[]{:S(2)}) %collective-permute-start.20) | collective-permute-done | bytes 131104 | tf_op jit(solution)/shard_map/ppermute | solution.py:927
  464.7 3.7 collective-permute-done.18
  475.2 1.8 convert_add_fusion.1
  479.0 1.2 copy-done.10
  480.2 2.8 input_grads.1
  483.0 8.6 %collective-permute-done.13 = bf16[256,1536]{1,0:T(8,128)(2,1)S(1)} collective-permute-done((bf16[256,1536]{1,0:T(8,128)(2,1)}, bf16[256,1536]{1,0:T(8,128)(2,1)S(1)}, u32[]{:S(2)}, u32[]{:S(2)}) %collective-permute-start.13) | collective-permute-done | bytes 786464 | tf_op jit(solution)/shard_map/ppermute | solution.py:930
  491.7 1.5 collective-permute-done.11
  493.2 1.4 convert_add_fusion.2
  494.6 2.2 reshape.63
  (171 shorter events, 44.9 us)
Async XLA Ops:
  7.2 406.0 %reduce-scatter.3.cloned.1.call-start = ((), (), s32[]{:S(2)}) async-start(), calls=%async_computation.2 | async-start | bytes 5242880 | tf_op jit(solution)/shard_map/reduce_scatter | solution.py:1142
  209.0 5.3 %copy-start.28 = (bf16[1024,512]{1,0:T(8,128)(2,1)S(1)}, bf16[1024,512]{1,0:T(8,128)(2,1)}, u32[]{:S(2)}) copy-start(bf16[1024,512]{1,0:T(8,128)(2,1)} %get-tuple-element.68.q_ref) | copy-start | bytes 3145732
  209.0 5.3 %copy-start.31 = (f32[2,8,1024]{2,1,0:T(8,128)S(1)}, f32[2,8,1024]{2,1,0:T(8,128)}, u32[]{:S(2)}) copy-start(f32[2,8,1024]{2,1,0:T(8,128)} %get-tuple-element.72.stat_ref) | copy-start | bytes 196612
  246.7 10.5 %collective-permute-start.1 = (bf16[1024,2048]{1,0:T(8,128)(2,1)}, bf16[1024,2048]{1,0:T(8,128)(2,1)}, u32[]{:S(2)}, u32[]{:S(2)}) collective-permute-start(bf16[1024,2048]{1,0:T(8,128)(2,1)} %far_product.4), channel_id=1, source_target_pairs={{0,4},{4,0},{8,12},{12,8},{1,5},{5,1},{9,13},{13,9},{2,6},{6,2},{1... | collective-permute-start | bytes 12582920 | tf_op jit(solution)/shard_map/ppermute | solution.py:933
  246.8 10.0 %collective-permute-start = (bf16[1024,1024]{1,0:T(8,128)(2,1)}, bf16[1024,1024]{1,0:T(8,128)(2,1)S(1)}, u32[]{:S(2)}, u32[]{:S(2)}) collective-permute-start(bf16[1024,1024]{1,0:T(8,128)(2,1)} %get-tuple-element.79), channel_id=1, source_target_pairs={{0,4},{4,0},{8,12},{12,8},{1,5},{5,1},{9,13},{13,9},{2,6},{6,2},{1... | collective-permute-start | bytes 6291464 | tf_op jit(solution)/shard_map/ppermute | solution.py:933
  247.3 231.7 %reduce-scatter.5.cloned.1.call-start = ((), (), s32[]{:S(2)}) async-start(), calls=%async_computation.3 | async-start | bytes 5242880 | tf_op jit(solution)/shard_map/reduce_scatter | solution.py:1155
  258.6 25.3 %collective-permute-start.2 = (bf16[512,1024]{1,0:T(8,128)(2,1)S(1)}, bf16[512,1024]{1,0:T(8,128)(2,1)S(1)}, u32[]{:S(2)}, u32[]{:S(2)}) collective-permute-start(bf16[512,1024]{1,0:T(8,128)(2,1)S(1)} %slice_add_fusion), channel_id=1, source_target_pairs={{0,8},{8,0},{4,12},{12,4},{1,9},{9,1},{5,13},{13,5},{2,10},{10,2},... | collective-permute-start | bytes 3145736 | tf_op jit(solution)/shard_map/ppermute | solution.py:930
  297.3 9.7 %copy-start.27 = (bf16[1024,2048]{1,0:T(8,128)(2,1)}, bf16[1024,2048]{1,0:T(8,128)(2,1)S(1)}, u32[]{:S(2)}) copy-start(bf16[1024,2048]{1,0:T(8,128)(2,1)S(1)} %get-tuple-element.100.gh_ref.b_ref) | copy-start | bytes 12582916
  297.3 11.0 %copy-start.7 = (f32[1024,384]{1,0:T(8,128)S(1)}, f32[1024,384]{1,0:T(8,128)}, u32[]{:S(2)}) copy-start(f32[1024,384]{1,0:T(8,128)} %get-tuple-element.75.table_ref) | copy-start | bytes 4718596
  308.3 7.9 %copy-start.13 = (bf16[256,2048]{1,0:T(8,128)(2,1)}, bf16[256,2048]{1,0:T(8,128)(2,1)S(1)}, u32[]{:S(2)}) copy-start(bf16[256,2048]{1,0:T(8,128)(2,1)S(1)} %get-tuple-element.118) | copy-start | bytes 3145732
  308.3 7.9 %copy-start.15 = (bf16[256,2048]{1,0:T(8,128)(2,1)}, bf16[256,2048]{1,0:T(8,128)(2,1)S(1)}, u32[]{:S(2)}) copy-start(bf16[256,2048]{1,0:T(8,128)(2,1)S(1)} %get-tuple-element.120) | copy-start | bytes 3145732
  308.3 7.9 %copy-start.21 = (bf16[256,2048]{1,0:T(8,128)(2,1)}, bf16[256,2048]{1,0:T(8,128)(2,1)S(1)}, u32[]{:S(2)}) copy-start(bf16[256,2048]{1,0:T(8,128)(2,1)S(1)} %get-tuple-element.119) | copy-start | bytes 3145732
  308.3 7.9 %copy-start.29 = (f32[1024,128]{1,0:T(8,128)S(1)}, f32[1024,128]{1,0:T(8,128)}, u32[]{:S(2)}) copy-start(f32[1024,128]{1,0:T(8,128)} %get-tuple-element.94.stat_ref) | copy-start | bytes 1572868
  308.4 7.9 %copy-start.30 = (f32[8,2048]{1,0:T(8,128)S(1)}, f32[8,2048]{1,0:T(8,128)}, u32[]{:S(2)}) copy-start(f32[8,2048]{1,0:T(8,128)} %get-tuple-element.95.gain_ref) | copy-start | bytes 196612
  340.4 8.6 %copy-start.1 = (bf16[256,2048]{1,0:T(8,128)(2,1)S(1)}, bf16[256,2048]{1,0:T(8,128)(2,1)}, u32[]{:S(2)}) copy-start(bf16[256,2048]{1,0:T(8,128)(2,1)} %g_ref.1) | copy-start | bytes 3145732
  349.1 7.9 %copy-start.22 = (bf16[256,2048]{1,0:T(8,128)(2,1)S(1)}, bf16[256,2048]{1,0:T(8,128)(2,1)}, u32[]{:S(2)}) copy-start(bf16[256,2048]{1,0:T(8,128)(2,1)} %copy-done.21) | copy-start | bytes 3145732
  349.1 41.3 %collective-permute-start.8 = (bf16[1024,2048]{1,0:T(8,128)(2,1)}, bf16[1024,2048]{1,0:T(8,128)(2,1)}, u32[]{:S(2)}, u32[]{:S(2)}) collective-permute-start(bf16[1024,2048]{1,0:T(8,128)(2,1)} %far_product.5), channel_id=1, source_target_pairs={{0,4},{4,0},{8,12},{12,8},{1,5},{5,1},{9,13},{13,9},{2,6},{6,2},{1... | collective-permute-start | bytes 12582920 | tf_op jit(solution)/shard_map/ppermute | solution.py:933
  349.3 6.6 %collective-permute-start.3 = (f32[5,2048]{1,0:T(8,128)S(1)}, f32[5,2048]{1,0:T(8,128)S(1)}, u32[]{:S(2)}, u32[]{:S(2)}) collective-permute-start(f32[5,2048]{1,0:T(8,128)S(1)} %pad_maximum_fusion.8), channel_id=1, source_target_pairs={{0,4},{4,0},{8,12},{12,8},{1,5},{5,1},{9,13},{13,9},{2,6},{6,2},{1... | collective-permute-start | bytes 122888 | tf_op jit(solution)/shard_map/ppermute | solution.py:933
  356.0 4.4 collective-permute-start.4
  358.0 20.2 %collective-permute-start.28 = (bf16[128,2048]{1,0:T(8,128)(2,1)}, bf16[128,2048]{1,0:T(8,128)(2,1)S(1)}, u32[]{:S(2)}, u32[]{:S(2)}) collective-permute-start(bf16[128,2048]{1,0:T(8,128)(2,1)} %get-tuple-element.126), channel_id=1, source_target_pairs={{0,16},{16,0},{1,17},{17,1},{2,18},{18,2},{3,19},{19,3},{4,20},{20... | collective-permute-start | bytes 1572872 | tf_op jit(solution)/shard_map/ppermute | solution.py:927
  360.4 4.3 collective-permute-start.5
  364.8 4.3 collective-permute-start.6
  365.3 3.9 collective-permute-start.14
  369.1 9.1 %collective-permute-start.7 = (f32[5,2048]{1,0:T(8,128)S(1)}, f32[5,2048]{1,0:T(8,128)S(1)}, u32[]{:S(2)}, u32[]{:S(2)}) collective-permute-start(f32[5,2048]{1,0:T(8,128)S(1)} %add.111), channel_id=1, source_target_pairs={{0,2},{1,3},{2,0},{3,1},{4,6},{5,7},{6,4},{7,5},{8,10},{9,11},{10,... | collective-permute-start | bytes 122888 | tf_op jit(solution)/shard_map/ppermute | solution.py:1033
  369.2 3.8 collective-permute-start.15
  373.0 3.9 collective-permute-start.16
  373.9 15.1 %collective-permute-start.26 = (bf16[128,2048]{1,0:T(8,128)(2,1)}, bf16[128,2048]{1,0:T(8,128)(2,1)S(1)}, u32[]{:S(2)}, u32[]{:S(2)}) collective-permute-start(bf16[128,2048]{1,0:T(8,128)(2,1)} %get-tuple-element.125), channel_id=1, source_target_pairs={{0,8},{8,0},{4,12},{12,4},{1,9},{9,1},{5,13},{13,5},{2,10},{10,2},... | collective-permute-start | bytes 1572872 | tf_op jit(solution)/shard_map/ppermute | solution.py:930
  378.2 10.8 %copy-start.14 = (bf16[256,2048]{1,0:T(8,128)(2,1)S(1)}, bf16[256,2048]{1,0:T(8,128)(2,1)}, u32[]{:S(2)}) copy-start(bf16[256,2048]{1,0:T(8,128)(2,1)} %copy-done.13) | copy-start | bytes 3145732
  378.4 33.0 %collective-permute-start.29 = (bf16[256,2048]{1,0:T(8,128)(2,1)S(1)}, bf16[256,2048]{1,0:T(8,128)(2,1)S(1)}, u32[]{:S(2)}, u32[]{:S(2)}) collective-permute-start(bf16[256,2048]{1,0:T(8,128)(2,1)S(1)} %pad_maximum_fusion.3), channel_id=1, source_target_pairs={{0,8},{8,0},{4,12},{12,4},{1,9},{9,1},{5,13},{13,5},{2,10},{10,2},... | collective-permute-start | bytes 3145736 | tf_op jit(solution)/shard_map/ppermute | solution.py:930
  389.3 22.1 %collective-permute-start.27 = (bf16[256,2048]{1,0:T(8,128)(2,1)S(1)}, bf16[256,2048]{1,0:T(8,128)(2,1)S(1)}, u32[]{:S(2)}, u32[]{:S(2)}) collective-permute-start(bf16[256,2048]{1,0:T(8,128)(2,1)S(1)} %pad_maximum_fusion.2), channel_id=1, source_target_pairs={{0,16},{16,0},{1,17},{17,1},{2,18},{18,2},{3,19},{19,3},{4,20},{20... | collective-permute-start | bytes 3145736 | tf_op jit(solution)/shard_map/ppermute | solution.py:927
  400.7 7.8 %copy-start.19 = (bf16[256,2048]{1,0:T(8,128)(2,1)}, bf16[256,2048]{1,0:T(8,128)(2,1)S(1)}, u32[]{:S(2)}) copy-start(bf16[256,2048]{1,0:T(8,128)(2,1)S(1)} %get-tuple-element.117) | copy-start | bytes 3145732
  408.5 27.0 %collective-permute-start.9 = (bf16[1024,1536]{1,0:T(8,128)(2,1)}, bf16[1024,1536]{1,0:T(8,128)(2,1)}, u32[]{:S(2)}, u32[]{:S(2)}) collective-permute-start(bf16[1024,1536]{1,0:T(8,128)(2,1)} %far_product.6), channel_id=1, source_target_pairs={{0,4},{4,0},{8,12},{12,8},{1,5},{5,1},{9,13},{13,9},{2,6},{6,2},{1... | collective-permute-start | bytes 9437192 | tf_op jit(solution)/shard_map/ppermute | solution.py:933
  410.4 14.6 %collective-permute-start.24 = (bf16[128,2048]{1,0:T(8,128)(2,1)}, bf16[128,2048]{1,0:T(8,128)(2,1)}, u32[]{:S(2)}, u32[]{:S(2)}) collective-permute-start(bf16[128,2048]{1,0:T(8,128)(2,1)} %get-tuple-element.132), channel_id=1, source_target_pairs={{0,16},{16,0},{1,17},{17,1},{2,18},{18,2},{3,19},{19,3},{4,20},{20... | collective-permute-start | bytes 1572872 | tf_op jit(solution)/shard_map/ppermute | solution.py:927
  416.2 8.7 %copy-start.20 = (bf16[256,2048]{1,0:T(8,128)(2,1)S(1)}, bf16[256,2048]{1,0:T(8,128)(2,1)}, u32[]{:S(2)}) copy-start(bf16[256,2048]{1,0:T(8,128)(2,1)} %copy-done.19) | copy-start | bytes 3145732
  419.2 24.1 %collective-permute-start.17 = (bf16[1024,512]{1,0:T(8,128)(2,1)S(1)}, bf16[1024,512]{1,0:T(8,128)(2,1)S(1)}, u32[]{:S(2)}, u32[]{:S(2)}) collective-permute-start(bf16[1024,512]{1,0:T(8,128)(2,1)S(1)} %far_product.7), channel_id=1, source_target_pairs={{0,4},{4,0},{8,12},{12,8},{1,5},{5,1},{9,13},{13,9},{2,6},{6,2},{1... | collective-permute-start | bytes 3145736 | tf_op jit(solution)/shard_map/ppermute | solution.py:933
  419.5 14.7 %collective-permute-start.22 = (bf16[128,2048]{1,0:T(8,128)(2,1)S(1)}, bf16[128,2048]{1,0:T(8,128)(2,1)S(1)}, u32[]{:S(2)}, u32[]{:S(2)}) collective-permute-start(bf16[128,2048]{1,0:T(8,128)(2,1)S(1)} %copy-done.32), channel_id=1, source_target_pairs={{0,8},{8,0},{4,12},{12,4},{1,9},{9,1},{5,13},{13,5},{2,10},{10,2},... | collective-permute-start | bytes 1572872 | tf_op jit(solution)/shard_map/ppermute | solution.py:930
  425.0 9.3 %copy-start.18 = (bf16[256,2048]{1,0:T(8,128)(2,1)S(1)}, bf16[256,2048]{1,0:T(8,128)(2,1)}, u32[]{:S(2)}) copy-start(bf16[256,2048]{1,0:T(8,128)(2,1)} %copy-done.17) | copy-start | bytes 3145732
  426.3 47.7 %collective-permute-start.25 = (bf16[256,2048]{1,0:T(8,128)(2,1)S(1)}, bf16[256,2048]{1,0:T(8,128)(2,1)S(1)}, u32[]{:S(2)}, u32[]{:S(2)}) collective-permute-start(bf16[256,2048]{1,0:T(8,128)(2,1)S(1)} %pad_maximum_fusion.1), channel_id=1, source_target_pairs={{0,8},{8,0},{4,12},{12,4},{1,9},{9,1},{5,13},{13,5},{2,10},{10,2},... | collective-permute-start | bytes 3145736 | tf_op jit(solution)/shard_map/ppermute | solution.py:930
  434.5 40.7 %collective-permute-start.23 = (bf16[256,2048]{1,0:T(8,128)(2,1)S(1)}, bf16[256,2048]{1,0:T(8,128)(2,1)S(1)}, u32[]{:S(2)}, u32[]{:S(2)}) collective-permute-start(bf16[256,2048]{1,0:T(8,128)(2,1)S(1)} %pad_maximum_fusion), channel_id=1, source_target_pairs={{0,16},{16,0},{1,17},{17,1},{2,18},{18,2},{3,19},{19,3},{4,20},{20... | collective-permute-start | bytes 3145736 | tf_op jit(solution)/shard_map/ppermute | solution.py:927
  446.3 17.2 %collective-permute-start.20 = (bf16[128,512]{1,0:T(8,128)(2,1)S(1)}, bf16[128,512]{1,0:T(8,128)(2,1)S(1)}, u32[]{:S(2)}, u32[]{:S(2)}) collective-permute-start(bf16[128,512]{1,0:T(8,128)(2,1)S(1)} %get-tuple-element.144), channel_id=1, source_target_pairs={{0,16},{16,0},{1,17},{17,1},{2,18},{18,2},{3,19},{19,3},{4,20},{20... | collective-permute-start | bytes 393224 | tf_op jit(solution)/shard_map/ppermute | solution.py:927
  447.4 22.4 %collective-permute-start.12 = (bf16[128,1536]{1,0:T(8,128)(2,1)S(1)}, bf16[128,1536]{1,0:T(8,128)(2,1)S(1)}, u32[]{:S(2)}, u32[]{:S(2)}) collective-permute-start(bf16[128,1536]{1,0:T(8,128)(2,1)S(1)} %get-tuple-element.138), channel_id=1, source_target_pairs={{0,16},{16,0},{1,17},{17,1},{2,18},{18,2},{3,19},{19,3},{4,20},{20... | collective-permute-start | bytes 1179656 | tf_op jit(solution)/shard_map/ppermute | solution.py:927
  448.5 23.4 %collective-permute-start.10 = (bf16[128,1536]{1,0:T(8,128)(2,1)S(1)}, bf16[128,1536]{1,0:T(8,128)(2,1)S(1)}, u32[]{:S(2)}, u32[]{:S(2)}) collective-permute-start(bf16[128,1536]{1,0:T(8,128)(2,1)S(1)} %get-tuple-element.137), channel_id=1, source_target_pairs={{0,8},{8,0},{4,12},{12,4},{1,9},{9,1},{5,13},{13,5},{2,10},{10,2},... | collective-permute-start | bytes 1179656 | tf_op jit(solution)/shard_map/ppermute | solution.py:930
  463.5 5.0 collective-permute-start.18
  468.4 8.8 %collective-permute-start.21 = (bf16[256,512]{1,0:T(8,128)(2,1)S(1)}, bf16[256,512]{1,0:T(8,128)(2,1)S(1)}, u32[]{:S(2)}, u32[]{:S(2)}) collective-permute-start(bf16[256,512]{1,0:T(8,128)(2,1)S(1)} %pad_maximum_fusion.7), channel_id=1, source_target_pairs={{0,8},{8,0},{4,12},{12,4},{1,9},{9,1},{5,13},{13,5},{2,10},{10,2},... | collective-permute-start | bytes 786440 | tf_op jit(solution)/shard_map/ppermute | solution.py:930
  469.8 8.2 %collective-permute-start.19 = (bf16[256,512]{1,0:T(8,128)(2,1)S(1)}, bf16[256,512]{1,0:T(8,128)(2,1)S(1)}, u32[]{:S(2)}, u32[]{:S(2)}) collective-permute-start(bf16[256,512]{1,0:T(8,128)(2,1)S(1)} %pad_maximum_fusion.6), channel_id=1, source_target_pairs={{0,16},{16,0},{1,17},{17,1},{2,18},{18,2},{3,19},{19,3},{4,20},{20... | collective-permute-start | bytes 786440 | tf_op jit(solution)/shard_map/ppermute | solution.py:927
  471.9 19.7 %collective-permute-start.13 = (bf16[256,1536]{1,0:T(8,128)(2,1)}, bf16[256,1536]{1,0:T(8,128)(2,1)S(1)}, u32[]{:S(2)}, u32[]{:S(2)}) collective-permute-start(bf16[256,1536]{1,0:T(8,128)(2,1)} %pad_maximum_fusion.5), channel_id=1, source_target_pairs={{0,8},{8,0},{4,12},{12,4},{1,9},{9,1},{5,13},{13,5},{2,10},{10,2},... | collective-permute-start | bytes 2359304 | tf_op jit(solution)/shard_map/ppermute | solution.py:930
  474.0 19.1 %collective-permute-start.11 = (bf16[256,1536]{1,0:T(8,128)(2,1)}, bf16[256,1536]{1,0:T(8,128)(2,1)}, u32[]{:S(2)}, u32[]{:S(2)}) collective-permute-start(bf16[256,1536]{1,0:T(8,128)(2,1)} %pad_maximum_fusion.4), channel_id=1, source_target_pairs={{0,16},{16,0},{1,17},{17,1},{2,18},{18,2},{3,19},{19,3},{4,20},{20... | collective-permute-start | bytes 2359304 | tf_op jit(solution)/shard_map/ppermute | solution.py:927
  480.2 13.0 %copy-start.9 = (f32[256,1536]{1,0:T(8,128)S(1)}, f32[256,1536]{1,0:T(8,128)}, u32[]{:S(2)}) copy-start(f32[256,1536]{1,0:T(8,128)} %copy-done.8) | copy-start | bytes 4718596
  (18 other events, 45.7 us)
Sparse Core Ops, SparseCore 0:
  247.4 73.9 reduce-scatter.2
  374.0 77.1 reduce-scatter.4
